TPU v7x, 128 devices: a whole 4x4x4 slice. The times are simulated.
128 devices in a mesh: ctx: 8 (over z, x_lo), kvh: 2 (over x_hi), exp: 8 (over y, core).
Axes of the slice: x: 4 (x_hi: 2, x_lo: 2; x = x_hi * 2 + x_lo), y: 4, z: 4, core: 2. Of those that a mesh axis runs over, the one named last changes fastest.
Arguments:
- queries: bfloat16 [32, 4, 8, 128], P('exp', 'kvh'), may hold values from -72 to 72
- key_cache: bfloat16 [32, 8192, 4, 128], P('exp', 'ctx', 'kvh'), may hold values from -6 to 6
- value_cache: bfloat16 [32, 8192, 4, 128], P('exp', 'ctx', 'kvh'), may hold values from -6 to 6
- centroid_keys: bfloat16 [32, 512, 4, 128], P('exp', 'ctx', 'kvh'), may hold values from -3 to 3
- centroid_values: bfloat16 [32, 512, 4, 128], P('exp', 'ctx', 'kvh'), may hold values from -6 to 6
- selected: int32 [32, 4, 16], P('exp', 'kvh', 'ctx'), may hold values from 0 to 511, as said below
- new_key: bfloat16 [32, 4, 128], P('exp', 'kvh'), may hold values from -6 to 6
- new_value: bfloat16 [32, 4, 128], P('exp', 'kvh'), may hold values from -6 to 6
- out_weight: bfloat16 [4, 8, 128, 4096], P('kvh', 'ctx'), may hold values from -0.5 to 0.5
- residual: bfloat16 [32, 4096], P('exp'), may hold values from -6 to 6
- norm_gain: float32 [4096], replicated, may hold values from 0.5 to 1.5
- expert_ids: int32 [32, 8], P('exp'), may hold values from 0 to 63, all different within a row; in each aligned block of 4 rows (0 to 3, 4 to 7, ...) at most 2 rows name the same one
- gate_weights: float32 [32, 8], P('exp'), may hold values from 0.05 to 0.5
- w_gate_up: bfloat16 [64, 4096, 2, 1536], P(('ctx', 'exp'), None, None, 'kvh'), may hold values from -0.09375 to 0.09375
- w_down: bfloat16 [64, 1536, 4096], P(('ctx', 'exp'), 'kvh'), may hold values from -0.15625 to 0.15625
Outputs:
- layer_out: bfloat16 [32, 4096], P('exp', ('ctx', 'kvh'))
Inputs may be any that keep to these rules, and one draw needn't show every extreme that they name: `selected`: entries k * 2 to (k + 1) * 2 - 1 of each list are different clusters held by context shard k, that is numbers from k * 64 to (k + 1) * 64 - 1. `expert_ids`: in the 4 rows of one index of exp no expert is named by more than 2 rows, a bound that some block reaches of them.
All inputs are finite; a program needn't handle non-finite values.
Results may differ from a plain program's by a relative error of at most 0.02.
Values may be sent and summed in bfloat16 or wider, within the bound.
No kernel may reach another device: no remote copies, remote signals or barrier semaphores. Data moves between devices by JAX's collectives and lax.ppermute only.
A program may use at most 128 MiB of HBM per device.

v0:
```python
import math

import jax
import jax.numpy as jnp
from jax import lax
from jax.sharding import PartitionSpec as P


def joined(value, axis, join):
    pieces = jax.tree.map(lambda part: lax.all_gather(part, axis), value)
    head = jax.tree.map(lambda part: part[0], pieces)
    tail = jax.tree.map(lambda part: part[1:], pieces)
    so_far, _ = lax.scan(lambda so_far, section: (join(so_far, section), None), head, tail)
    return so_far


def combine_parts(earlier, later):
    peak_left, sum_left, out_left = earlier
    peak_right, sum_right, out_right = later
    peak_both = jnp.maximum(peak_left, peak_right)
    scale_left = jnp.exp(peak_left - peak_both)
    scale_right = jnp.exp(peak_right - peak_both)
    return (
        peak_both,
        sum_left * scale_left + sum_right * scale_right,
        out_left * scale_left[..., None] + out_right * scale_right[..., None],
    )


def body(
    queries,
    key_cache,
    value_cache,
    centroid_keys,
    centroid_values,
    selected,
    new_key,
    new_value,
    out_weight,
    residual,
    norm_gain,
    expert_ids,
    gate_weights,
    w_gate_up,
    w_down,
):
    ctx_devices = lax.axis_size("ctx")
    exp_devices = lax.axis_size("exp")
    ctx_pos = lax.axis_index("ctx")
    seq_count, ctx_len, heads_kv, head_dim = key_cache.shape
    clusters_dev = centroid_keys.shape[1]
    block_len = ctx_len // clusters_dev
    sel_count = selected.shape[2]
    query_count = queries.shape[2]
    model_dim = residual.shape[1]
    score_scale = 1.0 / math.sqrt(head_dim)
    query_f32 = queries.astype(jnp.float32)
    block_index = jnp.transpose(selected - ctx_pos * clusters_dev, (0, 2, 1))[:, :, None, :, None]
    key_blocks = key_cache.reshape(seq_count, clusters_dev, block_len, heads_kv, head_dim)
    value_blocks = value_cache.reshape(seq_count, clusters_dev, block_len, heads_kv, head_dim)
    picked_keys = jnp.take_along_axis(key_blocks, block_index, axis=1).reshape(
        seq_count, sel_count * block_len, heads_kv, head_dim
    )
    picked_values = jnp.take_along_axis(value_blocks, block_index, axis=1).reshape(
        seq_count, sel_count * block_len, heads_kv, head_dim
    )
    all_keys = jnp.concatenate([centroid_keys, picked_keys], 1).astype(jnp.float32)
    all_values = jnp.concatenate([centroid_values, picked_values], 1).astype(jnp.float32)
    scores = jnp.einsum("sgqd,sjgd->sgqj", query_f32, all_keys) * score_scale
    peak_local = jnp.max(scores, axis=-1)
    probs = jnp.exp(scores - peak_local[..., None])
    exp_total = jnp.sum(probs, axis=-1)
    weighted = jnp.einsum("sgqj,sjgd->sgqd", probs, all_values)
    heads_mine = query_count // ctx_devices
    peak_all, exp_total, weighted = joined((peak_local, exp_total, weighted), "ctx", combine_parts)
    exp_total = lax.dynamic_slice_in_dim(exp_total, ctx_pos * heads_mine, heads_mine, 2)
    weighted = lax.dynamic_slice_in_dim(weighted, ctx_pos * heads_mine, heads_mine, 2)
    peak_all = lax.dynamic_slice_in_dim(peak_all, ctx_pos * heads_mine, heads_mine, 2)
    own_queries = lax.dynamic_slice_in_dim(query_f32, ctx_pos * heads_mine, heads_mine, 2)
    own_score = jnp.einsum("sgqd,sgd->sgq", own_queries, new_key.astype(jnp.float32)) * score_scale
    new_peak = jnp.maximum(peak_all, own_score)
    keep_old = jnp.exp(peak_all - new_peak)
    keep_new = jnp.exp(own_score - new_peak)
    exp_total = exp_total * keep_old + keep_new
    weighted = (
        weighted * keep_old[..., None]
        + keep_new[..., None] * new_value.astype(jnp.float32)[:, :, None, :]
    )
    attended = (weighted / exp_total[..., None]).astype(jnp.bfloat16)
    projected = jnp.dot(
        attended.reshape(seq_count, -1),
        out_weight.reshape(-1, model_dim),
        preferred_element_type=jnp.float32,
    )
    projected = lax.psum(projected.astype(jnp.bfloat16), ("ctx", "kvh")).astype(jnp.float32)
    hidden1 = residual.astype(jnp.float32) + projected
    mean_square = jnp.mean(hidden1 * hidden1, axis=-1, keepdims=True)
    normed = (hidden1 * lax.rsqrt(mean_square + 1e-06) * norm_gain).astype(jnp.bfloat16)
    experts_all = ctx_devices * exp_devices
    top_count = expert_ids.shape[1]
    capacity = max(2, 2 * seq_count * top_count // experts_all)
    matches = expert_ids[:, :, None] == jnp.arange(experts_all, dtype=jnp.int32)[None, None, :]
    onehot = jnp.sum(matches.astype(jnp.int32), axis=1)
    weight = jnp.sum(jnp.where(matches, gate_weights[:, :, None], 0.0), axis=1)
    onehot = lax.dynamic_slice_in_dim(onehot, ctx_pos * exp_devices, exp_devices, 1)
    weight = lax.dynamic_slice_in_dim(weight, ctx_pos * exp_devices, exp_devices, 1)
    slot_rank = jnp.cumsum(onehot, axis=0) - onehot
    slot_ids = jnp.arange(capacity, dtype=jnp.int32)
    slot_table = (onehot.T[:, None, :] > 0) & (slot_rank.T[:, None, :] == slot_ids[None, :, None])
    outgoing = jnp.einsum(
        "xcs,sd->xcd", slot_table.astype(jnp.bfloat16), normed, preferred_element_type=jnp.float32
    ).astype(jnp.bfloat16)
    gate_up = w_gate_up.reshape(model_dim, -1)
    down_proj = w_down.reshape(-1, model_dim)
    half_width = down_proj.shape[0]
    block_slots = lax.all_to_all(outgoing, "exp", split_axis=0, concat_axis=0, tiled=True)
    flat_rows = block_slots.reshape(-1, model_dim)
    gate_up_out = jnp.dot(flat_rows, gate_up, preferred_element_type=jnp.float32)
    activated = (jax.nn.silu(gate_up_out[:, :half_width]) * gate_up_out[:, half_width:]).astype(
        jnp.bfloat16
    )
    results = jnp.dot(activated, down_proj, preferred_element_type=jnp.float32).reshape(
        block_slots.shape
    )
    returned = lax.all_to_all(
        results.astype(jnp.bfloat16), "exp", split_axis=0, concat_axis=0, tiled=True
    ).astype(results.dtype)
    combine_weights = slot_table.astype(jnp.float32) * weight.T[:, None, :]
    expert_mix = jnp.einsum(
        "xcs,xcd->sd", combine_weights, returned, precision=lax.Precision.HIGHEST
    )
    expert_mix = lax.psum_scatter(
        expert_mix.astype(jnp.bfloat16), ("ctx", "kvh"), scatter_dimension=1, tiled=True
    ).astype(jnp.float32)
    slice_width = expert_mix.shape[1]
    own_slice = lax.dynamic_slice_in_dim(
        hidden1, lax.axis_index(("ctx", "kvh")) * slice_width, slice_width, 1
    )
    return (own_slice + expert_mix).astype(jnp.bfloat16)


def solution(mesh):
    in_specs = (
        P("exp", "kvh", None, None),
        P("exp", "ctx", "kvh", None),
        P("exp", "ctx", "kvh", None),
        P("exp", "ctx", "kvh", None),
        P("exp", "ctx", "kvh", None),
        P("exp", "kvh", "ctx"),
        P("exp", "kvh", None),
        P("exp", "kvh", None),
        P("kvh", "ctx", None, None),
        P("exp", None),
        P(),
        P("exp", None),
        P("exp", None),
        P(("ctx", "exp"), None, None, "kvh"),
        P(("ctx", "exp"), "kvh", None),
    )
    out_specs = P("exp", ("ctx", "kvh"))
    return jax.shard_map(body, mesh=mesh, in_specs=in_specs, out_specs=out_specs, check_vma=False)
```

profile of v0, /device:TPU:0, one launch (start us, length us, event | category | flops | bytes accessed | tf_op | source)
XLA Modules:
  0.0 306.4 jit_solution(17252843379650628604)
XLA Ops:
  6.5 0.0 copy-start
  6.5 0.8 subtract_bitcast_fusion.1
  7.4 0.1 copy.101
  7.5 0.1 reshape.128
  7.6 3.4 %copy.109 = bf16[4,64,16,2,128]{4,2,3,1,0:T(8,128)(2,1)} copy(bf16[4,64,16,2,128]{4,3,2,1,0:T(2,128)(2,1)} %bitcast.110) | data formatting | bytes 4194304 | tf_op jit(solution)/shard_map/reshape | solution.py:60
  11.0 0.0 copy-done.1
  11.0 1.7 copy.102
  12.7 2.2 gather_fusion.1
  14.9 2.2 gather_fusion
  17.2 0.1 copy.99
  17.3 0.1 select_bitcast_fusion
  17.5 0.3 fusion.52
  17.8 0.2 fusion.15
  18.0 30.3 %all-gather.2 = f32[32,2,8,128]{3,2,1,0:T(8,128)S(1)} all-gather(f32[4,2,8,128]{3,2,1,0:T(8,128)S(1)} %fusion.15), channel_id=4, replica_groups=mesh['ctx'=8,'kvh'=2,'exp'=8] {'ctx'}, dimensions={0}, use_global_device_ids=true | all-gather | bytes 294912 | tf_op jit(solution)/shard_map/all_gather | solution.py:10
  48.4 0.2 fusion.25
  48.6 28.1 %all-gather.1 = f32[32,2,8]{2,1,0:T(2,128)S(1)} all-gather(f32[4,2,8]{2,1,0:T(2,128)S(1)} %fusion.25), channel_id=3, replica_groups=mesh['ctx'=8,'kvh'=2,'exp'=8] {'ctx'}, dimensions={0}, use_global_device_ids=true | all-gather | bytes 2304 | tf_op jit(solution)/shard_map/all_gather | solution.py:10
  76.7 28.1 %all-gather = f32[32,2,8]{2,1,0:T(2,128)S(1)} all-gather(f32[4,2,8]{2,1,0:T(2,128)S(1)} %get-tuple-element.75), channel_id=2, replica_groups=mesh['ctx'=8,'kvh'=2,'exp'=8] {'ctx'}, dimensions={0}, use_global_device_ids=true | all-gather | bytes 2304 | tf_op jit(solution)/shard_map/all_gather | solution.py:10
  104.8 1.0 while.14
  104.8 0.1 fusion.60
  104.9 0.1 fusion.60
  105.1 0.1 fusion.60
  105.2 0.1 fusion.60
  105.3 0.1 fusion.60
  105.5 0.1 fusion.60
  105.6 0.1 fusion.60
  105.7 0.1 copy.112
  105.8 0.1 copy.115
  105.9 0.0 copy-done.8
  105.9 0.1 fusion.28
  106.0 0.1 copy.141
  106.1 0.1 copy.114
  106.2 0.1 copy.113
  106.3 0.1 copy.116
  106.4 0.1 convert_multiply_fusion.1
  106.5 0.1 divide_convert_fusion
  106.6 0.0 copy-done
  106.6 0.4 fusion.8
  107.0 74.3 %psum.7 = bf16[4,4096]{1,0:T(4,128)(2,1)S(1)} all-reduce(bf16[4,4096]{1,0:T(4,128)(2,1)S(1)} %fusion.8), channel_id=1, replica_groups=mesh['ctx'=8,'kvh'=2,'exp'=8] {'ctx','kvh'}, use_global_device_ids=true, to_apply=%region_4.6 | all-reduce | flops 16384 | bytes 65536 | tf_op jit(solution)/shard_map/psum | solution.py:95
  181.2 0.1 convert_add_fusion
  181.4 0.0 copy-done.6
  181.4 0.1 convert_reduce_fusion
  181.5 0.1 compare_bitcast_fusion
  181.6 0.0 copy-done.5
  181.6 0.2 convolution_convert_fusion
  181.9 0.8 copy.118
  182.7 4.5 %all-to-all-start = ((bf16[8,2,4096]{2,1,0:T(2,128)(2,1)}), bf16[8,2,4096]{2,1,0:T(2,128)(2,1)S(1)}, u32[]{:S(2)}, u32[]{:S(2)}) async-start(bf16[8,2,4096]{2,1,0:T(2,128)(2,1)} %copy.118), calls=%async_computation | async-start | bytes 262144 | tf_op jit(solution)/shard_map/all_to_all | solution.py:116
  187.1 13.1 %copy.140 = bf16[512,8,2,768]{3,1,2,0:T(8,128)(2,1)} copy(bf16[512,8,2,768]{3,2,1,0:T(2,128)(2,1)} %bitcast.108) | data formatting | bytes 25165824
  200.2 0.0 all-to-all-done
  200.2 0.1 reshape.89
  200.3 6.3 %fusion.53 = f32[16,1536]{1,0:T(8,128)S(1)} fusion(bf16[16,4096]{1,0:T(8,128)(2,1)S(1)} %reshape.89, bf16[4096,1536]{1,0:T(8,128)(2,1)} %bitcast.107), kind=kOutput, calls=%fused_computation.88 | convolution fusion | flops 201326592 | bytes 12812288 | tf_op jit(solution)/shard_map/dot_general | solution.py:118
  206.7 0.0 copy-start.7
  206.7 3.7 %fusion.5 = bf16[8,2,4096]{2,0,1:T(8,128)(2,1)S(1)} fusion(bf16[1,768,4096]{2,1,0:T(8,128)(2,1)} %param.33, bf16[8,2,768]{2,1,0:T(2,128)(2,1)S(1)} %dot_general.32), kind=kOutput, calls=%fused_computation.12 | convolution fusion | flops 100728832 | bytes 6447104 | tf_op jit(solution)/shard_map/dot_general | solution.py:122
  210.4 0.8 copy.120
  211.2 4.8 %all-to-all-start.1 = ((bf16[8,2,4096]{2,1,0:T(2,128)(2,1)}), bf16[8,2,4096]{2,1,0:T(2,128)(2,1)S(1)}, u32[]{:S(2)}, u32[]{:S(2)}) async-start(bf16[8,2,4096]{2,1,0:T(2,128)(2,1)} %copy.120), calls=%async_computation.1 | async-start | bytes 262144 | tf_op jit(solution)/shard_map/all_to_all | solution.py:125
  216.0 0.0 reduce-scatter.4.cloned.1.call-start
  216.0 0.1 select_reduce_fusion
  216.1 0.1 dynamic-slice_bitcast_fusion
  216.2 5.9 %all-to-all-done.1 = bf16[8,2,4096]{2,1,0:T(2,128)(2,1)S(1)} async-done(((bf16[8,2,4096]{2,1,0:T(2,128)(2,1)}), bf16[8,2,4096]{2,1,0:T(2,128)(2,1)S(1)}, u32[]{:S(2)}, u32[]{:S(2)}) %all-to-all-start.1) | async-done | bytes 131104 | tf_op jit(solution)/shard_map/all_to_all | solution.py:125
  222.1 0.3 fusion.9
  222.4 1.4 copy.137
  223.8 0.0 reduce-scatter.4.cloned.1.call-update
  223.8 74.2 %reduce-scatter.4.cloned.1.call-done = bf16[256,4]{1,0:T(8,128)(2,1)} async-done(((bf16[4096,4]{1,0:T(8,128)(2,1)}), bf16[256,4]{1,0:T(8,128)(2,1)}) %reduce-scatter.4.cloned.1.call-update) | async-done | bytes 2064
  298.0 0.9 copy.138
  298.9 0.6 add_convert_fusion
  (42 shorter events, 0.5 us)
Async XLA Ops:
  6.5 100.1 %copy-start = (bf16[2,1,128,4096]{3,2,1,0:T(8,128)(2,1)S(1)}, bf16[2,1,128,4096]{3,2,1,0:T(8,128)(2,1)}, u32[]{:S(2)}) copy-start(bf16[2,1,128,4096]{3,2,1,0:T(8,128)(2,1)} %param.27) | copy-start | bytes 6291460
  7.6 3.4 %copy-start.1 = (bf16[4,1024,2,128]{3,2,1,0:T(2,128)(2,1)S(1)}, bf16[4,1024,2,128]{3,2,1,0:T(2,128)(2,1)}, u32[]{:S(2)}) copy-start(bf16[4,1024,2,128]{3,2,1,0:T(2,128)(2,1)} %param.20) | copy-start | bytes 6291460
  11.0 6.4 %copy-start.2 = (bf16[4,64,2,128]{3,2,1,0:T(2,128)(2,1)S(1)}, bf16[4,64,2,128]{3,2,1,0:T(2,128)(2,1)}, u32[]{:S(2)}) copy-start(bf16[4,64,2,128]{3,2,1,0:T(2,128)(2,1)} %param.22) | copy-start | bytes 393220
  11.0 6.4 %copy-start.3 = (bf16[4,64,2,128]{3,2,1,0:T(2,128)(2,1)S(1)}, bf16[4,64,2,128]{3,2,1,0:T(2,128)(2,1)}, u32[]{:S(2)}) copy-start(bf16[4,64,2,128]{3,2,1,0:T(2,128)(2,1)} %param.23) | copy-start | bytes 393220
  11.0 6.5 %copy-start.10 = (bf16[4,2,8,128]{3,2,1,0:T(8,128)(2,1)S(1)}, bf16[4,2,8,128]{3,2,1,0:T(8,128)(2,1)}, u32[]{:S(2)}) copy-start(bf16[4,2,8,128]{3,2,1,0:T(8,128)(2,1)} %param.19) | copy-start | bytes 49156
  12.7 93.2 %copy-start.8 = (bf16[4,2,128]{2,1,0:T(2,128)(2,1)S(1)}, bf16[4,2,128]{2,1,0:T(2,128)(2,1)}, u32[]{:S(2)}) copy-start(bf16[4,2,128]{2,1,0:T(2,128)(2,1)} %param.25) | copy-start | bytes 6148
  12.7 93.7 %copy-start.9 = (bf16[4,2,128]{2,1,0:T(2,128)(2,1)S(1)}, bf16[4,2,128]{2,1,0:T(2,128)(2,1)}, u32[]{:S(2)}) copy-start(bf16[4,2,128]{2,1,0:T(2,128)(2,1)} %param.26) | copy-start | bytes 6148
  18.0 163.2 %copy-start.4 = (bf16[4,4096]{1,0:T(4,128)(2,1)S(1)}, bf16[4,4096]{1,0:T(4,128)(2,1)}, u32[]{:S(2)}) copy-start(bf16[4,4096]{1,0:T(4,128)(2,1)} %param.28) | copy-start | bytes 98308
  48.4 133.0 %copy-start.6 = (s32[4,8]{1,0:T(4,128)S(1)}, s32[4,8]{1,0:T(4,128)}, u32[]{:S(2)}) copy-start(s32[4,8]{1,0:T(4,128)} %param.30) | copy-start | bytes 388
  48.4 133.3 %copy-start.5 = (f32[4096]{0:T(1024)S(1)}, f32[4096]{0:T(1024)}, u32[]{:S(2)}) copy-start(f32[4096]{0:T(1024)} %param.29) | copy-start | bytes 49156
  182.7 17.6 %all-to-all-start = ((bf16[8,2,4096]{2,1,0:T(2,128)(2,1)}), bf16[8,2,4096]{2,1,0:T(2,128)(2,1)S(1)}, u32[]{:S(2)}, u32[]{:S(2)}) async-start(bf16[8,2,4096]{2,1,0:T(2,128)(2,1)} %copy.118), calls=%async_computation | async-start | bytes 262144 | tf_op jit(solution)/shard_map/all_to_all | solution.py:116
  206.7 9.3 %copy-start.7 = (f32[4,8]{1,0:T(4,128)S(1)}, f32[4,8]{1,0:T(4,128)}, u32[]{:S(2)}) copy-start(f32[4,8]{1,0:T(4,128)} %param.31) | copy-start | bytes 388
  211.2 10.9 %all-to-all-start.1 = ((bf16[8,2,4096]{2,1,0:T(2,128)(2,1)}), bf16[8,2,4096]{2,1,0:T(2,128)(2,1)S(1)}, u32[]{:S(2)}, u32[]{:S(2)}) async-start(bf16[8,2,4096]{2,1,0:T(2,128)(2,1)} %copy.120), calls=%async_computation.1 | async-start | bytes 262144 | tf_op jit(solution)/shard_map/all_to_all | solution.py:125
  216.0 82.1 %reduce-scatter.4.cloned.1.call-start = ((), (), s32[]{:S(2)}) async-start(), calls=%async_computation.3 | async-start | bytes 1114112
Sparse Core Ops, SparseCore 0:
  223.9 74.0 reduce-scatter.3
where the time goes:
time: 307 us; the launch traced here: 306 us
  blocking collectives  161 us (52%)
  waiting for transfers between devices  80.1 us (26%)
  local copies, waits for them, and re-layouts  27.7 us (9%)
  between operations  13.6 us (4%)
  matrix products  11.4 us (4%)
  starting transfers between devices  9.3 us (3%)
  other arithmetic  3.3 us (1%)
    all_gather x3, blocking collectives, joined(): pieces = jax.tree.map(lambda part: lax.all_gather(part, axis), value)  86.5 us
    psum x1, blocking collectives, body(): lax.psum(projected.astype(jnp.bfloat16), ('ctx', 'kvh')).astype(jnp.float32)  74.3 us
    unnamed x2, waiting for transfers between devices  74.2 us
    unnamed x28, local copies, waits for them, and re-layouts  15.6 us
    dot_general x1, matrix products, body(): jnp.dot(flat_rows, gate_up, preferred_element_type=jnp.float32)  6.3 us
  transfers between devices with their start and end apart: 3, of which 2 were waited for; matrix products, arithmetic and copies ran while one was open for 4% of the time, Pallas kernels for 0%

commit v1 on v0

v1 whole, which is shorter than its diff:
```python
import functools
import math

import jax
import jax.numpy as jnp
from jax import lax
from jax.experimental import pallas as pl
from jax.experimental.pallas import tpu as pltpu
from jax.sharding import PartitionSpec as P

VMEM_SPEC = pl.BlockSpec(memory_space=pltpu.VMEM)
SMEM_SPEC = pl.BlockSpec(memory_space=pltpu.SMEM)
ANY_SPEC = pl.BlockSpec(memory_space=pl.ANY)
MASKED = -1e30


def attention_kernel(
    selected,
    queries,
    new_key,
    new_value,
    centroid_keys,
    centroid_values,
    key_cache,
    value_cache,
    out,
    keys,
    values,
    picked_sem,
    centroid_sem,
):
    seq_count, heads_kv, query_count, head_dim = queries.shape
    clusters = centroid_keys.shape[1]
    sel_count = selected.shape[2]
    block_len = key_cache.shape[1] // clusters
    ctx_pos = lax.axis_index("ctx")
    copies = []
    for which, (source, held) in enumerate(((centroid_keys, keys), (centroid_values, values))):
        copies.append(
            pltpu.make_async_copy(source, held.at[:, pl.ds(0, clusters)], centroid_sem.at[which])
        )
    for s in range(seq_count):
        for g in range(heads_kv):
            for j in range(sel_count):
                block = selected[s, g, j] - ctx_pos * clusters
                place = clusters + (g * sel_count + j) * block_len
                for which, (source, held) in enumerate(((key_cache, keys), (value_cache, values))):
                    copies.append(
                        pltpu.make_async_copy(
                            source.at[s, pl.ds(block * block_len, block_len)],
                            held.at[s, pl.ds(place, block_len)],
                            picked_sem.at[which, s, g * sel_count + j],
                        )
                    )
    for copy in copies:
        copy.start()
    for copy in copies:
        copy.wait()
    positions = keys.shape[1]
    rows = positions * heads_kv
    flat_keys = keys.reshape(seq_count, rows, head_dim)
    flat_values = values.reshape(seq_count, rows, head_dim)
    shape = (heads_kv * query_count, rows)
    head_of_query = lax.broadcasted_iota(jnp.int32, shape, 0) // query_count
    column = lax.broadcasted_iota(jnp.int32, shape, 1)
    head_of_row = column % heads_kv
    position = column // heads_kv
    head_of_block = (position - clusters) // (sel_count * block_len)
    valid = (head_of_row == head_of_query) & (
        (position < clusters) | (head_of_block == head_of_query)
    )
    score_scale = 1.0 / math.sqrt(head_dim)
    for s in range(seq_count):
        query = queries[s].reshape(heads_kv * query_count, head_dim)
        scores = lax.dot_general(
            query, flat_keys[s], (((1,), (1,)), ((), ())), preferred_element_type=jnp.float32
        )
        scores = jnp.where(valid, scores * score_scale, MASKED)
        own = jnp.sum(
            queries[s].astype(jnp.float32) * new_key[s].astype(jnp.float32)[:, None, :],
            axis=-1,
            keepdims=True,
        ).reshape(heads_kv * query_count, 1)
        own = jnp.where(ctx_pos == 0, own * score_scale, MASKED)
        peak = jnp.maximum(jnp.max(scores, axis=-1, keepdims=True), own)
        probs = jnp.exp(scores - peak)
        own_prob = jnp.exp(own - peak)
        total = jnp.sum(probs, axis=-1, keepdims=True) + own_prob
        weighted = jnp.dot(
            probs.astype(jnp.bfloat16), flat_values[s], preferred_element_type=jnp.float32
        )
        own_value = jnp.broadcast_to(
            new_value[s].astype(jnp.float32)[:, None, :], (heads_kv, query_count, head_dim)
        ).reshape(heads_kv * query_count, head_dim)
        weighted = weighted + own_prob * own_value
        lane = lax.broadcasted_iota(jnp.int32, weighted.shape, 1)
        stats = jnp.where(lane < head_dim // 2, peak, total)
        for g in range(heads_kv):
            part = slice(g * query_count, (g + 1) * query_count)
            out[:, g * seq_count + s, :] = weighted[part]
            out[:, (heads_kv + g) * seq_count + s, :] = stats[part]


def attention(queries, key_cache, value_cache, centroid_keys, centroid_values, selected, new_key, new_value):
    seq_count, heads_kv, query_count, head_dim = queries.shape
    clusters = centroid_keys.shape[1]
    sel_count = selected.shape[2]
    block_len = key_cache.shape[1] // clusters
    held = pltpu.VMEM(
        (seq_count, clusters + heads_kv * sel_count * block_len, heads_kv, head_dim), jnp.bfloat16
    )
    return pl.pallas_call(
        attention_kernel,
        out_shape=jax.ShapeDtypeStruct((query_count, 2 * heads_kv * seq_count, head_dim), jnp.float32),
        in_specs=[SMEM_SPEC, VMEM_SPEC, VMEM_SPEC, VMEM_SPEC] + [ANY_SPEC] * 4,
        out_specs=VMEM_SPEC,
        scratch_shapes=[
            held,
            held,
            pltpu.SemaphoreType.DMA((2, seq_count, heads_kv * sel_count)),
            pltpu.SemaphoreType.DMA((2,)),
        ],
        compiler_params=pltpu.CompilerParams(vmem_limit_bytes=8 << 20),
    )(selected, queries, new_key, new_value, centroid_keys, centroid_values, key_cache, value_cache)


def project_kernel(parts, weight, out):
    rows = parts.shape[1] // 2
    half = parts.shape[2] // 2
    weighted = parts[:, :rows, :]
    peak = parts[:, rows:, 0:1]
    total = parts[:, rows:, half : half + 1]
    scale = jnp.exp(peak - jnp.max(peak, axis=0, keepdims=True))
    total = jnp.sum(total * scale, axis=0)
    attended = (jnp.sum(weighted * scale, axis=0) / total).astype(jnp.bfloat16)
    seq_count = out.shape[0]
    sums = None
    for g in range(weight.shape[0]):
        term = jnp.dot(
            attended[g * seq_count : (g + 1) * seq_count],
            weight[g, 0],
            preferred_element_type=jnp.float32,
        )
        sums = term if sums is None else sums + term
    out[...] = sums.astype(jnp.bfloat16)


def project(parts, weight):
    seq_count = parts.shape[1] // (2 * weight.shape[0])
    return pl.pallas_call(
        project_kernel,
        out_shape=jax.ShapeDtypeStruct((seq_count, weight.shape[3]), jnp.bfloat16),
        in_specs=[VMEM_SPEC, VMEM_SPEC],
        out_specs=VMEM_SPEC,
        compiler_params=pltpu.CompilerParams(vmem_limit_bytes=8 << 20),
    )(parts, weight)


def experts_kernel(
    blocks, chunks, x0, x1, x2, x3, gate_up, down, out, gate_up_held, down_held, spread, sem_up, sem_down
):
    block_rows, model_dim = x0.shape
    rows = 4 * block_rows
    tiles = gate_up.shape[3] // 128
    part = model_dim // chunks
    width = 1024
    exp_pos = lax.axis_index("exp")

    def up_copy(c, t):
        return pltpu.make_async_copy(
            gate_up.at[0, pl.ds(c * part, part), :, pl.ds(t * 128, 128)],
            gate_up_held.at[t, pl.ds(c * part, part)],
            sem_up.at[c, t],
        )

    def down_copy(j):
        return pltpu.make_async_copy(
            down.at[0, :, pl.ds(j * width, width)],
            down_held.at[:, pl.ds(j * width, width)],
            sem_down.at[j],
        )

    for c in range(chunks):
        for t in range(tiles):
            up_copy(c, t).start()
    for j in range(model_dim // width):
        down_copy(j).start()
    source = lax.broadcasted_iota(jnp.int32, (128, 256), 0)
    target = lax.broadcasted_iota(jnp.int32, (128, 256), 1)
    to_even = jnp.where(target == 2 * source, 1.0, 0.0).astype(jnp.bfloat16)
    to_odd = jnp.where(target == 2 * source + 1, 1.0, 0.0).astype(jnp.bfloat16)
    for k in range(model_dim // 128):
        piece = jnp.concatenate([x[:, k * 128 : (k + 1) * 128] for x in (x0, x1, x2, x3)], axis=0)
        columns = slice(k * 256, (k + 1) * 256)
        spread[0:rows, columns] = jnp.dot(
            piece, to_even, preferred_element_type=jnp.float32
        ).astype(jnp.bfloat16)
        spread[rows : 2 * rows, columns] = jnp.dot(
            piece, to_odd, preferred_element_type=jnp.float32
        ).astype(jnp.bfloat16)
    flat = gate_up_held.reshape(tiles, 2 * model_dim, 128)
    sums = [jnp.zeros((2 * rows, 256), jnp.float32) for _ in range(tiles // 2)]
    for c in range(chunks):
        for t in range(tiles):
            up_copy(c, t).wait()
        left = spread[:, c * 2 * part : (c + 1) * 2 * part]
        here = pl.ds(c * 2 * part, 2 * part)
        for u in range(tiles // 2):
            right = jnp.concatenate([flat[2 * u, here, :], flat[2 * u + 1, here, :]], axis=1)
            sums[u] = sums[u] + jnp.dot(left, right, preferred_element_type=jnp.float32)
    both = jnp.concatenate(sums, axis=1)
    gate, up = both[:rows], both[rows:]
    activated = (jax.nn.silu(gate) * up).astype(jnp.bfloat16)
    for j in range(model_dim // width):
        down_copy(j).wait()
        for q in range(width // 256):
            b = j * (width // 256) + q
            result = jnp.dot(
                activated, down_held[:, b * 256 : (b + 1) * 256], preferred_element_type=jnp.float32
            )
            for i in range(blocks):
                seq_count = rows // blocks
                piece = result[i * seq_count : (i + 1) * seq_count].astype(jnp.bfloat16)
                out[b * blocks + lax.bitwise_xor(exp_pos, i)] = piece


def experts(pieces, gate_up, down, blocks):
    block_rows, model_dim = pieces[0].shape
    rows = 4 * block_rows
    hidden = down.shape[1]
    tiles = hidden // 128
    chunks = 8
    return pl.pallas_call(
        functools.partial(experts_kernel, blocks, chunks),
        out_shape=jax.ShapeDtypeStruct(
            (model_dim // 256 * blocks, rows // blocks, 256), jnp.bfloat16
        ),
        in_specs=[VMEM_SPEC] * 4 + [ANY_SPEC] * 2,
        out_specs=VMEM_SPEC,
        scratch_shapes=[
            pltpu.VMEM((tiles, model_dim, 2, 128), jnp.bfloat16),
            pltpu.VMEM((hidden, model_dim), jnp.bfloat16),
            pltpu.VMEM((2 * rows, 2 * model_dim), jnp.bfloat16),
            pltpu.SemaphoreType.DMA((chunks, tiles)),
            pltpu.SemaphoreType.DMA((model_dim // 1024,)),
        ],
        compiler_params=pltpu.CompilerParams(vmem_limit_bytes=28 << 20),
    )(*pieces, gate_up, down)


def swapped(value, axes, count, mask):
    return lax.ppermute(value, axes, [(i, i ^ mask) for i in range(count)])


def body(
    queries,
    key_cache,
    value_cache,
    centroid_keys,
    centroid_values,
    selected,
    new_key,
    new_value,
    out_weight,
    residual,
    norm_gain,
    expert_ids,
    gate_weights,
    w_gate_up,
    w_down,
):
    ctx_devices = lax.axis_size("ctx")
    kvh_devices = lax.axis_size("kvh")
    exp_devices = lax.axis_size("exp")
    seq_count, model_dim = residual.shape
    plane = ctx_devices * kvh_devices

    parts = attention(
        queries, key_cache, value_cache, centroid_keys, centroid_values, selected, new_key, new_value
    )
    parts = lax.all_to_all(parts, "ctx", split_axis=0, concat_axis=0, tiled=True)
    projected = project(parts, out_weight)

    axes = ("ctx", "kvh")
    along_x = [swapped(projected, axes, plane, m) for m in (1, 2, 3)]
    sums = projected.astype(jnp.float32)
    for piece in along_x:
        sums = sums + piece.astype(jnp.float32)
    sums = sums.astype(jnp.bfloat16)
    along_z = [swapped(sums, axes, plane, m) for m in range(4, plane, 4)]
    sums = sums.astype(jnp.float32)
    for piece in along_z:
        sums = sums + piece.astype(jnp.float32)
    hidden1 = residual.astype(jnp.float32) + sums
    mean_square = jnp.mean(hidden1 * hidden1, axis=-1, keepdims=True)
    normed = (hidden1 * lax.rsqrt(mean_square + 1e-06) * norm_gain).astype(jnp.bfloat16)

    other = swapped(normed, "exp", exp_devices, 1)
    pair = jnp.concatenate([normed, other], axis=0)
    pieces = [pair] + [swapped(pair, "exp", exp_devices, m) for m in range(2, exp_devices, 2)]
    results = experts(pieces, w_gate_up, w_down, exp_devices)
    returned = lax.all_to_all(
        results, ("ctx", "kvh", "exp"), split_axis=0, concat_axis=0, tiled=True
    )

    expert = jnp.arange(ctx_devices * exp_devices, dtype=jnp.int32)
    matches = expert_ids[:, :, None] == expert[None, None, :]
    weight = jnp.sum(jnp.where(matches, gate_weights[:, :, None], 0.0), axis=1)
    weight = weight.T.reshape(ctx_devices, 1, exp_devices, seq_count)
    weight = jnp.broadcast_to(weight, (ctx_devices, kvh_devices, exp_devices, seq_count))
    weight = weight.reshape(ctx_devices * kvh_devices * exp_devices, seq_count, 1)
    expert_mix = jnp.sum(returned.astype(jnp.float32) * weight, axis=0)
    slice_width = expert_mix.shape[1]
    own_slice = lax.dynamic_slice_in_dim(
        hidden1, lax.axis_index(("ctx", "kvh")) * slice_width, slice_width, 1
    )
    return (own_slice + expert_mix).astype(jnp.bfloat16)


def solution(mesh):
    in_specs = (
        P("exp", "kvh", None, None),
        P("exp", "ctx", "kvh", None),
        P("exp", "ctx", "kvh", None),
        P("exp", "ctx", "kvh", None),
        P("exp", "ctx", "kvh", None),
        P("exp", "kvh", "ctx"),
        P("exp", "kvh", None),
        P("exp", "kvh", None),
        P("kvh", "ctx", None, None),
        P("exp", None),
        P(),
        P("exp", None),
        P("exp", None),
        P(("ctx", "exp"), None, None, "kvh"),
        P(("ctx", "exp"), "kvh", None),
    )
    out_specs = P("exp", ("ctx", "kvh"))
    return jax.shard_map(body, mesh=mesh, in_specs=in_specs, out_specs=out_specs, check_vma=False)
```

time: 307 us -> 95.3 us (0.31)
  the two profiles are of different devices: /device:TPU:0 before, /device:TPU:1 now
where the time goes in v1:
time: 95.3 us; the launch traced here: 94.9 us
  Pallas kernels  23.5 us (25%)
  waiting for transfers between devices  22.1 us (23%)
  starting transfers between devices  22 us (23%)
  local copies, waits for them, and re-layouts  14.1 us (15%)
  blocking collectives  11.8 us (12%)
  other arithmetic  1.23 us (1%)
    pallas_call x1, Pallas kernels, experts(): pl.pallas_call(functools.partial(experts_kernel, blocks, chunks), out_sha...  20.4 us
    ppermute x10, starting transfers between devices, swapped(): return lax.ppermute(value, axes, [(i, i ^ mask) for i in range(count)])  16.4 us
    unnamed x29, local copies, waits for them, and re-layouts  14 us
    all_to_all x1, blocking collectives, body(): lax.all_to_all(parts, 'ctx', split_axis=0, concat_axis=0, tiled=True)  11.8 us
    all_to_all x1, waiting for transfers between devices, body(): lax.all_to_all(results, ('ctx', 'kvh', 'exp'), split_axis=0, concat_axis=...  11.1 us
    ppermute x10, waiting for transfers between devices, swapped(): return lax.ppermute(value, axes, [(i, i ^ mask) for i in range(count)])  11 us
    all_to_all x1, starting transfers between devices, body(): lax.all_to_all(results, ('ctx', 'kvh', 'exp'), split_axis=0, concat_axis=...  5.58 us
    pallas_call x1, Pallas kernels, attention(): pl.pallas_call(attention_kernel, out_shape=jax.ShapeDtypeStruct((query_co...  2.61 us
  transfers between devices with their start and end apart: 11, of which 9 were waited for; matrix products, arithmetic and copies ran while one was open for 0% of the time, Pallas kernels for 0%

profile of v1, /device:TPU:1, one launch (start us, length us, event | category | flops | bytes accessed | tf_op | source)
XLA Modules:
  0.0 94.9 jit_solution(2989886774072651696)
XLA Ops:
  0.0 0.8 copy.17.selected
  0.8 0.0 copy-start.2
  0.8 1.6 %copy-done.2 = bf16[4,1024,2,128]{3,2,1,0:T(2,128)(2,1)S(1)} copy-done((bf16[4,1024,2,128]{3,2,1,0:T(2,128)(2,1)S(1)}, bf16[4,1024,2,128]{3,2,1,0:T(2,128)(2,1)}, u32[]{:S(2)}) %copy-start.2) | copy-done | bytes 2097176
  2.4 0.0 copy-start.3
  2.4 1.6 %copy-done.3 = bf16[4,1024,2,128]{3,2,1,0:T(2,128)(2,1)S(1)} copy-done((bf16[4,1024,2,128]{3,2,1,0:T(2,128)(2,1)S(1)}, bf16[4,1024,2,128]{3,2,1,0:T(2,128)(2,1)}, u32[]{:S(2)}) %copy-start.3) | copy-done | bytes 2097176
  4.0 0.0 copy-start.5
  4.0 0.9 copy-done.5
  4.9 0.0 copy-start.6
  4.9 0.9 copy-done.6
  5.8 0.0 copy-start.7
  5.8 0.7 copy-done.7
  6.5 0.0 copy-start.8
  6.5 0.7 copy-done.8
  7.2 0.0 copy-start.9
  7.2 0.7 copy-done.9
  7.8 0.0 copy-start.1
  7.9 2.6 %shard_map.145 = f32[8,16,128]{2,1,0:T(8,128)S(1)} custom-call(s32[4,2,2]{2,1,0:T(2,128)S(1)} %copy.17.selected, bf16[4,2,8,128]{3,2,1,0:T(8,128)(2,1)S(1)} %copy-done.7, bf16[4,2,128]{2,1,0:T(2,128)(2,1)S(1)} %copy-done.8, bf16[4,2,128]{2,1,0:T(2,128)(2,1)S(1)} %copy-done.9, bf16[4,64,2,128]{3,2,1,0:T(2,128)(2,1)S(1)} %copy-done.5, ...), custom_call_target="tpu_custom_call" | custom-call | tf_op jit(solution)/shard_map/pallas_call | solution.py:112
  10.5 11.8 %all_to_all.10.parts = f32[8,16,128]{2,1,0:T(8,128)S(1)} all-to-all(f32[8,16,128]{2,1,0:T(8,128)S(1)} %shard_map.145), channel_id=1, replica_groups=mesh['ctx'=8,'kvh'=2,'exp'=8] {'ctx'}, dimensions={0} | all-to-all | bytes 131072 | tf_op jit(solution)/shard_map/all_to_all | solution.py:281
  22.3 0.0 copy-start.4
  22.3 1.6 %copy-done.4 = bf16[2,1,128,4096]{3,2,1,0:T(8,128)(2,1)S(1)} copy-done((bf16[2,1,128,4096]{3,2,1,0:T(8,128)(2,1)S(1)}, bf16[2,1,128,4096]{3,2,1,0:T(8,128)(2,1)}, u32[]{:S(2)}) %copy-start.4) | copy-done | bytes 2097176
  23.8 0.0 copy-start.10
  23.8 0.0 copy-start.11
  23.9 0.5 shard_map.146
  24.4 2.5 %collective-permute-start = (bf16[4,4096]{1,0:T(4,128)(2,1)S(1)}, bf16[4,4096]{1,0:T(4,128)(2,1)S(1)}, u32[]{:S(2)}, u32[]{:S(2)}) collective-permute-start(bf16[4,4096]{1,0:T(4,128)(2,1)S(1)} %shard_map.146), channel_id=1, source_target_pairs={{0,8},{8,0},{16,24},{24,16},{32,40},{40,32},{48,56},{56,48},{64,72... | collective-permute-start | bytes 98312 | tf_op jit(solution)/shard_map/ppermute | solution.py:252
  26.9 0.0 collective-permute-start.1
  26.9 0.8 collective-permute-start.2
  27.7 1.0 %collective-permute-done = bf16[4,4096]{1,0:T(4,128)(2,1)S(1)} collective-permute-done((bf16[4,4096]{1,0:T(4,128)(2,1)S(1)}, bf16[4,4096]{1,0:T(4,128)(2,1)S(1)}, u32[]{:S(2)}, u32[]{:S(2)}) %collective-permute-start) | collective-permute-done | bytes 32800 | tf_op jit(solution)/shard_map/ppermute | solution.py:252
  28.7 0.9 collective-permute-done.1
  29.7 1.5 %collective-permute-done.2 = bf16[4,4096]{1,0:T(4,128)(2,1)S(1)} collective-permute-done((bf16[4,4096]{1,0:T(4,128)(2,1)S(1)}, bf16[4,4096]{1,0:T(4,128)(2,1)S(1)}, u32[]{:S(2)}, u32[]{:S(2)}) %collective-permute-start.2) | collective-permute-done | bytes 32800 | tf_op jit(solution)/shard_map/ppermute | solution.py:252
  31.2 0.4 collective-permute-start.3
  31.6 1.8 %collective-permute-start.4 = (bf16[4,4096]{1,0:T(4,128)(2,1)S(1)}, bf16[4,4096]{1,0:T(4,128)(2,1)S(1)}, u32[]{:S(2)}, u32[]{:S(2)}) collective-permute-start(bf16[4,4096]{1,0:T(4,128)(2,1)S(1)} %add_convert_fusion), channel_id=1, source_target_pairs={{0,64},{8,72},{16,80},{24,88},{32,96},{40,104},{48,112},{56,120},{... | collective-permute-start | bytes 98312 | tf_op jit(solution)/shard_map/ppermute | solution.py:252
  33.4 1.8 %collective-permute-start.5 = (bf16[4,4096]{1,0:T(4,128)(2,1)S(1)}, bf16[4,4096]{1,0:T(4,128)(2,1)S(1)}, u32[]{:S(2)}, u32[]{:S(2)}) collective-permute-start(bf16[4,4096]{1,0:T(4,128)(2,1)S(1)} %add_convert_fusion), channel_id=1, source_target_pairs={{0,96},{8,104},{16,112},{24,120},{32,64},{40,72},{48,80},{56,88},{... | collective-permute-start | bytes 98312 | tf_op jit(solution)/shard_map/ppermute | solution.py:252
  35.2 0.0 collective-permute-done.3
  35.2 0.7 collective-permute-done.4
  35.8 1.5 %collective-permute-done.5 = bf16[4,4096]{1,0:T(4,128)(2,1)S(1)} collective-permute-done((bf16[4,4096]{1,0:T(4,128)(2,1)S(1)}, bf16[4,4096]{1,0:T(4,128)(2,1)S(1)}, u32[]{:S(2)}, u32[]{:S(2)}) %collective-permute-start.5) | collective-permute-done | bytes 32800 | tf_op jit(solution)/shard_map/ppermute | solution.py:252
  37.3 0.0 copy-done.10
  37.3 0.2 multiply_reduce_fusion.1
  37.5 0.0 copy-done.11
  37.5 0.1 multiply_convert_fusion
  37.6 5.2 %collective-permute-start.6 = (bf16[4,4096]{1,0:T(4,128)(2,1)S(1)}, bf16[4,4096]{1,0:T(4,128)(2,1)S(1)}, u32[]{:S(2)}, u32[]{:S(2)}) collective-permute-start(bf16[4,4096]{1,0:T(4,128)(2,1)S(1)} %multiply_convert_fusion), channel_id=1, source_target_pairs={{0,1},{1,0},{2,3},{3,2},{4,5},{5,4},{6,7},{7,6},{8,9},{9,8},{10,11... | collective-permute-start | bytes 98312 | tf_op jit(solution)/shard_map/ppermute | solution.py:252
  42.8 0.9 collective-permute-done.6
  43.6 0.0 copy-start.12
  43.6 0.0 copy-start.13
  43.7 1.4 %collective-permute-start.7 = (bf16[8,4096]{1,0:T(8,128)(2,1)S(1)}, bf16[8,4096]{1,0:T(8,128)(2,1)S(1)}, u32[]{:S(2)}, u32[]{:S(2)}) collective-permute-start(bf16[8,4096]{1,0:T(8,128)(2,1)S(1)} %pad_maximum_fusion.x0), channel_id=1, source_target_pairs={{0,2},{1,3},{2,0},{3,1},{4,6},{5,7},{6,4},{7,5},{8,10},{9,11},{10,... | collective-permute-start | bytes 196616 | tf_op jit(solution)/shard_map/ppermute | solution.py:252
  45.1 2.6 %collective-permute-start.8 = (bf16[8,4096]{1,0:T(8,128)(2,1)S(1)}, bf16[8,4096]{1,0:T(8,128)(2,1)S(1)}, u32[]{:S(2)}, u32[]{:S(2)}) collective-permute-start(bf16[8,4096]{1,0:T(8,128)(2,1)S(1)} %pad_maximum_fusion.x0), channel_id=1, source_target_pairs={{0,4},{1,5},{2,6},{3,7},{4,0},{5,1},{6,2},{7,3},{8,12},{9,13},{10,... | collective-permute-start | bytes 196616 | tf_op jit(solution)/shard_map/ppermute | solution.py:252
  47.7 0.0 collective-permute-start.9
  47.7 0.0 collective-permute-done.7.x1
  47.7 3.0 %collective-permute-done.8.x2 = bf16[8,4096]{1,0:T(8,128)(2,1)S(1)} collective-permute-done((bf16[8,4096]{1,0:T(8,128)(2,1)S(1)}, bf16[8,4096]{1,0:T(8,128)(2,1)S(1)}, u32[]{:S(2)}, u32[]{:S(2)}) %collective-permute-start.8) | collective-permute-done | bytes 65568 | tf_op jit(solution)/shard_map/ppermute | solution.py:252
  50.7 1.5 %collective-permute-done.9.x3 = bf16[8,4096]{1,0:T(8,128)(2,1)S(1)} collective-permute-done((bf16[8,4096]{1,0:T(8,128)(2,1)S(1)}, bf16[8,4096]{1,0:T(8,128)(2,1)S(1)}, u32[]{:S(2)}, u32[]{:S(2)}) %collective-permute-start.9) | collective-permute-done | bytes 65568 | tf_op jit(solution)/shard_map/ppermute | solution.py:252
  52.1 0.0 copy-done.1
  52.1 0.0 copy-start
  52.1 4.6 %copy-done = bf16[1,4096,2,768]{3,2,1,0:T(2,128)(2,1)S(1)} copy-done((bf16[1,4096,2,768]{3,2,1,0:T(2,128)(2,1)S(1)}, bf16[1,4096,2,768]{3,2,1,0:T(2,128)(2,1)}, u32[]{:S(2)}) %copy-start) | copy-done | bytes 12582936
  56.7 20.4 %shard_map.147 = bf16[128,4,256]{2,1,0:T(4,128)(2,1)} custom-call(bf16[8,4096]{1,0:T(8,128)(2,1)S(1)} %pad_maximum_fusion.x0, bf16[8,4096]{1,0:T(8,128)(2,1)S(1)} %collective-permute-done.7.x1, bf16[8,4096]{1,0:T(8,128)(2,1)S(1)} %collective-permute-done.8.x2, bf16[8,4096]{1,0:T(8,128)(2,1)S(1)} %collective-permute-done.9.x3, ...), custom_call_target="tpu_custom_call" | custom-call | tf_op jit(solution)/shard_map/pallas_call | solution.py:233
  77.1 5.6 %all-to-all-start.1 = ((bf16[128,4,256]{2,1,0:T(4,128)(2,1)}), bf16[128,4,256]{2,1,0:T(4,128)(2,1)S(1)}, u32[]{:S(2)}, u32[]{:S(2)}) async-start(bf16[128,4,256]{2,1,0:T(4,128)(2,1)} %shard_map.147), calls=%async_computation.1 | async-start | bytes 524288 | tf_op jit(solution)/shard_map/all_to_all | solution.py:302
  82.7 0.0 copy-done.12
  82.7 0.0 copy-done.13
  82.7 0.1 select_reduce_fusion
  82.8 0.1 copy.19
  82.9 11.1 %all-to-all-done.1 = bf16[128,4,256]{2,1,0:T(4,128)(2,1)S(1)} async-done(((bf16[128,4,256]{2,1,0:T(4,128)(2,1)}), bf16[128,4,256]{2,1,0:T(4,128)(2,1)S(1)}, u32[]{:S(2)}, u32[]{:S(2)}) %all-to-all-start.1) | async-done | bytes 262176 | tf_op jit(solution)/shard_map/all_to_all | solution.py:302
  94.1 0.2 multiply_reduce_fusion
  94.3 0.6 add_convert_fusion.1
  (4 shorter events, 0.1 us)
Async XLA Ops:
  0.8 1.6 %copy-start.2 = (bf16[4,1024,2,128]{3,2,1,0:T(2,128)(2,1)S(1)}, bf16[4,1024,2,128]{3,2,1,0:T(2,128)(2,1)}, u32[]{:S(2)}) copy-start(bf16[4,1024,2,128]{3,2,1,0:T(2,128)(2,1)} %key_cache.1) | copy-start | bytes 6291460
  2.4 1.6 %copy-start.3 = (bf16[4,1024,2,128]{3,2,1,0:T(2,128)(2,1)S(1)}, bf16[4,1024,2,128]{3,2,1,0:T(2,128)(2,1)}, u32[]{:S(2)}) copy-start(bf16[4,1024,2,128]{3,2,1,0:T(2,128)(2,1)} %value_cache.1) | copy-start | bytes 6291460
  4.0 0.9 copy-start.5
  4.9 0.9 copy-start.6
  5.8 0.7 copy-start.7
  6.5 0.7 copy-start.8
  7.2 0.7 copy-start.9
  7.8 44.3 %copy-start.1 = (bf16[1,768,4096]{2,1,0:T(8,128)(2,1)S(1)}, bf16[1,768,4096]{2,1,0:T(8,128)(2,1)}, u32[]{:S(2)}) copy-start(bf16[1,768,4096]{2,1,0:T(8,128)(2,1)} %down.1) | copy-start | bytes 18874372
  22.3 1.6 %copy-start.4 = (bf16[2,1,128,4096]{3,2,1,0:T(8,128)(2,1)S(1)}, bf16[2,1,128,4096]{3,2,1,0:T(8,128)(2,1)}, u32[]{:S(2)}) copy-start(bf16[2,1,128,4096]{3,2,1,0:T(8,128)(2,1)} %weight.1) | copy-start | bytes 6291460
  23.8 13.5 %copy-start.10 = (bf16[4,4096]{1,0:T(4,128)(2,1)S(1)}, bf16[4,4096]{1,0:T(4,128)(2,1)}, u32[]{:S(2)}) copy-start(bf16[4,4096]{1,0:T(4,128)(2,1)} %param.24) | copy-start | bytes 98308
  23.8 13.7 %copy-start.11 = (f32[4096]{0:T(1024)S(1)}, f32[4096]{0:T(1024)}, u32[]{:S(2)}) copy-start(f32[4096]{0:T(1024)} %param.25) | copy-start | bytes 49156
  24.4 4.3 %collective-permute-start = (bf16[4,4096]{1,0:T(4,128)(2,1)S(1)}, bf16[4,4096]{1,0:T(4,128)(2,1)S(1)}, u32[]{:S(2)}, u32[]{:S(2)}) collective-permute-start(bf16[4,4096]{1,0:T(4,128)(2,1)S(1)} %shard_map.146), channel_id=1, source_target_pairs={{0,8},{8,0},{16,24},{24,16},{32,40},{40,32},{48,56},{56,48},{64,72... | collective-permute-start | bytes 98312 | tf_op jit(solution)/shard_map/ppermute | solution.py:252
  26.9 2.8 %collective-permute-start.1 = (bf16[4,4096]{1,0:T(4,128)(2,1)S(1)}, bf16[4,4096]{1,0:T(4,128)(2,1)S(1)}, u32[]{:S(2)}, u32[]{:S(2)}) collective-permute-start(bf16[4,4096]{1,0:T(4,128)(2,1)S(1)} %shard_map.146), channel_id=1, source_target_pairs={{0,16},{8,24},{16,0},{24,8},{32,48},{40,56},{48,32},{56,40},{64,80... | collective-permute-start | bytes 98312 | tf_op jit(solution)/shard_map/ppermute | solution.py:252
  26.9 4.3 %collective-permute-start.2 = (bf16[4,4096]{1,0:T(4,128)(2,1)S(1)}, bf16[4,4096]{1,0:T(4,128)(2,1)S(1)}, u32[]{:S(2)}, u32[]{:S(2)}) collective-permute-start(bf16[4,4096]{1,0:T(4,128)(2,1)S(1)} %shard_map.146), channel_id=1, source_target_pairs={{0,24},{8,16},{16,8},{24,0},{32,56},{40,48},{48,40},{56,32},{64,88... | collective-permute-start | bytes 98312 | tf_op jit(solution)/shard_map/ppermute | solution.py:252
  31.2 3.9 %collective-permute-start.3 = (bf16[4,4096]{1,0:T(4,128)(2,1)S(1)}, bf16[4,4096]{1,0:T(4,128)(2,1)S(1)}, u32[]{:S(2)}, u32[]{:S(2)}) collective-permute-start(bf16[4,4096]{1,0:T(4,128)(2,1)S(1)} %add_convert_fusion), channel_id=1, source_target_pairs={{0,32},{8,40},{16,48},{24,56},{32,0},{40,8},{48,16},{56,24},{64,96... | collective-permute-start | bytes 98312 | tf_op jit(solution)/shard_map/ppermute | solution.py:252
  31.6 4.3 %collective-permute-start.4 = (bf16[4,4096]{1,0:T(4,128)(2,1)S(1)}, bf16[4,4096]{1,0:T(4,128)(2,1)S(1)}, u32[]{:S(2)}, u32[]{:S(2)}) collective-permute-start(bf16[4,4096]{1,0:T(4,128)(2,1)S(1)} %add_convert_fusion), channel_id=1, source_target_pairs={{0,64},{8,72},{16,80},{24,88},{32,96},{40,104},{48,112},{56,120},{... | collective-permute-start | bytes 98312 | tf_op jit(solution)/shard_map/ppermute | solution.py:252
  33.4 4.0 %collective-permute-start.5 = (bf16[4,4096]{1,0:T(4,128)(2,1)S(1)}, bf16[4,4096]{1,0:T(4,128)(2,1)S(1)}, u32[]{:S(2)}, u32[]{:S(2)}) collective-permute-start(bf16[4,4096]{1,0:T(4,128)(2,1)S(1)} %add_convert_fusion), channel_id=1, source_target_pairs={{0,96},{8,104},{16,112},{24,120},{32,64},{40,72},{48,80},{56,88},{... | collective-permute-start | bytes 98312 | tf_op jit(solution)/shard_map/ppermute | solution.py:252
  37.6 6.0 %collective-permute-start.6 = (bf16[4,4096]{1,0:T(4,128)(2,1)S(1)}, bf16[4,4096]{1,0:T(4,128)(2,1)S(1)}, u32[]{:S(2)}, u32[]{:S(2)}) collective-permute-start(bf16[4,4096]{1,0:T(4,128)(2,1)S(1)} %multiply_convert_fusion), channel_id=1, source_target_pairs={{0,1},{1,0},{2,3},{3,2},{4,5},{5,4},{6,7},{7,6},{8,9},{9,8},{10,11... | collective-permute-start | bytes 98312 | tf_op jit(solution)/shard_map/ppermute | solution.py:252
  43.6 39.1 %copy-start.12 = (f32[4,8]{1,0:T(4,128)S(1)}, f32[4,8]{1,0:T(4,128)}, u32[]{:S(2)}) copy-start(f32[4,8]{1,0:T(4,128)} %param.27) | copy-start | bytes 388
  43.6 39.1 %copy-start.13 = (s32[4,8]{1,0:T(4,128)S(1)}, s32[4,8]{1,0:T(4,128)}, u32[]{:S(2)}) copy-start(s32[4,8]{1,0:T(4,128)} %param.26) | copy-start | bytes 388
  43.7 4.0 %collective-permute-start.7 = (bf16[8,4096]{1,0:T(8,128)(2,1)S(1)}, bf16[8,4096]{1,0:T(8,128)(2,1)S(1)}, u32[]{:S(2)}, u32[]{:S(2)}) collective-permute-start(bf16[8,4096]{1,0:T(8,128)(2,1)S(1)} %pad_maximum_fusion.x0), channel_id=1, source_target_pairs={{0,2},{1,3},{2,0},{3,1},{4,6},{5,7},{6,4},{7,5},{8,10},{9,11},{10,... | collective-permute-start | bytes 196616 | tf_op jit(solution)/shard_map/ppermute | solution.py:252
  45.1 5.6 %collective-permute-start.8 = (bf16[8,4096]{1,0:T(8,128)(2,1)S(1)}, bf16[8,4096]{1,0:T(8,128)(2,1)S(1)}, u32[]{:S(2)}, u32[]{:S(2)}) collective-permute-start(bf16[8,4096]{1,0:T(8,128)(2,1)S(1)} %pad_maximum_fusion.x0), channel_id=1, source_target_pairs={{0,4},{1,5},{2,6},{3,7},{4,0},{5,1},{6,2},{7,3},{8,12},{9,13},{10,... | collective-permute-start | bytes 196616 | tf_op jit(solution)/shard_map/ppermute | solution.py:252
  47.7 4.5 %collective-permute-start.9 = (bf16[8,4096]{1,0:T(8,128)(2,1)S(1)}, bf16[8,4096]{1,0:T(8,128)(2,1)S(1)}, u32[]{:S(2)}, u32[]{:S(2)}) collective-permute-start(bf16[8,4096]{1,0:T(8,128)(2,1)S(1)} %pad_maximum_fusion.x0), channel_id=1, source_target_pairs={{0,6},{1,7},{2,4},{3,5},{4,2},{5,3},{6,0},{7,1},{8,14},{9,15},{10,... | collective-permute-start | bytes 196616 | tf_op jit(solution)/shard_map/ppermute | solution.py:252
  52.1 4.6 %copy-start = (bf16[1,4096,2,768]{3,2,1,0:T(2,128)(2,1)S(1)}, bf16[1,4096,2,768]{3,2,1,0:T(2,128)(2,1)}, u32[]{:S(2)}) copy-start(bf16[1,4096,2,768]{3,2,1,0:T(2,128)(2,1)} %gate_up.1) | copy-start | bytes 37748740
  77.1 16.9 %all-to-all-start.1 = ((bf16[128,4,256]{2,1,0:T(4,128)(2,1)}), bf16[128,4,256]{2,1,0:T(4,128)(2,1)S(1)}, u32[]{:S(2)}, u32[]{:S(2)}) async-start(bf16[128,4,256]{2,1,0:T(4,128)(2,1)} %shard_map.147), calls=%async_computation.1 | async-start | bytes 524288 | tf_op jit(solution)/shard_map/all_to_all | solution.py:302

commit v2 on v1

v2 whole, which is shorter than its diff:
```python
import functools
import math

import jax
import jax.numpy as jnp
from jax import lax
from jax.experimental import pallas as pl
from jax.experimental.pallas import tpu as pltpu
from jax.sharding import PartitionSpec as P

VMEM_SPEC = pl.BlockSpec(memory_space=pltpu.VMEM)
SMEM_SPEC = pl.BlockSpec(memory_space=pltpu.SMEM)
ANY_SPEC = pl.BlockSpec(memory_space=pl.ANY)
MASKED = -1e30


def in_hbm(value):
    return pltpu.with_memory_space_constraint(value, pltpu.HBM)


def attention_kernel(
    selected_in,
    queries_in,
    new_key_in,
    new_value_in,
    centroid_keys,
    centroid_values,
    key_cache,
    value_cache,
    weight_in,
    out,
    weight_out,
    selected,
    queries,
    new_key,
    new_value,
    keys,
    values,
    small_sem,
    picked_sem,
):
    seq_count, heads_kv, query_count, head_dim = queries.shape
    clusters = centroid_keys.shape[1]
    sel_count = selected.shape[1]
    block_len = key_cache.shape[1] // clusters
    ctx_pos = lax.axis_index("ctx")
    pairs = (
        (selected_in, selected),
        (centroid_keys, keys.at[:, pl.ds(0, clusters)]),
        (queries_in, queries),
        (new_key_in, new_key),
        (new_value_in, new_value),
        (centroid_values, values.at[:, pl.ds(0, clusters)]),
        (weight_in, weight_out),
    )
    small = [
        pltpu.make_async_copy(source, held, small_sem.at[i]) for i, (source, held) in enumerate(pairs)
    ]
    for copy in small:
        copy.start()
    small[0].wait()
    picked = []
    for which, (source, held) in enumerate(((key_cache, keys), (value_cache, values))):
        for s in range(seq_count):
            for g in range(heads_kv):
                for j in range(sel_count):
                    block = selected[g, j, s] - ctx_pos * clusters
                    place = clusters + (g * sel_count + j) * block_len
                    picked.append(
                        pltpu.make_async_copy(
                            source.at[s, pl.ds(block * block_len, block_len)],
                            held.at[s, pl.ds(place, block_len)],
                            picked_sem.at[which, s, g * sel_count + j],
                        )
                    )
    for copy in picked:
        copy.start()
    for copy in small[1:6]:
        copy.wait()
    for copy in picked:
        copy.wait()
    positions = keys.shape[1]
    rows = positions * heads_kv
    flat_keys = keys.reshape(seq_count, rows, head_dim)
    flat_values = values.reshape(seq_count, rows, head_dim)
    shape = (heads_kv * query_count, rows)
    head_of_query = lax.broadcasted_iota(jnp.int32, shape, 0) // query_count
    column = lax.broadcasted_iota(jnp.int32, shape, 1)
    head_of_row = column % heads_kv
    position = column // heads_kv
    head_of_block = (position - clusters) // (sel_count * block_len)
    valid = (head_of_row == head_of_query) & (
        (position < clusters) | (head_of_block == head_of_query)
    )
    score_scale = 1.0 / math.sqrt(head_dim)
    for s in range(seq_count):
        query = queries[s].reshape(heads_kv * query_count, head_dim)
        scores = lax.dot_general(
            query, flat_keys[s], (((1,), (1,)), ((), ())), preferred_element_type=jnp.float32
        )
        scores = jnp.where(valid, scores * score_scale, MASKED)
        own = jnp.sum(
            queries[s].astype(jnp.float32) * new_key[s].astype(jnp.float32)[:, None, :],
            axis=-1,
            keepdims=True,
        ).reshape(heads_kv * query_count, 1)
        own = jnp.where(ctx_pos == 0, own * score_scale, MASKED)
        peak = jnp.maximum(jnp.max(scores, axis=-1, keepdims=True), own)
        probs = jnp.exp(scores - peak)
        own_prob = jnp.exp(own - peak)
        total = jnp.sum(probs, axis=-1, keepdims=True) + own_prob
        weighted = jnp.dot(
            probs.astype(jnp.bfloat16), flat_values[s], preferred_element_type=jnp.float32
        )
        own_value = jnp.broadcast_to(
            new_value[s].astype(jnp.float32)[:, None, :], (heads_kv, query_count, head_dim)
        ).reshape(heads_kv * query_count, head_dim)
        weighted = weighted + own_prob * own_value
        lane = lax.broadcasted_iota(jnp.int32, weighted.shape, 1)
        stats = jnp.where(lane < head_dim // 2, peak, total)
        for g in range(heads_kv):
            part = slice(g * query_count, (g + 1) * query_count)
            out[:, g * seq_count + s, :] = weighted[part]
            out[:, (heads_kv + g) * seq_count + s, :] = stats[part]
    small[6].wait()


def attention(
    queries, key_cache, value_cache, centroid_keys, centroid_values, selected, new_key, new_value, weight
):
    seq_count, heads_kv, query_count, head_dim = queries.shape
    clusters = centroid_keys.shape[1]
    sel_count = selected.shape[2]
    selected = selected.transpose(1, 2, 0)
    block_len = key_cache.shape[1] // clusters
    held = pltpu.VMEM(
        (seq_count, clusters + heads_kv * sel_count * block_len, heads_kv, head_dim), jnp.bfloat16
    )
    operands = (
        selected, queries, new_key, new_value, centroid_keys, centroid_values, key_cache, value_cache, weight
    )
    return pl.pallas_call(
        attention_kernel,
        out_shape=(
            pltpu.VMEM((query_count, 2 * heads_kv * seq_count, head_dim), jnp.float32),
            pltpu.VMEM(weight.shape, weight.dtype),
        ),
        in_specs=[ANY_SPEC] * 9,
        out_specs=(VMEM_SPEC, VMEM_SPEC),
        scratch_shapes=[
            pltpu.SMEM(selected.shape, selected.dtype),
            pltpu.VMEM(queries.shape, queries.dtype),
            pltpu.VMEM(new_key.shape, new_key.dtype),
            pltpu.VMEM(new_value.shape, new_value.dtype),
            held,
            held,
            pltpu.SemaphoreType.DMA((7,)),
            pltpu.SemaphoreType.DMA((2, seq_count, heads_kv * sel_count)),
        ],
        compiler_params=pltpu.CompilerParams(vmem_limit_bytes=12 << 20),
    )(*[in_hbm(operand) for operand in operands])


def project_kernel(parts, weight, before, out):
    rows = parts.shape[1] // 2
    half = parts.shape[2] // 2
    weighted = parts[:, :rows, :]
    peak = parts[:, rows:, 0:1]
    total = parts[:, rows:, half : half + 1]
    scale = jnp.exp(peak - jnp.max(peak, axis=0, keepdims=True))
    total = jnp.sum(total * scale, axis=0)
    attended = (jnp.sum(weighted * scale, axis=0) / total).astype(jnp.bfloat16)
    seq_count = out.shape[0]
    sums = None
    for g in range(weight.shape[0]):
        term = jnp.dot(
            attended[g * seq_count : (g + 1) * seq_count],
            weight[g, 0],
            preferred_element_type=jnp.float32,
        )
        sums = term if sums is None else sums + term
    out[...] = sums.astype(jnp.bfloat16)


def project(parts, weight, before):
    seq_count = parts.shape[1] // (2 * weight.shape[0])
    return pl.pallas_call(
        project_kernel,
        out_shape=jax.ShapeDtypeStruct((seq_count, weight.shape[3]), jnp.bfloat16),
        in_specs=[VMEM_SPEC, VMEM_SPEC, ANY_SPEC],
        out_specs=VMEM_SPEC,
        compiler_params=pltpu.CompilerParams(vmem_limit_bytes=8 << 20),
    )(parts, weight, before)


def fetch_kernel(first, source, *refs):
    out, sem = refs[-2:]
    count = out.shape[0]
    chunks = 4
    part = source.shape[1] // chunks
    copies = [
        pltpu.make_async_copy(
            source.at[0, pl.ds(c * part, part), :, pl.ds((first + t) * 128, 128)],
            out.at[t, pl.ds(c * part, part)],
            sem.at[t, c],
        )
        for c in range(chunks)
        for t in range(count)
    ]
    for copy in copies:
        copy.start()
    for copy in copies:
        copy.wait()


def fetch(weights, first, count, *after):
    depth = weights.shape[1]
    tiles = pl.pallas_call(
        functools.partial(fetch_kernel, first),
        out_shape=pltpu.VMEM((count, depth, 2, 128), weights.dtype),
        in_specs=[ANY_SPEC] * (1 + len(after)),
        out_specs=VMEM_SPEC,
        scratch_shapes=[pltpu.SemaphoreType.DMA((count, 4))],
        compiler_params=pltpu.CompilerParams(vmem_limit_bytes=1 << 20),
        cost_estimate=pl.CostEstimate(
            flops=0, bytes_accessed=count * depth * 512, transcendentals=0
        ),
    )(in_hbm(weights), *after)
    return tiles.reshape(count, 2 * depth, 128)


def experts_kernel(blocks, x0, x1, x2, x3, *refs):
    *tiles, down, out, spread = refs
    block_rows, model_dim = x0.shape
    rows = 4 * block_rows
    seq_count = rows // blocks
    exp_pos = lax.axis_index("exp")
    source = lax.broadcasted_iota(jnp.int32, (128, 512), 0)
    target = lax.broadcasted_iota(jnp.int32, (128, 512), 1)
    ends = (target == 2 * source) | (target == 2 * source + 257)
    to_both = jnp.where(ends, 1.0, 0.0).astype(jnp.bfloat16)
    group = 8

    def spread_group(k, carry):
        pieces = []
        for j in range(group):
            columns = pl.ds(pl.multiple_of((k * group + j) * 128, 128), 128)
            pieces += [x[:, columns] for x in (x0, x1, x2, x3)]
        result = jnp.dot(
            jnp.concatenate(pieces, axis=0), to_both, preferred_element_type=jnp.float32
        ).astype(jnp.bfloat16)
        for j in range(group):
            columns = pl.ds(pl.multiple_of((k * group + j) * 256, 256), 256)
            spread[0:rows, columns] = result[j * rows : (j + 1) * rows, 0:256]
            spread[rows : 2 * rows, columns] = result[j * rows : (j + 1) * rows, 256:512]
        return carry

    lax.fori_loop(0, model_dim // 128 // group, spread_group, 0)
    lanes = [tile.at[t] for tile in tiles for t in range(tile.shape[0])]
    depth = 1024
    both = []
    for u in range(len(lanes) // 2):
        total = jnp.zeros((2 * rows, 256), jnp.float32)
        for c in range(2 * model_dim // depth):
            here = slice(c * depth, (c + 1) * depth)
            right = jnp.concatenate([lanes[2 * u][here, :], lanes[2 * u + 1][here, :]], axis=1)
            total = total + jnp.dot(spread[:, here], right, preferred_element_type=jnp.float32)
        both.append(total)
    both = jnp.concatenate(both, axis=1)
    gate, up = both[:rows], both[rows:]
    activated = (jax.nn.silu(gate) * up).astype(jnp.bfloat16)
    width = 512

    def down_part(b, carry):
        columns = pl.ds(pl.multiple_of(b * width, width), width)
        result = jnp.dot(
            activated, down[0, :, columns], preferred_element_type=jnp.float32
        ).astype(jnp.bfloat16)
        for q in range(width // 256):
            for i in range(blocks):
                place = (b * (width // 256) + q) * blocks + lax.bitwise_xor(exp_pos, i)
                out[place] = result[i * seq_count : (i + 1) * seq_count, q * 256 : (q + 1) * 256]
        return carry

    lax.fori_loop(0, model_dim // width, down_part, 0)


def experts(pieces, tiles, down, blocks):
    block_rows, model_dim = pieces[0].shape
    rows = 4 * block_rows
    return pl.pallas_call(
        functools.partial(experts_kernel, blocks),
        out_shape=pltpu.VMEM((model_dim // 256 * blocks, rows // blocks, 256), jnp.bfloat16),
        in_specs=[VMEM_SPEC] * (5 + len(tiles)),
        out_specs=VMEM_SPEC,
        scratch_shapes=[pltpu.VMEM((2 * rows, 2 * model_dim), jnp.bfloat16)],
        compiler_params=pltpu.CompilerParams(vmem_limit_bytes=16 << 20),
    )(*pieces, *tiles, down)


def sum_kernel(p0, p1, p2, p3, before, out):
    total = p0[...].astype(jnp.float32)
    for piece in (p1, p2, p3):
        total = total + piece[...].astype(jnp.float32)
    out[...] = total.astype(out.dtype)


def sum_pieces(pieces, before):
    return pl.pallas_call(
        sum_kernel,
        out_shape=pltpu.VMEM(pieces[0].shape, pieces[0].dtype),
        in_specs=[VMEM_SPEC] * 4 + [ANY_SPEC],
        out_specs=VMEM_SPEC,
        compiler_params=pltpu.CompilerParams(vmem_limit_bytes=2 << 20),
    )(*pieces, before)


def norm_kernel(p0, p1, p2, p3, residual, gain, before, hidden, normed):
    total = residual[...].astype(jnp.float32)
    for piece in (p0, p1, p2, p3):
        total = total + piece[...].astype(jnp.float32)
    mean_square = jnp.mean(total * total, axis=-1, keepdims=True)
    hidden[...] = total
    normed[...] = (total * lax.rsqrt(mean_square + 1e-06) * gain[...]).astype(normed.dtype)


def norm(pieces, residual, gain, before):
    shape = residual.shape
    return pl.pallas_call(
        norm_kernel,
        out_shape=(pltpu.VMEM(shape, jnp.float32), pltpu.VMEM(shape, jnp.bfloat16)),
        in_specs=[VMEM_SPEC] * 6 + [ANY_SPEC],
        out_specs=(VMEM_SPEC, VMEM_SPEC),
        compiler_params=pltpu.CompilerParams(vmem_limit_bytes=2 << 20),
    )(*pieces, residual, gain.reshape(1, -1), before)


def swapped(value, axes, count, mask):
    return lax.ppermute(value, axes, [(i, i ^ mask) for i in range(count)])


def body(
    queries,
    key_cache,
    value_cache,
    centroid_keys,
    centroid_values,
    selected,
    new_key,
    new_value,
    out_weight,
    residual,
    norm_gain,
    expert_ids,
    gate_weights,
    w_gate_up,
    w_down,
):
    ctx_devices = lax.axis_size("ctx")
    kvh_devices = lax.axis_size("kvh")
    exp_devices = lax.axis_size("exp")
    seq_count, model_dim = residual.shape
    plane = ctx_devices * kvh_devices

    parts, out_weight = attention(
        queries,
        key_cache,
        value_cache,
        centroid_keys,
        centroid_values,
        selected,
        new_key,
        new_value,
        out_weight,
    )
    parts = lax.all_to_all(parts, "ctx", split_axis=0, concat_axis=0, tiled=True)

    device = jnp.arange(plane * exp_devices, dtype=jnp.int32)
    expert = device // (kvh_devices * exp_devices) * exp_devices + device % exp_devices
    matches = expert_ids.T[:, None, :] == expert[None, :, None]
    weight = jnp.sum(jnp.where(matches, gate_weights.T[:, None, :], 0.0), axis=0)
    projected = project(parts, out_weight, weight)

    axes = ("ctx", "kvh")
    along_x = [projected] + [swapped(projected, axes, plane, m) for m in (1, 2, 3)]
    tiles = [fetch(w_gate_up, 0, 2, projected)]
    sums = sum_pieces(along_x, tiles[0])
    along_z = [sums] + [swapped(sums, axes, plane, m) for m in range(4, plane, 4)]
    tiles.append(fetch(w_gate_up, 2, 2, sums))
    hidden1, normed = norm(along_z, residual, norm_gain, tiles[1])

    other = swapped(normed, "exp", exp_devices, 1)
    pair = jnp.concatenate([normed, other], axis=0)
    tiles.append(fetch(w_gate_up, 4, 2, pair))
    pieces = [pair] + [swapped(pair, "exp", exp_devices, m) for m in range(2, exp_devices, 2)]
    results = experts(pieces, tiles, w_down, exp_devices)
    returned = lax.all_to_all(
        results, ("ctx", "kvh", "exp"), split_axis=0, concat_axis=0, tiled=True
    )

    expert_mix = jnp.sum(returned.astype(jnp.float32) * weight[:, :, None], axis=0)
    slice_width = expert_mix.shape[1]
    own_slice = lax.dynamic_slice_in_dim(
        hidden1, lax.axis_index(("ctx", "kvh")) * slice_width, slice_width, 1
    )
    return (own_slice + expert_mix).astype(jnp.bfloat16)


def solution(mesh):
    in_specs = (
        P("exp", "kvh", None, None),
        P("exp", "ctx", "kvh", None),
        P("exp", "ctx", "kvh", None),
        P("exp", "ctx", "kvh", None),
        P("exp", "ctx", "kvh", None),
        P("exp", "kvh", "ctx"),
        P("exp", "kvh", None),
        P("exp", "kvh", None),
        P("kvh", "ctx", None, None),
        P("exp", None),
        P(),
        P("exp", None),
        P("exp", None),
        P(("ctx", "exp"), None, None, "kvh"),
        P(("ctx", "exp"), "kvh", None),
    )
    out_specs = P("exp", ("ctx", "kvh"))
    return jax.shard_map(body, mesh=mesh, in_specs=in_specs, out_specs=out_specs, check_vma=False)
```

time: 95.3 us -> 68.2 us (0.72)
  local copies, waits for them, and re-layouts: 14.1 us -> 0.15 us
  blocking collectives: 11.8 us -> 0 us
  starting transfers between devices: 22 us -> 28.7 us
  Pallas kernels: 23.5 us -> 17.3 us
  waiting for transfers between devices: 22.1 us -> 20.6 us
    unnamed x29 -> x12, local copies, waits for them, and re-layouts: 14 us -> 0.04 us
    all_to_all x1 -> x0, blocking collectives: 11.8 us -> none  [body(): lax.all_to_all(parts, 'ctx', split_axis=0, concat_axis=0, tiled=True)]
    all_to_all x0 -> x1, starting transfers between devices: none -> 6.8 us  [body(): lax.all_to_all(parts, 'ctx', split_axis=0, concat_axis=0, tiled=True)]
    ppermute x10, waiting for transfers between devices: 11 us -> 4.32 us  [swapped(): return lax.ppermute(value, axes, [(i, i ^ mask) for i in range(count)])]
    pallas_call x2 -> x7, Pallas kernels: 23 us -> 16.8 us  [the longest x3 6.64 us: fetch(): pl.pallas_call(functools.partial(fetch_kernel, first), out_shape=pltpu.VM...]
    all_to_all x0 -> x1, waiting for transfers between devices: none -> 4.96 us  [body(): lax.all_to_all(parts, 'ctx', split_axis=0, concat_axis=0, tiled=True)]
  transfers between devices with their start and end apart: 11 -> 12, of which waited for: 9 -> 6; matrix products, arithmetic and copies ran while one was open for 0% -> 0% of each run, Pallas kernels for 0% -> 10%
where the time goes in v2:
time: 68.2 us; the launch traced here: 67.9 us
  starting transfers between devices  28.7 us (42%)
  waiting for transfers between devices  20.6 us (30%)
  Pallas kernels  17.3 us (25%)
  other arithmetic  0.93 us (1%)
    ppermute x10, starting transfers between devices, swapped(): return lax.ppermute(value, axes, [(i, i ^ mask) for i in range(count)])  16.3 us
    all_to_all x1, waiting for transfers between devices, body(): lax.all_to_all(results, ('ctx', 'kvh', 'exp'), split_axis=0, concat_axis=...  11.4 us
    all_to_all x1, starting transfers between devices, body(): lax.all_to_all(parts, 'ctx', split_axis=0, concat_axis=0, tiled=True)  6.8 us
    pallas_call x3, Pallas kernels, fetch(): pl.pallas_call(functools.partial(fetch_kernel, first), out_shape=pltpu.VM...  6.64 us
    pallas_call x1, Pallas kernels, experts(): pl.pallas_call(functools.partial(experts_kernel, blocks), out_shape=pltpu...  6.03 us
    all_to_all x1, starting transfers between devices, body(): lax.all_to_all(results, ('ctx', 'kvh', 'exp'), split_axis=0, concat_axis=...  5.57 us
    all_to_all x1, waiting for transfers between devices, body(): lax.all_to_all(parts, 'ctx', split_axis=0, concat_axis=0, tiled=True)  4.96 us
    ppermute x10, waiting for transfers between devices, swapped(): return lax.ppermute(value, axes, [(i, i ^ mask) for i in range(count)])  4.32 us
  transfers between devices with their start and end apart: 12, of which 6 were waited for; matrix products, arithmetic and copies ran while one was open for 0% of the time, Pallas kernels for 10%

profile of v2, /device:TPU:1, one launch (start us, length us, event | category | flops | bytes accessed | tf_op | source)
XLA Modules:
  0.0 67.9 jit_solution(2216635303598992044)
XLA Ops:
  0.0 0.0 copy-start.3
  0.0 0.0 copy-start.2
  0.0 3.9 %shard_map.145 = (f32[8,16,128]{2,1,0:T(8,128)}, bf16[2,1,128,4096]{3,2,1,0:T(8,128)(2,1)S(1)}) custom-call(s32[2,2,4]{2,1,0:T(2,128)} %bitcast.15, bf16[4,2,8,128]{3,2,1,0:T(8,128)(2,1)} %queries_in.1, bf16[4,2,128]{2,1,0:T(2,128)(2,1)} %new_key_in.1, bf16[4,2,128]{2,1,0:T(2,128)(2,1)} %new_value_in.1, bf16[4,64,2,128]{3,2,1,0:T(2,128)(2,1)} %centroid_keys.1, ...), custom_call_target="tpu_custom_call" | custom-call | tf_op jit(solution)/shard_map/pallas_call | solution.py:142
  4.0 6.8 %all-to-all-start = ((f32[8,16,128]{2,1,0:T(8,128)}), f32[8,16,128]{2,1,0:T(8,128)S(1)}, u32[]{:S(2)}, u32[]{:S(2)}) async-start(f32[8,16,128]{2,1,0:T(8,128)} %get-tuple-element.9), calls=%async_computation | async-start | bytes 131072 | tf_op jit(solution)/shard_map/all_to_all | solution.py:376
  10.8 0.0 copy-done.3
  10.8 0.0 copy-done.2
  10.8 0.1 select_reduce_fusion
  10.9 0.1 copy.18.before
  11.0 5.0 %all-to-all-done.parts = f32[8,16,128]{2,1,0:T(8,128)S(1)} async-done(((f32[8,16,128]{2,1,0:T(8,128)}), f32[8,16,128]{2,1,0:T(8,128)S(1)}, u32[]{:S(2)}, u32[]{:S(2)}) %all-to-all-start) | async-done | bytes 65568 | tf_op jit(solution)/shard_map/all_to_all | solution.py:376
  16.0 0.5 shard_map.146.refs_0_.p0
  16.5 2.5 %collective-permute-start = (bf16[4,4096]{1,0:T(4,128)(2,1)S(1)}, bf16[4,4096]{1,0:T(4,128)(2,1)S(1)}, u32[]{:S(2)}, u32[]{:S(2)}) collective-permute-start(bf16[4,4096]{1,0:T(4,128)(2,1)S(1)} %shard_map.146.refs_0_.p0), channel_id=1, source_target_pairs={{0,8},{8,0},{16,24},{24,16},{32,40},{40,32},{48,56},{56,48},{64,72... | collective-permute-start | bytes 98312 | tf_op jit(solution)/shard_map/ppermute | solution.py:339
  19.0 0.0 collective-permute-start.1
  19.0 0.8 %collective-permute-start.2 = (bf16[4,4096]{1,0:T(4,128)(2,1)S(1)}, bf16[4,4096]{1,0:T(4,128)(2,1)S(1)}, u32[]{:S(2)}, u32[]{:S(2)}) collective-permute-start(bf16[4,4096]{1,0:T(4,128)(2,1)S(1)} %shard_map.146.refs_0_.p0), channel_id=1, source_target_pairs={{0,24},{8,16},{16,8},{24,0},{32,56},{40,48},{48,40},{56,32},{64,88... | collective-permute-start | bytes 98312 | tf_op jit(solution)/shard_map/ppermute | solution.py:339
  19.8 2.2 %shard_map.147 = bf16[2,4096,2,128]{3,2,1,0:T(2,128)(2,1)S(1)} custom-call(bf16[1,4096,2,768]{3,2,1,0:T(2,128)(2,1)} %source.5, bf16[4,4096]{1,0:T(4,128)(2,1)S(1)} %shard_map.146.refs_0_.p0), custom_call_target="tpu_custom_call" | custom-call | bytes 4194304 | tf_op jit(solution)/shard_map/pallas_call | solution.py:218
  22.0 0.0 collective-permute-done.p1
  22.0 0.0 collective-permute-done.1.p2
  22.0 1.2 %collective-permute-done.2.p3 = bf16[4,4096]{1,0:T(4,128)(2,1)S(1)} collective-permute-done((bf16[4,4096]{1,0:T(4,128)(2,1)S(1)}, bf16[4,4096]{1,0:T(4,128)(2,1)S(1)}, u32[]{:S(2)}, u32[]{:S(2)}) %collective-permute-start.2) | collective-permute-done | bytes 32800 | tf_op jit(solution)/shard_map/ppermute | solution.py:339
  23.3 0.0 copy-start
  23.3 0.0 copy-start.1
  23.3 0.4 collective-permute-start.3
  23.7 1.8 %collective-permute-start.4 = (bf16[4,4096]{1,0:T(4,128)(2,1)S(1)}, bf16[4,4096]{1,0:T(4,128)(2,1)S(1)}, u32[]{:S(2)}, u32[]{:S(2)}) collective-permute-start(bf16[4,4096]{1,0:T(4,128)(2,1)S(1)} %shard_map.148.refs_0_.p0), channel_id=1, source_target_pairs={{0,64},{8,72},{16,80},{24,88},{32,96},{40,104},{48,112},{56,120},{... | collective-permute-start | bytes 98312 | tf_op jit(solution)/shard_map/ppermute | solution.py:339
  25.5 1.8 %collective-permute-start.5 = (bf16[4,4096]{1,0:T(4,128)(2,1)S(1)}, bf16[4,4096]{1,0:T(4,128)(2,1)S(1)}, u32[]{:S(2)}, u32[]{:S(2)}) collective-permute-start(bf16[4,4096]{1,0:T(4,128)(2,1)S(1)} %shard_map.148.refs_0_.p0), channel_id=1, source_target_pairs={{0,96},{8,104},{16,112},{24,120},{32,64},{40,72},{48,80},{56,88},{... | collective-permute-start | bytes 98312 | tf_op jit(solution)/shard_map/ppermute | solution.py:339
  27.3 2.2 %shard_map.149 = bf16[2,4096,2,128]{3,2,1,0:T(2,128)(2,1)S(1)} custom-call(bf16[1,4096,2,768]{3,2,1,0:T(2,128)(2,1)} %source.5, bf16[4,4096]{1,0:T(4,128)(2,1)S(1)} %shard_map.148.refs_0_.p0), custom_call_target="tpu_custom_call" | custom-call | bytes 4194304 | tf_op jit(solution)/shard_map/pallas_call | solution.py:218
  29.5 0.0 collective-permute-done.3.p1
  29.5 0.0 collective-permute-done.4.p2
  29.5 0.0 collective-permute-done.5.p3
  29.5 0.0 copy-done
  29.5 0.0 copy-done.1
  29.5 0.0 slice-start
  29.6 0.2 shard_map.150
  29.7 5.1 %collective-permute-start.6 = (bf16[4,4096]{1,0:T(4,128)(2,1)S(1)}, bf16[4,4096]{1,0:T(4,128)(2,1)S(1)}, u32[]{:S(2)}, u32[]{:S(2)}) collective-permute-start(bf16[4,4096]{1,0:T(4,128)(2,1)S(1)} %get-tuple-element.12), channel_id=1, source_target_pairs={{0,1},{1,0},{2,3},{3,2},{4,5},{5,4},{6,7},{7,6},{8,9},{9,8},{10,11... | collective-permute-start | bytes 98312 | tf_op jit(solution)/shard_map/ppermute | solution.py:339
  34.8 0.9 %collective-permute-done.6 = bf16[4,4096]{1,0:T(4,128)(2,1)S(1)} collective-permute-done((bf16[4,4096]{1,0:T(4,128)(2,1)S(1)}, bf16[4,4096]{1,0:T(4,128)(2,1)S(1)}, u32[]{:S(2)}, u32[]{:S(2)}) %collective-permute-start.6) | collective-permute-done | bytes 32800 | tf_op jit(solution)/shard_map/ppermute | solution.py:339
  35.7 0.0 slice-start.1
  35.7 1.4 %collective-permute-start.7 = (bf16[8,4096]{1,0:T(8,128)(2,1)S(1)}, bf16[8,4096]{1,0:T(8,128)(2,1)S(1)}, u32[]{:S(2)}, u32[]{:S(2)}) collective-permute-start(bf16[8,4096]{1,0:T(8,128)(2,1)S(1)} %pad_maximum_fusion.refs_0_.x0), channel_id=1, source_target_pairs={{0,2},{1,3},{2,0},{3,1},{4,6},{5,7},{6,4},{7,5},{8,10},{9,11},{10,... | collective-permute-start | bytes 196616 | tf_op jit(solution)/shard_map/ppermute | solution.py:339
  37.1 2.6 %collective-permute-start.8 = (bf16[8,4096]{1,0:T(8,128)(2,1)S(1)}, bf16[8,4096]{1,0:T(8,128)(2,1)S(1)}, u32[]{:S(2)}, u32[]{:S(2)}) collective-permute-start(bf16[8,4096]{1,0:T(8,128)(2,1)S(1)} %pad_maximum_fusion.refs_0_.x0), channel_id=1, source_target_pairs={{0,4},{1,5},{2,6},{3,7},{4,0},{5,1},{6,2},{7,3},{8,12},{9,13},{10,... | collective-permute-start | bytes 196616 | tf_op jit(solution)/shard_map/ppermute | solution.py:339
  39.7 0.0 collective-permute-start.9
  39.7 2.2 %shard_map.151 = bf16[2,4096,2,128]{3,2,1,0:T(2,128)(2,1)S(1)} custom-call(bf16[1,4096,2,768]{3,2,1,0:T(2,128)(2,1)} %source.5, bf16[8,4096]{1,0:T(8,128)(2,1)S(1)} %pad_maximum_fusion.refs_0_.x0), custom_call_target="tpu_custom_call" | custom-call | bytes 4194304 | tf_op jit(solution)/shard_map/pallas_call | solution.py:218
  41.9 0.0 collective-permute-done.7.x1
  41.9 0.7 %collective-permute-done.8.x2 = bf16[8,4096]{1,0:T(8,128)(2,1)S(1)} collective-permute-done((bf16[8,4096]{1,0:T(8,128)(2,1)S(1)}, bf16[8,4096]{1,0:T(8,128)(2,1)S(1)}, u32[]{:S(2)}, u32[]{:S(2)}) %collective-permute-start.8) | collective-permute-done | bytes 65568 | tf_op jit(solution)/shard_map/ppermute | solution.py:339
  42.7 1.5 %collective-permute-done.9.x3 = bf16[8,4096]{1,0:T(8,128)(2,1)S(1)} collective-permute-done((bf16[8,4096]{1,0:T(8,128)(2,1)S(1)}, bf16[8,4096]{1,0:T(8,128)(2,1)S(1)}, u32[]{:S(2)}, u32[]{:S(2)}) %collective-permute-start.9) | collective-permute-done | bytes 65568 | tf_op jit(solution)/shard_map/ppermute | solution.py:339
  44.2 0.0 slice-done
  44.2 0.0 slice-done.1
  44.2 6.0 %shard_map.152 = bf16[128,4,256]{2,1,0:T(4,128)(2,1)} custom-call(bf16[8,4096]{1,0:T(8,128)(2,1)S(1)} %pad_maximum_fusion.refs_0_.x0, bf16[8,4096]{1,0:T(8,128)(2,1)S(1)} %collective-permute-done.7.x1, bf16[8,4096]{1,0:T(8,128)(2,1)S(1)} %collective-permute-done.8.x2, bf16[8,4096]{1,0:T(8,128)(2,1)S(1)} %collective-permute-done.9.x3, ...), custom_call_target="tpu_custom_call" | custom-call | tf_op jit(solution)/shard_map/pallas_call | solution.py:291
  50.2 5.6 %all-to-all-start.1 = ((bf16[128,4,256]{2,1,0:T(4,128)(2,1)}), bf16[128,4,256]{2,1,0:T(4,128)(2,1)S(1)}, u32[]{:S(2)}, u32[]{:S(2)}) async-start(bf16[128,4,256]{2,1,0:T(4,128)(2,1)} %shard_map.152), calls=%async_computation.1 | async-start | bytes 524288 | tf_op jit(solution)/shard_map/all_to_all | solution.py:397
  55.8 11.4 %all-to-all-done.1 = bf16[128,4,256]{2,1,0:T(4,128)(2,1)S(1)} async-done(((bf16[128,4,256]{2,1,0:T(4,128)(2,1)}), bf16[128,4,256]{2,1,0:T(4,128)(2,1)S(1)}, u32[]{:S(2)}, u32[]{:S(2)}) %all-to-all-start.1) | async-done | bytes 262176 | tf_op jit(solution)/shard_map/all_to_all | solution.py:397
  67.1 0.2 multiply_reduce_fusion
  67.3 0.6 add_convert_fusion
  (4 shorter events, 0.1 us)
Async XLA Ops:
  0.0 10.8 %copy-start.3 = (s32[4,8]{1,0:T(4,128)S(1)}, s32[4,8]{1,0:T(4,128)}, u32[]{:S(2)}) copy-start(s32[4,8]{1,0:T(4,128)} %param.26) | copy-start | bytes 388
  0.0 10.8 %copy-start.2 = (f32[4,8]{1,0:T(4,128)S(1)}, f32[4,8]{1,0:T(4,128)}, u32[]{:S(2)}) copy-start(f32[4,8]{1,0:T(4,128)} %param.27) | copy-start | bytes 388
  4.0 12.0 %all-to-all-start = ((f32[8,16,128]{2,1,0:T(8,128)}), f32[8,16,128]{2,1,0:T(8,128)S(1)}, u32[]{:S(2)}, u32[]{:S(2)}) async-start(f32[8,16,128]{2,1,0:T(8,128)} %get-tuple-element.9), calls=%async_computation | async-start | bytes 131072 | tf_op jit(solution)/shard_map/all_to_all | solution.py:376
  16.5 5.6 %collective-permute-start = (bf16[4,4096]{1,0:T(4,128)(2,1)S(1)}, bf16[4,4096]{1,0:T(4,128)(2,1)S(1)}, u32[]{:S(2)}, u32[]{:S(2)}) collective-permute-start(bf16[4,4096]{1,0:T(4,128)(2,1)S(1)} %shard_map.146.refs_0_.p0), channel_id=1, source_target_pairs={{0,8},{8,0},{16,24},{24,16},{32,40},{40,32},{48,56},{56,48},{64,72... | collective-permute-start | bytes 98312 | tf_op jit(solution)/shard_map/ppermute | solution.py:339
  19.0 3.0 %collective-permute-start.1 = (bf16[4,4096]{1,0:T(4,128)(2,1)S(1)}, bf16[4,4096]{1,0:T(4,128)(2,1)S(1)}, u32[]{:S(2)}, u32[]{:S(2)}) collective-permute-start(bf16[4,4096]{1,0:T(4,128)(2,1)S(1)} %shard_map.146.refs_0_.p0), channel_id=1, source_target_pairs={{0,16},{8,24},{16,0},{24,8},{32,48},{40,56},{48,32},{56,40},{64,80... | collective-permute-start | bytes 98312 | tf_op jit(solution)/shard_map/ppermute | solution.py:339
  19.0 4.3 %collective-permute-start.2 = (bf16[4,4096]{1,0:T(4,128)(2,1)S(1)}, bf16[4,4096]{1,0:T(4,128)(2,1)S(1)}, u32[]{:S(2)}, u32[]{:S(2)}) collective-permute-start(bf16[4,4096]{1,0:T(4,128)(2,1)S(1)} %shard_map.146.refs_0_.p0), channel_id=1, source_target_pairs={{0,24},{8,16},{16,8},{24,0},{32,56},{40,48},{48,40},{56,32},{64,88... | collective-permute-start | bytes 98312 | tf_op jit(solution)/shard_map/ppermute | solution.py:339
  23.3 6.2 %copy-start = (bf16[4,4096]{1,0:T(4,128)(2,1)S(1)}, bf16[4,4096]{1,0:T(4,128)(2,1)}, u32[]{:S(2)}) copy-start(bf16[4,4096]{1,0:T(4,128)(2,1)} %residual.1) | copy-start | bytes 98308
  23.3 6.2 %copy-start.1 = (f32[4096]{0:T(1024)S(1)}, f32[4096]{0:T(1024)}, u32[]{:S(2)}) copy-start(f32[4096]{0:T(1024)} %param.25) | copy-start | bytes 49156
  23.3 6.2 %collective-permute-start.3 = (bf16[4,4096]{1,0:T(4,128)(2,1)S(1)}, bf16[4,4096]{1,0:T(4,128)(2,1)S(1)}, u32[]{:S(2)}, u32[]{:S(2)}) collective-permute-start(bf16[4,4096]{1,0:T(4,128)(2,1)S(1)} %shard_map.148.refs_0_.p0), channel_id=1, source_target_pairs={{0,32},{8,40},{16,48},{24,56},{32,0},{40,8},{48,16},{56,24},{64,96... | collective-permute-start | bytes 98312 | tf_op jit(solution)/shard_map/ppermute | solution.py:339
  23.7 5.8 %collective-permute-start.4 = (bf16[4,4096]{1,0:T(4,128)(2,1)S(1)}, bf16[4,4096]{1,0:T(4,128)(2,1)S(1)}, u32[]{:S(2)}, u32[]{:S(2)}) collective-permute-start(bf16[4,4096]{1,0:T(4,128)(2,1)S(1)} %shard_map.148.refs_0_.p0), channel_id=1, source_target_pairs={{0,64},{8,72},{16,80},{24,88},{32,96},{40,104},{48,112},{56,120},{... | collective-permute-start | bytes 98312 | tf_op jit(solution)/shard_map/ppermute | solution.py:339
  25.5 4.0 %collective-permute-start.5 = (bf16[4,4096]{1,0:T(4,128)(2,1)S(1)}, bf16[4,4096]{1,0:T(4,128)(2,1)S(1)}, u32[]{:S(2)}, u32[]{:S(2)}) collective-permute-start(bf16[4,4096]{1,0:T(4,128)(2,1)S(1)} %shard_map.148.refs_0_.p0), channel_id=1, source_target_pairs={{0,96},{8,104},{16,112},{24,120},{32,64},{40,72},{48,80},{56,88},{... | collective-permute-start | bytes 98312 | tf_op jit(solution)/shard_map/ppermute | solution.py:339
  29.5 14.6 %slice-start = ((s8[6291456]{0:T(1024)(128)(4,1)}), s8[4194304]{0:T(1024)(128)(4,1)S(1)}, s32[]{:S(2)}) async-start(s8[6291456]{0:T(1024)(128)(4,1)} %bitcast.12), calls=%async_computation.2 | async-start | bytes 8388608
  29.7 5.9 %collective-permute-start.6 = (bf16[4,4096]{1,0:T(4,128)(2,1)S(1)}, bf16[4,4096]{1,0:T(4,128)(2,1)S(1)}, u32[]{:S(2)}, u32[]{:S(2)}) collective-permute-start(bf16[4,4096]{1,0:T(4,128)(2,1)S(1)} %get-tuple-element.12), channel_id=1, source_target_pairs={{0,1},{1,0},{2,3},{3,2},{4,5},{5,4},{6,7},{7,6},{8,9},{9,8},{10,11... | collective-permute-start | bytes 98312 | tf_op jit(solution)/shard_map/ppermute | solution.py:339
  35.7 8.5 %slice-start.1 = ((s8[6291456]{0:T(1024)(128)(4,1)}), s8[2097152]{0:T(1024)(128)(4,1)S(1)}, s32[]{:S(2)}) async-start(s8[6291456]{0:T(1024)(128)(4,1)} %bitcast.12), calls=%async_computation.3 | async-start | bytes 4194304
  35.7 6.2 %collective-permute-start.7 = (bf16[8,4096]{1,0:T(8,128)(2,1)S(1)}, bf16[8,4096]{1,0:T(8,128)(2,1)S(1)}, u32[]{:S(2)}, u32[]{:S(2)}) collective-permute-start(bf16[8,4096]{1,0:T(8,128)(2,1)S(1)} %pad_maximum_fusion.refs_0_.x0), channel_id=1, source_target_pairs={{0,2},{1,3},{2,0},{3,1},{4,6},{5,7},{6,4},{7,5},{8,10},{9,11},{10,... | collective-permute-start | bytes 196616 | tf_op jit(solution)/shard_map/ppermute | solution.py:339
  37.1 5.6 %collective-permute-start.8 = (bf16[8,4096]{1,0:T(8,128)(2,1)S(1)}, bf16[8,4096]{1,0:T(8,128)(2,1)S(1)}, u32[]{:S(2)}, u32[]{:S(2)}) collective-permute-start(bf16[8,4096]{1,0:T(8,128)(2,1)S(1)} %pad_maximum_fusion.refs_0_.x0), channel_id=1, source_target_pairs={{0,4},{1,5},{2,6},{3,7},{4,0},{5,1},{6,2},{7,3},{8,12},{9,13},{10,... | collective-permute-start | bytes 196616 | tf_op jit(solution)/shard_map/ppermute | solution.py:339
  39.7 4.5 %collective-permute-start.9 = (bf16[8,4096]{1,0:T(8,128)(2,1)S(1)}, bf16[8,4096]{1,0:T(8,128)(2,1)S(1)}, u32[]{:S(2)}, u32[]{:S(2)}) collective-permute-start(bf16[8,4096]{1,0:T(8,128)(2,1)S(1)} %pad_maximum_fusion.refs_0_.x0), channel_id=1, source_target_pairs={{0,6},{1,7},{2,4},{3,5},{4,2},{5,3},{6,0},{7,1},{8,14},{9,15},{10,... | collective-permute-start | bytes 196616 | tf_op jit(solution)/shard_map/ppermute | solution.py:339
  50.2 16.9 %all-to-all-start.1 = ((bf16[128,4,256]{2,1,0:T(4,128)(2,1)}), bf16[128,4,256]{2,1,0:T(4,128)(2,1)S(1)}, u32[]{:S(2)}, u32[]{:S(2)}) async-start(bf16[128,4,256]{2,1,0:T(4,128)(2,1)} %shard_map.152), calls=%async_computation.1 | async-start | bytes 524288 | tf_op jit(solution)/shard_map/all_to_all | solution.py:397

commit v3 on v2

v3 whole, which is shorter than its diff:
```python
import functools
import math

import jax
import jax.numpy as jnp
from jax import lax
from jax.experimental import pallas as pl
from jax.experimental.pallas import tpu as pltpu
from jax.sharding import PartitionSpec as P

VMEM_SPEC = pl.BlockSpec(memory_space=pltpu.VMEM)
SMEM_SPEC = pl.BlockSpec(memory_space=pltpu.SMEM)
ANY_SPEC = pl.BlockSpec(memory_space=pl.ANY)
MASKED = -1e30


def in_hbm(value):
    return pltpu.with_memory_space_constraint(value, pltpu.HBM)


def attention_kernel(
    selected_in,
    queries_in,
    new_key_in,
    new_value_in,
    centroid_keys,
    centroid_values,
    key_cache,
    value_cache,
    weight_in,
    out,
    weight_out,
    selected,
    queries,
    new_key,
    new_value,
    keys,
    values,
    small_sem,
    picked_sem,
):
    seq_count, heads_kv, query_count, head_dim = queries.shape
    centroid_rows = centroid_keys.shape[1]
    clusters = centroid_rows // heads_kv
    sel_count = selected.shape[1]
    block_rows = key_cache.shape[1] // clusters
    ctx_pos = lax.axis_index("ctx")
    pairs = (
        (selected_in, selected),
        (centroid_keys, keys.at[:, pl.ds(0, centroid_rows)]),
        (queries_in, queries),
        (new_key_in, new_key),
        (new_value_in, new_value),
        (centroid_values, values.at[:, pl.ds(0, centroid_rows)]),
        (weight_in, weight_out),
    )
    small = [
        pltpu.make_async_copy(source, held, small_sem.at[i]) for i, (source, held) in enumerate(pairs)
    ]
    for copy in small[:6]:
        copy.start()
    small[0].wait()
    picked = ([], [])
    for which, (source, held) in enumerate(((key_cache, keys), (value_cache, values))):
        for s in range(seq_count):
            for g in range(heads_kv):
                for j in range(sel_count):
                    block = selected[g, j, s] - ctx_pos * clusters
                    start = pl.multiple_of(block * block_rows, block_rows)
                    place = centroid_rows + (g * sel_count + j) * block_rows
                    copy = pltpu.make_async_copy(
                        source.at[s, pl.ds(start, block_rows)],
                        held.at[s, pl.ds(place, block_rows)],
                        picked_sem.at[which, s, g * sel_count + j],
                    )
                    copy.start()
                    picked[which].append(copy)
    small[6].start()
    for copy in small[1:4] + picked[0]:
        copy.wait()
    rows = keys.shape[1]
    heads = heads_kv * query_count
    shape = (seq_count * heads, rows)
    head_of_query = lax.broadcasted_iota(jnp.int32, shape, 0) // query_count % heads_kv
    column = lax.broadcasted_iota(jnp.int32, shape, 1)
    head_of_block = (column - centroid_rows) // (sel_count * block_rows)
    valid = (column % heads_kv == head_of_query) & (
        (column < centroid_rows) | (head_of_block == head_of_query)
    )
    score_scale = 1.0 / math.sqrt(head_dim)
    scores, own = [], []
    for s in range(seq_count):
        scores.append(
            lax.dot_general(
                queries[s].reshape(heads, head_dim),
                keys[s],
                (((1,), (1,)), ((), ())),
                preferred_element_type=jnp.float32,
            )
        )
        products = queries[s].astype(jnp.float32) * new_key[s].astype(jnp.float32)[:, None, :]
        own.append(jnp.sum(products, axis=-1, keepdims=True).reshape(heads, 1))
    scores = jnp.where(valid, jnp.concatenate(scores, axis=0) * score_scale, MASKED)
    own = jnp.where(ctx_pos == 0, jnp.concatenate(own, axis=0) * score_scale, MASKED)
    peak = jnp.maximum(jnp.max(scores, axis=-1, keepdims=True), own)
    probs = jnp.exp(scores - peak)
    own_prob = jnp.exp(own - peak)
    total = jnp.sum(probs, axis=-1, keepdims=True) + own_prob
    probs = probs.astype(jnp.bfloat16)
    lane = lax.broadcasted_iota(jnp.int32, (seq_count * heads, head_dim), 1)
    stats = jnp.where(lane < head_dim // 2, peak, total)
    for copy in small[4:6] + picked[1]:
        copy.wait()
    for s in range(seq_count):
        mine = slice(s * heads, (s + 1) * heads)
        weighted = jnp.dot(probs[mine], values[s], preferred_element_type=jnp.float32)
        own_value = jnp.broadcast_to(
            new_value[s].astype(jnp.float32)[:, None, :], (heads_kv, query_count, head_dim)
        ).reshape(heads, head_dim)
        weighted = weighted + own_prob[mine] * own_value
        for g in range(heads_kv):
            part = slice(g * query_count, (g + 1) * query_count)
            out[:, g * seq_count + s, :] = weighted[part]
            out[:, (heads_kv + g) * seq_count + s, :] = stats[mine][part]
    small[6].wait()


def attention(
    queries, key_cache, value_cache, centroid_keys, centroid_values, selected, new_key, new_value, weight
):
    seq_count, heads_kv, query_count, head_dim = queries.shape
    clusters = centroid_keys.shape[1]
    sel_count = selected.shape[2]
    block_rows = key_cache.shape[1] // clusters * heads_kv
    selected = selected.transpose(1, 2, 0)
    centroid_keys, centroid_values, key_cache, value_cache = (
        value.reshape(seq_count, -1, head_dim)
        for value in (centroid_keys, centroid_values, key_cache, value_cache)
    )
    held_rows = clusters * heads_kv + heads_kv * sel_count * block_rows
    held = pltpu.VMEM((seq_count, held_rows, head_dim), jnp.bfloat16)
    operands = (
        selected, queries, new_key, new_value, centroid_keys, centroid_values, key_cache, value_cache, weight
    )
    return pl.pallas_call(
        attention_kernel,
        out_shape=(
            pltpu.VMEM((query_count, 2 * heads_kv * seq_count, head_dim), jnp.float32),
            pltpu.VMEM(weight.shape, weight.dtype),
        ),
        in_specs=[ANY_SPEC] * 9,
        out_specs=(VMEM_SPEC, VMEM_SPEC),
        scratch_shapes=[
            pltpu.SMEM(selected.shape, selected.dtype),
            pltpu.VMEM(queries.shape, queries.dtype),
            pltpu.VMEM(new_key.shape, new_key.dtype),
            pltpu.VMEM(new_value.shape, new_value.dtype),
            held,
            held,
            pltpu.SemaphoreType.DMA((7,)),
            pltpu.SemaphoreType.DMA((2, seq_count, heads_kv * sel_count)),
        ],
        compiler_params=pltpu.CompilerParams(vmem_limit_bytes=12 << 20),
    )(*[in_hbm(operand) for operand in operands])


def project_kernel(parts, weight, out):
    rows = parts.shape[1] // 2
    half = parts.shape[2] // 2
    weighted = parts[:, :rows, :]
    peak = parts[:, rows:, 0:1]
    total = parts[:, rows:, half : half + 1]
    scale = jnp.exp(peak - jnp.max(peak, axis=0, keepdims=True))
    total = jnp.sum(total * scale, axis=0)
    attended = (jnp.sum(weighted * scale, axis=0) / total).astype(jnp.bfloat16)
    seq_count = out.shape[0]
    sums = None
    for g in range(weight.shape[0]):
        term = jnp.dot(
            attended[g * seq_count : (g + 1) * seq_count],
            weight[g, 0],
            preferred_element_type=jnp.float32,
        )
        sums = term if sums is None else sums + term
    out[...] = sums.astype(jnp.bfloat16)


def project(parts, weight):
    seq_count = parts.shape[1] // (2 * weight.shape[0])
    return pl.pallas_call(
        project_kernel,
        out_shape=jax.ShapeDtypeStruct((seq_count, weight.shape[3]), jnp.bfloat16),
        in_specs=[VMEM_SPEC, VMEM_SPEC],
        out_specs=VMEM_SPEC,
        compiler_params=pltpu.CompilerParams(vmem_limit_bytes=8 << 20),
    )(parts, weight)


def fetch_kernel(first, source, *refs):
    out, sem = refs[-2:]
    count = out.shape[0]
    chunks = 4
    part = source.shape[1] // chunks
    copies = [
        pltpu.make_async_copy(
            source.at[0, pl.ds(c * part, part), :, pl.ds((first + t) * 128, 128)],
            out.at[t, pl.ds(c * part, part)],
            sem.at[t, c],
        )
        for c in range(chunks)
        for t in range(count)
    ]
    for copy in copies:
        copy.start()
    for copy in copies:
        copy.wait()


def fetch(weights, first, count, *after):
    depth = weights.shape[1]
    tiles = pl.pallas_call(
        functools.partial(fetch_kernel, first),
        out_shape=pltpu.VMEM((count, depth, 2, 128), weights.dtype),
        in_specs=[ANY_SPEC] * (1 + len(after)),
        out_specs=VMEM_SPEC,
        scratch_shapes=[pltpu.SemaphoreType.DMA((count, 4))],
        compiler_params=pltpu.CompilerParams(vmem_limit_bytes=1 << 20),
        cost_estimate=pl.CostEstimate(
            flops=0, bytes_accessed=count * depth * 512, transcendentals=0
        ),
    )(in_hbm(weights), *after)
    return tiles.reshape(count, 2 * depth, 128)


def experts_kernel(order, x0, x1, *refs):
    *tiles, down, out, spread = refs
    half, model_dim = x0.shape
    rows = 2 * half
    blocks = len(order)
    seq_count = rows // blocks
    exp_pos = lax.axis_index("exp")
    source = lax.broadcasted_iota(jnp.int32, (128, 512), 0)
    target = lax.broadcasted_iota(jnp.int32, (128, 512), 1)
    ends = (target == 2 * source) | (target == 2 * source + 257)
    to_both = jnp.where(ends, 1.0, 0.0).astype(jnp.bfloat16)
    pieces = []
    for j in range(model_dim // 128):
        pieces += [x[:, j * 128 : (j + 1) * 128] for x in (x0, x1)]
    result = jnp.dot(
        jnp.concatenate(pieces, axis=0), to_both, preferred_element_type=jnp.float32
    ).astype(jnp.bfloat16)
    for j in range(model_dim // 128):
        columns = slice(j * 256, (j + 1) * 256)
        spread[0:rows, columns] = result[j * rows : (j + 1) * rows, 0:256]
        spread[rows : 2 * rows, columns] = result[j * rows : (j + 1) * rows, 256:512]
    lanes = [tile.at[t] for tile in tiles for t in range(tile.shape[0])]
    depth = 1024
    both = []
    for u in range(len(lanes) // 2):
        total = jnp.zeros((2 * rows, 256), jnp.float32)
        for c in range(2 * model_dim // depth):
            here = slice(c * depth, (c + 1) * depth)
            right = jnp.concatenate([lanes[2 * u][here, :], lanes[2 * u + 1][here, :]], axis=1)
            total = total + jnp.dot(spread[:, here], right, preferred_element_type=jnp.float32)
        both.append(total)
    both = jnp.concatenate(both, axis=1)
    gate, up = both[:rows], both[rows:]
    activated = (jax.nn.silu(gate) * up).astype(jnp.bfloat16)
    width = 1024

    def down_part(b, carry):
        columns = pl.ds(pl.multiple_of(b * width, width), width)
        result = jnp.dot(
            activated, down[0, :, columns], preferred_element_type=jnp.float32
        ).astype(jnp.bfloat16)
        for q in range(width // 256):
            for p, i in enumerate(order):
                place = (b * (width // 256) + q) * blocks + lax.bitwise_xor(exp_pos, i)
                mine = result[p * seq_count : (p + 1) * seq_count]
                out[place, 0:seq_count] = mine[:, q * 256 : q * 256 + 128]
                out[place, seq_count : 2 * seq_count] = mine[:, q * 256 + 128 : (q + 1) * 256]
        return carry

    lax.fori_loop(0, model_dim // width, down_part, 0)


def experts(pieces, tiles, down, order):
    half, model_dim = pieces[0].shape
    rows = 2 * half
    blocks = len(order)
    return pl.pallas_call(
        functools.partial(experts_kernel, order),
        out_shape=pltpu.VMEM((model_dim // 256 * blocks, 2 * rows // blocks, 128), jnp.bfloat16),
        in_specs=[VMEM_SPEC] * (3 + len(tiles)),
        out_specs=VMEM_SPEC,
        scratch_shapes=[pltpu.VMEM((2 * rows, 2 * model_dim), jnp.bfloat16)],
        compiler_params=pltpu.CompilerParams(vmem_limit_bytes=16 << 20),
    )(*pieces, *tiles, down)


def sum_kernel(p0, p1, p2, p3, before, out):
    total = p0[...].astype(jnp.float32)
    for piece in (p1, p2, p3):
        total = total + piece[...].astype(jnp.float32)
    out[...] = total.astype(out.dtype)


def sum_pieces(pieces, before):
    return pl.pallas_call(
        sum_kernel,
        out_shape=pltpu.VMEM(pieces[0].shape, pieces[0].dtype),
        in_specs=[VMEM_SPEC] * 4 + [ANY_SPEC],
        out_specs=VMEM_SPEC,
        compiler_params=pltpu.CompilerParams(vmem_limit_bytes=2 << 20),
    )(*pieces, before)


def norm_kernel(sizes, p0, p1, p2, p3, residual, gain, ids, gates, before, own, normed, mix):
    kvh_devices, exp_devices = sizes
    seq_count = residual.shape[0]
    total = residual[...].astype(jnp.float32)
    for piece in (p0, p1, p2, p3):
        total = total + piece[...].astype(jnp.float32)
    mean_square = jnp.mean(total * total, axis=-1, keepdims=True)
    normed[...] = (total * lax.rsqrt(mean_square + 1e-06) * gain[...]).astype(normed.dtype)
    place = lax.axis_index("ctx") * kvh_devices + lax.axis_index("kvh")
    width = own.shape[1]
    own[...] = jnp.zeros(own.shape, own.dtype)
    for p in range(total.shape[1] // width):
        @pl.when(place == p)
        def _():
            own[...] = total[:, p * width : (p + 1) * width]

    shape = (2 * seq_count, mix.shape[1])
    column = lax.broadcasted_iota(jnp.int32, shape, 1)
    device = column // (2 * seq_count)
    expert = device // (kvh_devices * exp_devices) * exp_devices + device % exp_devices
    expert = jnp.where(
        column % (2 * seq_count) == lax.broadcasted_iota(jnp.int32, shape, 0), expert, -1
    )
    weight = jnp.zeros(shape, jnp.float32)
    both_ids = jnp.concatenate([ids[...], ids[...]], axis=0)
    both_gates = jnp.concatenate([gates[...], gates[...]], axis=0)
    for k in range(ids.shape[1]):
        weight = weight + jnp.where(both_ids[:, k : k + 1] == expert, both_gates[:, k : k + 1], 0.0)
    high = weight.astype(jnp.bfloat16)
    mix[0 : 2 * seq_count] = high
    mix[2 * seq_count : 4 * seq_count] = (weight - high.astype(jnp.float32)).astype(jnp.bfloat16)


def norm(pieces, residual, gain, ids, gates, before, sizes, devices):
    seq_count, model_dim = residual.shape
    columns = devices * 2 * seq_count
    return pl.pallas_call(
        functools.partial(norm_kernel, sizes),
        out_shape=(
            pltpu.VMEM((seq_count, 256), jnp.float32),
            pltpu.VMEM((seq_count, model_dim), jnp.bfloat16),
            pltpu.VMEM((4 * seq_count, columns), jnp.bfloat16),
        ),
        in_specs=[VMEM_SPEC] * 8 + [ANY_SPEC],
        out_specs=(VMEM_SPEC,) * 3,
        compiler_params=pltpu.CompilerParams(vmem_limit_bytes=2 << 20),
    )(*pieces, residual, gain.reshape(1, -1), ids, gates, before)


def stack_kernel(p0, p1, p2, p3, before, out):
    out[...] = jnp.concatenate([p0[...], p1[...], p2[...], p3[...]], axis=0)


def stack(pieces, before):
    rows, columns = pieces[0].shape
    return pl.pallas_call(
        stack_kernel,
        out_shape=pltpu.VMEM((4 * rows, columns), pieces[0].dtype),
        in_specs=[VMEM_SPEC] * 4 + [ANY_SPEC],
        out_specs=VMEM_SPEC,
        compiler_params=pltpu.CompilerParams(vmem_limit_bytes=2 << 20),
    )(*pieces, before)


def mix_kernel(returned, mix, own, out):
    seq_count = own.shape[0]
    sums = jnp.dot(mix[...], returned[...], preferred_element_type=jnp.float32)
    sums = sums[0 : 2 * seq_count] + sums[2 * seq_count : 4 * seq_count]
    width = sums.shape[1]
    out[:, 0:width] = (own[:, 0:width] + sums[0:seq_count]).astype(out.dtype)
    out[:, width : 2 * width] = (own[:, width : 2 * width] + sums[seq_count:]).astype(out.dtype)


def mix_results(returned, mix, own):
    return pl.pallas_call(
        mix_kernel,
        out_shape=jax.ShapeDtypeStruct(own.shape, jnp.bfloat16),
        in_specs=[VMEM_SPEC] * 3,
        out_specs=VMEM_SPEC,
        compiler_params=pltpu.CompilerParams(vmem_limit_bytes=2 << 20),
    )(returned.reshape(-1, returned.shape[2]), mix, own)


def swapped(value, axes, count, mask):
    return lax.ppermute(value, axes, [(i, i ^ mask) for i in range(count)])


def body(
    queries,
    key_cache,
    value_cache,
    centroid_keys,
    centroid_values,
    selected,
    new_key,
    new_value,
    out_weight,
    residual,
    norm_gain,
    expert_ids,
    gate_weights,
    w_gate_up,
    w_down,
):
    ctx_devices = lax.axis_size("ctx")
    kvh_devices = lax.axis_size("kvh")
    exp_devices = lax.axis_size("exp")
    plane = ctx_devices * kvh_devices

    parts, out_weight = attention(
        queries,
        key_cache,
        value_cache,
        centroid_keys,
        centroid_values,
        selected,
        new_key,
        new_value,
        out_weight,
    )
    parts = lax.all_to_all(parts, "ctx", split_axis=0, concat_axis=0, tiled=True)

    projected = project(parts, out_weight)

    axes = ("ctx", "kvh")
    along_x = [projected] + [swapped(projected, axes, plane, m) for m in (1, 2, 3)]
    tiles = [fetch(w_gate_up, 0, 2, projected)]
    sums = sum_pieces(along_x, tiles[0])
    along_z = [sums] + [swapped(sums, axes, plane, m) for m in range(4, plane, 4)]
    tiles.append(fetch(w_gate_up, 2, 2, sums))
    own, normed, mix = norm(
        along_z,
        residual,
        norm_gain,
        expert_ids,
        gate_weights,
        tiles[1],
        (kvh_devices, exp_devices),
        plane * exp_devices,
    )

    steps = range(0, exp_devices, 2)
    along_y = [normed] + [swapped(normed, "exp", exp_devices, m) for m in steps[1:]]
    tiles.append(fetch(w_gate_up, 4, 2, normed))
    mine = stack(along_y, tiles[2])
    other = swapped(mine, "exp", exp_devices, 1)
    order = tuple(steps) + tuple(m + 1 for m in steps)
    results = experts((mine, other), tiles, w_down, order)
    returned = lax.all_to_all(
        results, ("ctx", "kvh", "exp"), split_axis=0, concat_axis=0, tiled=True
    )
    return mix_results(returned, mix, own)


def solution(mesh):
    in_specs = (
        P("exp", "kvh", None, None),
        P("exp", "ctx", "kvh", None),
        P("exp", "ctx", "kvh", None),
        P("exp", "ctx", "kvh", None),
        P("exp", "ctx", "kvh", None),
        P("exp", "kvh", "ctx"),
        P("exp", "kvh", None),
        P("exp", "kvh", None),
        P("kvh", "ctx", None, None),
        P("exp", None),
        P(),
        P("exp", None),
        P("exp", None),
        P(("ctx", "exp"), None, None, "kvh"),
        P(("ctx", "exp"), "kvh", None),
    )
    out_specs = P("exp", ("ctx", "kvh"))
    return jax.shard_map(body, mesh=mesh, in_specs=in_specs, out_specs=out_specs, check_vma=False)
```

time: 68.2 us -> 64.8 us (0.950)
  blocking collectives: 0 us -> 29.2 us
  waiting for transfers between devices: 20.6 us -> 2.69 us
  starting transfers between devices: 28.7 us -> 17.1 us
  Pallas kernels: 17.3 us -> 15.3 us
  other arithmetic: 0.93 us -> 0.01 us
    all_to_all x0 -> x2, blocking collectives: none -> 29.2 us  [the longest x1 17.4 us: body(): lax.all_to_all(results, ('ctx', 'kvh', 'exp'), split_axis=0, concat_axis=...]
    all_to_all x2 -> x0, waiting for transfers between devices: 16.3 us -> none  [the longest x1 11.4 us: body(): lax.all_to_all(results, ('ctx', 'kvh', 'exp'), split_axis=0, concat_axis=...]
    all_to_all x2 -> x0, starting transfers between devices: 12.4 us -> none  [the longest x1 6.8 us: body(): lax.all_to_all(parts, 'ctx', split_axis=0, concat_axis=0, tiled=True)]
    ppermute x10, waiting for transfers between devices: 4.32 us -> 2.69 us  [swapped(): return lax.ppermute(value, axes, [(i, i ^ mask) for i in range(count)])]
    pallas_call x1, Pallas kernels: 3.94 us -> 2.91 us  [attention(): pl.pallas_call(attention_kernel, out_shape=(pltpu.VMEM((query_count, 2 *...]
    pallas_call x2 -> x4, Pallas kernels: 6.19 us -> 5.23 us  [the longest x1 4.14 us: experts(): pl.pallas_call(functools.partial(experts_kernel, order), out_shape=pltpu....]
    ppermute x10, starting transfers between devices: 16.3 us -> 17.1 us  [swapped(): return lax.ppermute(value, axes, [(i, i ^ mask) for i in range(count)])]
  transfers between devices with their start and end apart: 12 -> 10, of which waited for: 6 -> 3; matrix products, arithmetic and copies ran while one was open for 0% -> 0% of each run, Pallas kernels for 10% -> 10%
where the time goes in v3:
time: 64.8 us; the launch traced here: 64.5 us
  blocking collectives  29.2 us (45%)
  starting transfers between devices  17.1 us (26%)
  Pallas kernels  15.3 us (24%)
  waiting for transfers between devices  2.69 us (4%)
    all_to_all x1, blocking collectives, body(): lax.all_to_all(results, ('ctx', 'kvh', 'exp'), split_axis=0, concat_axis=...  17.4 us
    ppermute x10, starting transfers between devices, swapped(): return lax.ppermute(value, axes, [(i, i ^ mask) for i in range(count)])  17.1 us
    all_to_all x1, blocking collectives, body(): lax.all_to_all(parts, 'ctx', split_axis=0, concat_axis=0, tiled=True)  11.8 us
    pallas_call x3, Pallas kernels, fetch(): pl.pallas_call(functools.partial(fetch_kernel, first), out_shape=pltpu.VM...  6.64 us
    pallas_call x1, Pallas kernels, experts(): pl.pallas_call(functools.partial(experts_kernel, order), out_shape=pltpu....  4.14 us
    pallas_call x1, Pallas kernels, attention(): pl.pallas_call(attention_kernel, out_shape=(pltpu.VMEM((query_count, 2 *...  2.91 us
    ppermute x10, waiting for transfers between devices, swapped(): return lax.ppermute(value, axes, [(i, i ^ mask) for i in range(count)])  2.69 us
  transfers between devices with their start and end apart: 10, of which 3 were waited for; matrix products, arithmetic and copies ran while one was open for 0% of the time, Pallas kernels for 10%

profile of v3, /device:TPU:1, one launch (start us, length us, event | category | flops | bytes accessed | tf_op | source)
XLA Modules:
  0.0 64.5 jit_solution(5053257066383570038)
XLA Ops:
  0.0 2.9 %shard_map.145 = (f32[8,16,128]{2,1,0:T(8,128)S(1)}, bf16[2,1,128,4096]{3,2,1,0:T(8,128)(2,1)S(1)}) custom-call(s32[2,2,4]{2,1,0:T(2,128)} %bitcast.24, bf16[4,2,8,128]{3,2,1,0:T(8,128)(2,1)} %queries_in.1, bf16[4,2,128]{2,1,0:T(2,128)(2,1)} %new_key_in.1, bf16[4,2,128]{2,1,0:T(2,128)(2,1)} %new_value_in.1, bf16[4,128,128]{2,1,0:T(8,128)(2,1)} %bitcast.22, ...), custom_call_target="tpu_custom_call" | custom-call | tf_op jit(solution)/shard_map/pallas_call | solution.py:145
  2.9 11.8 %all_to_all.10.parts = f32[8,16,128]{2,1,0:T(8,128)S(1)} all-to-all(f32[8,16,128]{2,1,0:T(8,128)S(1)} %get-tuple-element.10), channel_id=1, replica_groups=mesh['ctx'=8,'kvh'=2,'exp'=8] {'ctx'}, dimensions={0} | all-to-all | bytes 131072 | tf_op jit(solution)/shard_map/all_to_all | solution.py:438
  14.7 0.5 shard_map.146.refs_0_.p0
  15.2 1.8 %collective-permute-start.2 = (bf16[4,4096]{1,0:T(4,128)(2,1)S(1)}, bf16[4,4096]{1,0:T(4,128)(2,1)S(1)}, u32[]{:S(2)}, u32[]{:S(2)}) collective-permute-start(bf16[4,4096]{1,0:T(4,128)(2,1)S(1)} %shard_map.146.refs_0_.p0), channel_id=1, source_target_pairs={{0,24},{8,16},{16,8},{24,0},{32,56},{40,48},{48,40},{56,32},{64,88... | collective-permute-start | bytes 98312 | tf_op jit(solution)/shard_map/ppermute | solution.py:402
  17.0 0.4 collective-permute-start.1
  17.4 1.7 %collective-permute-start = (bf16[4,4096]{1,0:T(4,128)(2,1)S(1)}, bf16[4,4096]{1,0:T(4,128)(2,1)S(1)}, u32[]{:S(2)}, u32[]{:S(2)}) collective-permute-start(bf16[4,4096]{1,0:T(4,128)(2,1)S(1)} %shard_map.146.refs_0_.p0), channel_id=1, source_target_pairs={{0,8},{8,0},{16,24},{24,16},{32,40},{40,32},{48,56},{56,48},{64,72... | collective-permute-start | bytes 98312 | tf_op jit(solution)/shard_map/ppermute | solution.py:402
  19.2 2.2 %shard_map.147 = bf16[2,4096,2,128]{3,2,1,0:T(2,128)(2,1)S(1)} custom-call(bf16[1,4096,2,768]{3,2,1,0:T(2,128)(2,1)} %source.5, bf16[4,4096]{1,0:T(4,128)(2,1)S(1)} %shard_map.146.refs_0_.p0), custom_call_target="tpu_custom_call" | custom-call | bytes 4194304 | tf_op jit(solution)/shard_map/pallas_call | solution.py:221
  21.4 0.0 collective-permute-done.2.p3
  21.4 0.0 collective-permute-done.1.p2
  21.4 0.3 collective-permute-done.p1
  21.8 0.0 copy-start
  21.8 0.0 copy-start.1
  21.8 0.0 copy-start.2
  21.8 0.0 copy-start.3
  21.8 1.0 %collective-permute-start.5 = (bf16[4,4096]{1,0:T(4,128)(2,1)S(1)}, bf16[4,4096]{1,0:T(4,128)(2,1)S(1)}, u32[]{:S(2)}, u32[]{:S(2)}) collective-permute-start(bf16[4,4096]{1,0:T(4,128)(2,1)S(1)} %shard_map.148.refs_0_.p0), channel_id=1, source_target_pairs={{0,96},{8,104},{16,112},{24,120},{32,64},{40,72},{48,80},{56,88},{... | collective-permute-start | bytes 98312 | tf_op jit(solution)/shard_map/ppermute | solution.py:402
  22.8 1.2 %collective-permute-start.4 = (bf16[4,4096]{1,0:T(4,128)(2,1)S(1)}, bf16[4,4096]{1,0:T(4,128)(2,1)S(1)}, u32[]{:S(2)}, u32[]{:S(2)}) collective-permute-start(bf16[4,4096]{1,0:T(4,128)(2,1)S(1)} %shard_map.148.refs_0_.p0), channel_id=1, source_target_pairs={{0,64},{8,72},{16,80},{24,88},{32,96},{40,104},{48,112},{56,120},{... | collective-permute-start | bytes 98312 | tf_op jit(solution)/shard_map/ppermute | solution.py:402
  24.0 1.2 %collective-permute-start.3 = (bf16[4,4096]{1,0:T(4,128)(2,1)S(1)}, bf16[4,4096]{1,0:T(4,128)(2,1)S(1)}, u32[]{:S(2)}, u32[]{:S(2)}) collective-permute-start(bf16[4,4096]{1,0:T(4,128)(2,1)S(1)} %shard_map.148.refs_0_.p0), channel_id=1, source_target_pairs={{0,32},{8,40},{16,48},{24,56},{32,0},{40,8},{48,16},{56,24},{64,96... | collective-permute-start | bytes 98312 | tf_op jit(solution)/shard_map/ppermute | solution.py:402
  25.1 2.2 %shard_map.149 = bf16[2,4096,2,128]{3,2,1,0:T(2,128)(2,1)S(1)} custom-call(bf16[1,4096,2,768]{3,2,1,0:T(2,128)(2,1)} %source.5, bf16[4,4096]{1,0:T(4,128)(2,1)S(1)} %shard_map.148.refs_0_.p0), custom_call_target="tpu_custom_call" | custom-call | bytes 4194304 | tf_op jit(solution)/shard_map/pallas_call | solution.py:221
  27.4 0.0 collective-permute-done.5.p3
  27.4 0.0 collective-permute-done.4.p2
  27.4 0.0 collective-permute-done.3.p1
  27.4 0.0 copy-done
  27.4 0.0 copy-done.1
  27.4 0.0 copy-done.2
  27.4 0.0 copy-done.3
  27.4 0.3 shard_map.150
  27.7 0.0 slice-start
  27.8 0.0 slice-start.1
  27.8 2.8 %collective-permute-start.8 = (bf16[4,4096]{1,0:T(4,128)(2,1)S(1)}, bf16[4,4096]{1,0:T(4,128)(2,1)S(1)}, u32[]{:S(2)}, u32[]{:S(2)}) collective-permute-start(bf16[4,4096]{1,0:T(4,128)(2,1)S(1)} %get-tuple-element.12.refs_0_.p0), channel_id=1, source_target_pairs={{0,6},{1,7},{2,4},{3,5},{4,2},{5,3},{6,0},{7,1},{8,14},{9,15},{10,... | collective-permute-start | bytes 98312 | tf_op jit(solution)/shard_map/ppermute | solution.py:402
  30.6 0.3 collective-permute-start.7
  30.9 0.3 collective-permute-start.6
  31.3 2.2 %shard_map.151 = bf16[2,4096,2,128]{3,2,1,0:T(2,128)(2,1)S(1)} custom-call(bf16[1,4096,2,768]{3,2,1,0:T(2,128)(2,1)} %source.5, bf16[4,4096]{1,0:T(4,128)(2,1)S(1)} %get-tuple-element.12.refs_0_.p0), custom_call_target="tpu_custom_call" | custom-call | bytes 4194304 | tf_op jit(solution)/shard_map/pallas_call | solution.py:221
  33.5 0.0 collective-permute-done.8.p3
  33.5 1.4 %collective-permute-done.7.p2 = bf16[4,4096]{1,0:T(4,128)(2,1)S(1)} collective-permute-done((bf16[4,4096]{1,0:T(4,128)(2,1)S(1)}, bf16[4,4096]{1,0:T(4,128)(2,1)S(1)}, u32[]{:S(2)}, u32[]{:S(2)}) %collective-permute-start.7) | collective-permute-done | bytes 32800 | tf_op jit(solution)/shard_map/ppermute | solution.py:402
  34.9 0.0 collective-permute-done.6.p1
  34.9 6.4 %collective-permute-start.9 = (bf16[16,4096]{1,0:T(8,128)(2,1)S(1)}, bf16[16,4096]{1,0:T(8,128)(2,1)S(1)}, u32[]{:S(2)}, u32[]{:S(2)}) collective-permute-start(bf16[16,4096]{1,0:T(8,128)(2,1)S(1)} %shard_map.152.x0), channel_id=1, source_target_pairs={{0,1},{1,0},{2,3},{3,2},{4,5},{5,4},{6,7},{7,6},{8,9},{9,8},{10,11... | collective-permute-start | bytes 393224 | tf_op jit(solution)/shard_map/ppermute | solution.py:402
  41.3 1.0 %collective-permute-done.9.x1 = bf16[16,4096]{1,0:T(8,128)(2,1)S(1)} collective-permute-done((bf16[16,4096]{1,0:T(8,128)(2,1)S(1)}, bf16[16,4096]{1,0:T(8,128)(2,1)S(1)}, u32[]{:S(2)}, u32[]{:S(2)}) %collective-permute-start.9) | collective-permute-done | bytes 131104 | tf_op jit(solution)/shard_map/ppermute | solution.py:402
  42.3 0.0 slice-done
  42.3 0.0 slice-done.1
  42.3 4.1 %shard_map.153 = bf16[128,8,128]{2,1,0:T(8,128)(2,1)S(1)} custom-call(bf16[16,4096]{1,0:T(8,128)(2,1)S(1)} %shard_map.152.x0, bf16[16,4096]{1,0:T(8,128)(2,1)S(1)} %collective-permute-done.9.x1, bf16[2,8192,128]{2,1,0:T(8,128)(2,1)S(1)} %bitcast.11, bf16[2,8192,128]{2,1,0:T(8,128)(2,1)S(1)} %bitcast.13, bf16[2,8192,128]{2,1,0:T(8,128)(2,1)S(1)} %bitcast.15, ...), custom_call_target="tpu_custom_call" | custom-call | tf_op jit(solution)/shard_map/pallas_call | solution.py:291
  46.4 17.4 %all_to_all.11 = bf16[128,8,128]{2,1,0:T(8,128)(2,1)S(1)} all-to-all(bf16[128,8,128]{2,1,0:T(8,128)(2,1)S(1)} %shard_map.153), channel_id=1, replica_groups=mesh['ctx'=8,'kvh'=2,'exp'=8] {'ctx','kvh','exp'}, dimensions={0} | all-to-all | bytes 524288 | tf_op jit(solution)/shard_map/all_to_all | solution.py:466
  63.8 0.7 %shard_map.154 = bf16[4,256]{1,0:T(4,128)(2,1)} custom-call(bf16[1024,128]{1,0:T(8,128)(2,1)S(1)} %bitcast.18, bf16[16,1024]{1,0:T(8,128)(2,1)S(1)} %get-tuple-element.13.mix, f32[4,256]{1,0:T(4,128)S(1)} %get-tuple-element.14.own), custom_call_target="tpu_custom_call" | custom-call | tf_op jit(solution)/shard_map/pallas_call | solution.py:392
  (3 shorter events, 0.1 us)
Async XLA Ops:
  15.2 6.2 %collective-permute-start.2 = (bf16[4,4096]{1,0:T(4,128)(2,1)S(1)}, bf16[4,4096]{1,0:T(4,128)(2,1)S(1)}, u32[]{:S(2)}, u32[]{:S(2)}) collective-permute-start(bf16[4,4096]{1,0:T(4,128)(2,1)S(1)} %shard_map.146.refs_0_.p0), channel_id=1, source_target_pairs={{0,24},{8,16},{16,8},{24,0},{32,56},{40,48},{48,40},{56,32},{64,88... | collective-permute-start | bytes 98312 | tf_op jit(solution)/shard_map/ppermute | solution.py:402
  17.0 4.4 %collective-permute-start.1 = (bf16[4,4096]{1,0:T(4,128)(2,1)S(1)}, bf16[4,4096]{1,0:T(4,128)(2,1)S(1)}, u32[]{:S(2)}, u32[]{:S(2)}) collective-permute-start(bf16[4,4096]{1,0:T(4,128)(2,1)S(1)} %shard_map.146.refs_0_.p0), channel_id=1, source_target_pairs={{0,16},{8,24},{16,0},{24,8},{32,48},{40,56},{48,32},{56,40},{64,80... | collective-permute-start | bytes 98312 | tf_op jit(solution)/shard_map/ppermute | solution.py:402
  17.4 4.3 %collective-permute-start = (bf16[4,4096]{1,0:T(4,128)(2,1)S(1)}, bf16[4,4096]{1,0:T(4,128)(2,1)S(1)}, u32[]{:S(2)}, u32[]{:S(2)}) collective-permute-start(bf16[4,4096]{1,0:T(4,128)(2,1)S(1)} %shard_map.146.refs_0_.p0), channel_id=1, source_target_pairs={{0,8},{8,0},{16,24},{24,16},{32,40},{40,32},{48,56},{56,48},{64,72... | collective-permute-start | bytes 98312 | tf_op jit(solution)/shard_map/ppermute | solution.py:402
  21.8 5.6 %copy-start = (bf16[4,4096]{1,0:T(4,128)(2,1)S(1)}, bf16[4,4096]{1,0:T(4,128)(2,1)}, u32[]{:S(2)}) copy-start(bf16[4,4096]{1,0:T(4,128)(2,1)} %residual.1) | copy-start | bytes 98308
  21.8 5.6 %copy-start.1 = (f32[4096]{0:T(1024)S(1)}, f32[4096]{0:T(1024)}, u32[]{:S(2)}) copy-start(f32[4096]{0:T(1024)} %param.25) | copy-start | bytes 49156
  21.8 5.6 %copy-start.2 = (s32[4,8]{1,0:T(4,128)S(1)}, s32[4,8]{1,0:T(4,128)}, u32[]{:S(2)}) copy-start(s32[4,8]{1,0:T(4,128)} %ids.1) | copy-start | bytes 388
  21.8 5.6 %copy-start.3 = (f32[4,8]{1,0:T(4,128)S(1)}, f32[4,8]{1,0:T(4,128)}, u32[]{:S(2)}) copy-start(f32[4,8]{1,0:T(4,128)} %gates.1) | copy-start | bytes 388
  21.8 5.6 %collective-permute-start.5 = (bf16[4,4096]{1,0:T(4,128)(2,1)S(1)}, bf16[4,4096]{1,0:T(4,128)(2,1)S(1)}, u32[]{:S(2)}, u32[]{:S(2)}) collective-permute-start(bf16[4,4096]{1,0:T(4,128)(2,1)S(1)} %shard_map.148.refs_0_.p0), channel_id=1, source_target_pairs={{0,96},{8,104},{16,112},{24,120},{32,64},{40,72},{48,80},{56,88},{... | collective-permute-start | bytes 98312 | tf_op jit(solution)/shard_map/ppermute | solution.py:402
  22.8 4.6 %collective-permute-start.4 = (bf16[4,4096]{1,0:T(4,128)(2,1)S(1)}, bf16[4,4096]{1,0:T(4,128)(2,1)S(1)}, u32[]{:S(2)}, u32[]{:S(2)}) collective-permute-start(bf16[4,4096]{1,0:T(4,128)(2,1)S(1)} %shard_map.148.refs_0_.p0), channel_id=1, source_target_pairs={{0,64},{8,72},{16,80},{24,88},{32,96},{40,104},{48,112},{56,120},{... | collective-permute-start | bytes 98312 | tf_op jit(solution)/shard_map/ppermute | solution.py:402
  24.0 3.4 %collective-permute-start.3 = (bf16[4,4096]{1,0:T(4,128)(2,1)S(1)}, bf16[4,4096]{1,0:T(4,128)(2,1)S(1)}, u32[]{:S(2)}, u32[]{:S(2)}) collective-permute-start(bf16[4,4096]{1,0:T(4,128)(2,1)S(1)} %shard_map.148.refs_0_.p0), channel_id=1, source_target_pairs={{0,32},{8,40},{16,48},{24,56},{32,0},{40,8},{48,16},{56,24},{64,96... | collective-permute-start | bytes 98312 | tf_op jit(solution)/shard_map/ppermute | solution.py:402
  27.7 14.5 %slice-start = ((s8[6291456]{0:T(1024)(128)(4,1)}), s8[4194304]{0:T(1024)(128)(4,1)S(1)}, s32[]{:S(2)}) async-start(s8[6291456]{0:T(1024)(128)(4,1)} %bitcast.16), calls=%async_computation.2 | async-start | bytes 8388608
  27.8 14.5 %slice-start.1 = ((s8[6291456]{0:T(1024)(128)(4,1)}), s8[2097152]{0:T(1024)(128)(4,1)S(1)}, s32[]{:S(2)}) async-start(s8[6291456]{0:T(1024)(128)(4,1)} %bitcast.16), calls=%async_computation.3 | async-start | bytes 4194304
  27.8 5.7 %collective-permute-start.8 = (bf16[4,4096]{1,0:T(4,128)(2,1)S(1)}, bf16[4,4096]{1,0:T(4,128)(2,1)S(1)}, u32[]{:S(2)}, u32[]{:S(2)}) collective-permute-start(bf16[4,4096]{1,0:T(4,128)(2,1)S(1)} %get-tuple-element.12.refs_0_.p0), channel_id=1, source_target_pairs={{0,6},{1,7},{2,4},{3,5},{4,2},{5,3},{6,0},{7,1},{8,14},{9,15},{10,... | collective-permute-start | bytes 98312 | tf_op jit(solution)/shard_map/ppermute | solution.py:402
  30.6 4.3 %collective-permute-start.7 = (bf16[4,4096]{1,0:T(4,128)(2,1)S(1)}, bf16[4,4096]{1,0:T(4,128)(2,1)S(1)}, u32[]{:S(2)}, u32[]{:S(2)}) collective-permute-start(bf16[4,4096]{1,0:T(4,128)(2,1)S(1)} %get-tuple-element.12.refs_0_.p0), channel_id=1, source_target_pairs={{0,4},{1,5},{2,6},{3,7},{4,0},{5,1},{6,2},{7,3},{8,12},{9,13},{10,... | collective-permute-start | bytes 98312 | tf_op jit(solution)/shard_map/ppermute | solution.py:402
  30.9 3.9 %collective-permute-start.6 = (bf16[4,4096]{1,0:T(4,128)(2,1)S(1)}, bf16[4,4096]{1,0:T(4,128)(2,1)S(1)}, u32[]{:S(2)}, u32[]{:S(2)}) collective-permute-start(bf16[4,4096]{1,0:T(4,128)(2,1)S(1)} %get-tuple-element.12.refs_0_.p0), channel_id=1, source_target_pairs={{0,2},{1,3},{2,0},{3,1},{4,6},{5,7},{6,4},{7,5},{8,10},{9,11},{10,... | collective-permute-start | bytes 98312 | tf_op jit(solution)/shard_map/ppermute | solution.py:402
  34.9 7.4 %collective-permute-start.9 = (bf16[16,4096]{1,0:T(8,128)(2,1)S(1)}, bf16[16,4096]{1,0:T(8,128)(2,1)S(1)}, u32[]{:S(2)}, u32[]{:S(2)}) collective-permute-start(bf16[16,4096]{1,0:T(8,128)(2,1)S(1)} %shard_map.152.x0), channel_id=1, source_target_pairs={{0,1},{1,0},{2,3},{3,2},{4,5},{5,4},{6,7},{7,6},{8,9},{9,8},{10,11... | collective-permute-start | bytes 393224 | tf_op jit(solution)/shard_map/ppermute | solution.py:402

commit v4 on v3

--- a/solution.py
+++ b/solution.py
@@ -12,6 +12,7 @@
 SMEM_SPEC = pl.BlockSpec(memory_space=pltpu.SMEM)
 ANY_SPEC = pl.BlockSpec(memory_space=pl.ANY)
 MASKED = -1e30
+ROW_SLOTS = 2
 
 
 def in_hbm(value):
@@ -234,11 +235,32 @@
 
 def experts_kernel(order, x0, x1, *refs):
     *tiles, down, out, spread = refs
-    half, model_dim = x0.shape
+    half = x0.shape[0]
+    model_dim = spread.shape[1] // 2
     rows = 2 * half
     blocks = len(order)
     seq_count = rows // blocks
+    slots = out.shape[1] // 2
     exp_pos = lax.axis_index("exp")
+    names = jnp.concatenate([x0[:, model_dim:], x1[:, model_dim:]], axis=0).astype(jnp.float32)
+    lane = lax.broadcasted_iota(jnp.int32, names.shape, 1)
+    here = lax.axis_index("ctx") * blocks + exp_pos
+    named = jnp.sum(jnp.where(lane == here, names, 0.0), axis=-1, keepdims=True)
+    row = lax.broadcasted_iota(jnp.int32, (rows, rows), 0)
+    col = lax.broadcasted_iota(jnp.int32, (rows, rows), 1)
+    earlier = (row // seq_count == col // seq_count) & (row < col)
+    ones = jnp.ones((blocks * slots, rows), jnp.bfloat16)
+    by_column = jnp.dot(
+        ones, jnp.where(row == col, named, 0.0).astype(jnp.bfloat16), preferred_element_type=jnp.float32
+    )
+    rank = jnp.dot(
+        ones, jnp.where(earlier, named, 0.0).astype(jnp.bfloat16), preferred_element_type=jnp.float32
+    )
+    slot = lax.broadcasted_iota(jnp.int32, by_column.shape, 0)
+    member = lax.broadcasted_iota(jnp.int32, by_column.shape, 1)
+    chosen = (by_column > 0.5) & (slot // slots == member // seq_count)
+    chosen = chosen & (jnp.abs(rank - (slot % slots).astype(jnp.float32)) < 0.5)
+    chosen = jnp.where(chosen, 1.0, 0.0).astype(jnp.bfloat16)
     source = lax.broadcasted_iota(jnp.int32, (128, 512), 0)
     target = lax.broadcasted_iota(jnp.int32, (128, 512), 1)
     ends = (target == 2 * source) | (target == 2 * source + 257)
@@ -266,6 +288,7 @@
     both = jnp.concatenate(both, axis=1)
     gate, up = both[:rows], both[rows:]
     activated = (jax.nn.silu(gate) * up).astype(jnp.bfloat16)
+    activated = jnp.dot(chosen, activated, preferred_element_type=jnp.float32).astype(jnp.bfloat16)
     width = 1024
 
     def down_part(b, carry):
@@ -276,21 +299,22 @@
         for q in range(width // 256):
             for p, i in enumerate(order):
                 place = (b * (width // 256) + q) * blocks + lax.bitwise_xor(exp_pos, i)
-                mine = result[p * seq_count : (p + 1) * seq_count]
-                out[place, 0:seq_count] = mine[:, q * 256 : q * 256 + 128]
-                out[place, seq_count : 2 * seq_count] = mine[:, q * 256 + 128 : (q + 1) * 256]
+                mine = result[p * slots : (p + 1) * slots]
+                out[place, 0:slots] = mine[:, q * 256 : q * 256 + 128]
+                out[place, slots : 2 * slots] = mine[:, q * 256 + 128 : (q + 1) * 256]
         return carry
 
     lax.fori_loop(0, model_dim // width, down_part, 0)
 
 
-def experts(pieces, tiles, down, order):
-    half, model_dim = pieces[0].shape
+def experts(pieces, tiles, down, order, slots):
+    half = pieces[0].shape[0]
+    model_dim = down.shape[2]
     rows = 2 * half
     blocks = len(order)
     return pl.pallas_call(
         functools.partial(experts_kernel, order),
-        out_shape=pltpu.VMEM((model_dim // 256 * blocks, 2 * rows // blocks, 128), jnp.bfloat16),
+        out_shape=pltpu.VMEM((model_dim // 256 * blocks, 2 * slots, 128), jnp.bfloat16),
         in_specs=[VMEM_SPEC] * (3 + len(tiles)),
         out_specs=VMEM_SPEC,
         scratch_shapes=[pltpu.VMEM((2 * rows, 2 * model_dim), jnp.bfloat16)],
@@ -315,53 +339,76 @@
     )(*pieces, before)
 
 
-def norm_kernel(sizes, p0, p1, p2, p3, residual, gain, ids, gates, before, own, normed, mix):
-    kvh_devices, exp_devices = sizes
-    seq_count = residual.shape[0]
+def norm_kernel(kvh_devices, p0, p1, p2, p3, residual, gain, ids, before, own, normed):
     total = residual[...].astype(jnp.float32)
     for piece in (p0, p1, p2, p3):
         total = total + piece[...].astype(jnp.float32)
+    seq_count, model_dim = total.shape
     mean_square = jnp.mean(total * total, axis=-1, keepdims=True)
-    normed[...] = (total * lax.rsqrt(mean_square + 1e-06) * gain[...]).astype(normed.dtype)
+    rows = total * lax.rsqrt(mean_square + 1e-06) * gain[...]
+    normed[:, :model_dim] = rows.astype(normed.dtype)
+    lane = lax.broadcasted_iota(jnp.int32, (seq_count, normed.shape[1] - model_dim), 1)
+    names = jnp.zeros(lane.shape, jnp.float32)
+    for k in range(ids.shape[1]):
+        names = jnp.where(ids[:, k : k + 1] == lane, 1.0, names)
+    normed[:, model_dim:] = names.astype(normed.dtype)
     place = lax.axis_index("ctx") * kvh_devices + lax.axis_index("kvh")
     width = own.shape[1]
-    own[...] = jnp.zeros(own.shape, own.dtype)
-    for p in range(total.shape[1] // width):
+    for p in range(model_dim // width):
         @pl.when(place == p)
         def _():
             own[...] = total[:, p * width : (p + 1) * width]
 
-    shape = (2 * seq_count, mix.shape[1])
+
+def norm(pieces, residual, gain, ids, before, kvh_devices):
+    seq_count, model_dim = residual.shape
+    return pl.pallas_call(
+        functools.partial(norm_kernel, kvh_devices),
+        out_shape=(
+            pltpu.VMEM((seq_count, 256), jnp.float32),
+            pltpu.VMEM((seq_count, model_dim + 128), jnp.bfloat16),
+        ),
+        in_specs=[VMEM_SPEC] * 7 + [ANY_SPEC],
+        out_specs=(VMEM_SPEC,) * 2,
+        compiler_params=pltpu.CompilerParams(vmem_limit_bytes=2 << 20),
+    )(*pieces, residual, gain.reshape(1, -1), ids, before)
+
+
+def weights_kernel(sizes, ids, gates, after, mix):
+    kvh_devices, exp_devices, slots = sizes
+    seq_count = ids.shape[0]
+    shape = (seq_count, mix.shape[1])
     column = lax.broadcasted_iota(jnp.int32, shape, 1)
-    device = column // (2 * seq_count)
+    device = column // (2 * slots)
     expert = device // (kvh_devices * exp_devices) * exp_devices + device % exp_devices
-    expert = jnp.where(
-        column % (2 * seq_count) == lax.broadcasted_iota(jnp.int32, shape, 0), expert, -1
-    )
     weight = jnp.zeros(shape, jnp.float32)
-    both_ids = jnp.concatenate([ids[...], ids[...]], axis=0)
-    both_gates = jnp.concatenate([gates[...], gates[...]], axis=0)
+    named = jnp.zeros(shape, jnp.float32)
     for k in range(ids.shape[1]):
-        weight = weight + jnp.where(both_ids[:, k : k + 1] == expert, both_gates[:, k : k + 1], 0.0)
+        match = ids[:, k : k + 1] == expert
+        weight = jnp.where(match, gates[:, k : k + 1], weight)
+        named = jnp.where(match, 1.0, named)
+    rank = [jnp.zeros((1, shape[1]), jnp.float32)]
+    for r in range(seq_count - 1):
+        rank.append(rank[-1] + named[r : r + 1])
+    rank = jnp.concatenate(rank, axis=0)
+    slot = (column % slots).astype(jnp.float32)
+    weight = jnp.where(jnp.abs(rank - slot) < 0.5, weight, 0.0)
+    half = column // slots % 2
+    weight = jnp.concatenate([jnp.where(half == h, weight, 0.0) for h in range(2)], axis=0)
     high = weight.astype(jnp.bfloat16)
     mix[0 : 2 * seq_count] = high
     mix[2 * seq_count : 4 * seq_count] = (weight - high.astype(jnp.float32)).astype(jnp.bfloat16)
 
 
-def norm(pieces, residual, gain, ids, gates, before, sizes, devices):
-    seq_count, model_dim = residual.shape
-    columns = devices * 2 * seq_count
-    return pl.pallas_call(
-        functools.partial(norm_kernel, sizes),
-        out_shape=(
-            pltpu.VMEM((seq_count, 256), jnp.float32),
-            pltpu.VMEM((seq_count, model_dim), jnp.bfloat16),
-            pltpu.VMEM((4 * seq_count, columns), jnp.bfloat16),
-        ),
-        in_specs=[VMEM_SPEC] * 8 + [ANY_SPEC],
-        out_specs=(VMEM_SPEC,) * 3,
+def mixing_weights(ids, gates, after, sizes, devices):
+    slots = sizes[2]
+    return pl.pallas_call(
+        functools.partial(weights_kernel, sizes),
+        out_shape=pltpu.VMEM((4 * ids.shape[0], devices * 2 * slots), jnp.bfloat16),
+        in_specs=[VMEM_SPEC] * 2 + [ANY_SPEC],
+        out_specs=VMEM_SPEC,
         compiler_params=pltpu.CompilerParams(vmem_limit_bytes=2 << 20),
-    )(*pieces, residual, gain.reshape(1, -1), ids, gates, before)
+    )(ids, gates, after)
 
 
 def stack_kernel(p0, p1, p2, p3, before, out):
@@ -445,16 +492,7 @@
     sums = sum_pieces(along_x, tiles[0])
     along_z = [sums] + [swapped(sums, axes, plane, m) for m in range(4, plane, 4)]
     tiles.append(fetch(w_gate_up, 2, 2, sums))
-    own, normed, mix = norm(
-        along_z,
-        residual,
-        norm_gain,
-        expert_ids,
-        gate_weights,
-        tiles[1],
-        (kvh_devices, exp_devices),
-        plane * exp_devices,
-    )
+    own, normed = norm(along_z, residual, norm_gain, expert_ids, tiles[1], kvh_devices)
 
     steps = range(0, exp_devices, 2)
     along_y = [normed] + [swapped(normed, "exp", exp_devices, m) for m in steps[1:]]
@@ -462,10 +500,12 @@
     mine = stack(along_y, tiles[2])
     other = swapped(mine, "exp", exp_devices, 1)
     order = tuple(steps) + tuple(m + 1 for m in steps)
-    results = experts((mine, other), tiles, w_down, order)
+    results = experts((mine, other), tiles, w_down, order, ROW_SLOTS)
     returned = lax.all_to_all(
         results, ("ctx", "kvh", "exp"), split_axis=0, concat_axis=0, tiled=True
     )
+    sizes = (kvh_devices, exp_devices, ROW_SLOTS)
+    mix = mixing_weights(expert_ids, gate_weights, results, sizes, plane * exp_devices)
     return mix_results(returned, mix, own)
 
 

time: 64.8 us -> 64.3 us (level)
  blocking collectives: 29.2 us -> 11.8 us
  waiting for transfers between devices: 2.69 us -> 12.7 us
  starting transfers between devices: 17.1 us -> 23.3 us
    all_to_all x1 -> x0, blocking collectives: 17.4 us -> none  [body(): lax.all_to_all(results, ('ctx', 'kvh', 'exp'), split_axis=0, concat_axis=...]
    all_to_all x0 -> x1, waiting for transfers between devices: none -> 10 us  [body(): lax.all_to_all(results, ('ctx', 'kvh', 'exp'), split_axis=0, concat_axis=...]
    all_to_all x0 -> x1, starting transfers between devices: none -> 6.2 us  [body(): lax.all_to_all(results, ('ctx', 'kvh', 'exp'), split_axis=0, concat_axis=...]
  transfers between devices with their start and end apart: 10 -> 11, of which waited for: 3 -> 4; matrix products, arithmetic and copies ran while one was open for 0% -> 0% of each run, Pallas kernels for 10% -> 11%
where the time goes in v4:
time: 64.3 us; the launch traced here: 64 us
  starting transfers between devices  23.3 us (36%)
  Pallas kernels  15.9 us (25%)
  waiting for transfers between devices  12.7 us (20%)
  blocking collectives  11.8 us (18%)
    ppermute x10, starting transfers between devices, swapped(): return lax.ppermute(value, axes, [(i, i ^ mask) for i in range(count)])  17.1 us
    all_to_all x1, blocking collectives, body(): lax.all_to_all(parts, 'ctx', split_axis=0, concat_axis=0, tiled=True)  11.8 us
    all_to_all x1, waiting for transfers between devices, body(): lax.all_to_all(results, ('ctx', 'kvh', 'exp'), split_axis=0, concat_axis=...  10 us
    pallas_call x3, Pallas kernels, fetch(): pl.pallas_call(functools.partial(fetch_kernel, first), out_shape=pltpu.VM...  6.64 us
    all_to_all x1, starting transfers between devices, body(): lax.all_to_all(results, ('ctx', 'kvh', 'exp'), split_axis=0, concat_axis=...  6.2 us
    pallas_call x1, Pallas kernels, experts(): pl.pallas_call(functools.partial(experts_kernel, order), out_shape=pltpu....  4.77 us
    pallas_call x1, Pallas kernels, attention(): pl.pallas_call(attention_kernel, out_shape=(pltpu.VMEM((query_count, 2 *...  2.91 us
    ppermute x10, waiting for transfers between devices, swapped(): return lax.ppermute(value, axes, [(i, i ^ mask) for i in range(count)])  2.7 us
  transfers between devices with their start and end apart: 11, of which 4 were waited for; matrix products, arithmetic and copies ran while one was open for 0% of the time, Pallas kernels for 11%

profile of v4, /device:TPU:1, one launch (start us, length us, event | category | flops | bytes accessed | tf_op | source)
XLA Modules:
  0.0 64.0 jit_solution(6733216851327803827)
XLA Ops:
  0.0 2.9 %shard_map.145 = (f32[8,16,128]{2,1,0:T(8,128)S(1)}, bf16[2,1,128,4096]{3,2,1,0:T(8,128)(2,1)S(1)}) custom-call(s32[2,2,4]{2,1,0:T(2,128)} %bitcast.24, bf16[4,2,8,128]{3,2,1,0:T(8,128)(2,1)} %queries_in.1, bf16[4,2,128]{2,1,0:T(2,128)(2,1)} %new_key_in.1, bf16[4,2,128]{2,1,0:T(2,128)(2,1)} %new_value_in.1, bf16[4,128,128]{2,1,0:T(8,128)(2,1)} %bitcast.22, ...), custom_call_target="tpu_custom_call" | custom-call | tf_op jit(solution)/shard_map/pallas_call | solution.py:146
  2.9 11.8 %all_to_all.10.parts = f32[8,16,128]{2,1,0:T(8,128)S(1)} all-to-all(f32[8,16,128]{2,1,0:T(8,128)S(1)} %get-tuple-element.9), channel_id=1, replica_groups=mesh['ctx'=8,'kvh'=2,'exp'=8] {'ctx'}, dimensions={0} | all-to-all | bytes 131072 | tf_op jit(solution)/shard_map/all_to_all | solution.py:485
  14.7 0.5 shard_map.146.refs_0_.p0
  15.2 1.8 %collective-permute-start.2 = (bf16[4,4096]{1,0:T(4,128)(2,1)S(1)}, bf16[4,4096]{1,0:T(4,128)(2,1)S(1)}, u32[]{:S(2)}, u32[]{:S(2)}) collective-permute-start(bf16[4,4096]{1,0:T(4,128)(2,1)S(1)} %shard_map.146.refs_0_.p0), channel_id=1, source_target_pairs={{0,24},{8,16},{16,8},{24,0},{32,56},{40,48},{48,40},{56,32},{64,88... | collective-permute-start | bytes 98312 | tf_op jit(solution)/shard_map/ppermute | solution.py:449
  17.0 0.4 collective-permute-start.1
  17.4 1.7 %collective-permute-start = (bf16[4,4096]{1,0:T(4,128)(2,1)S(1)}, bf16[4,4096]{1,0:T(4,128)(2,1)S(1)}, u32[]{:S(2)}, u32[]{:S(2)}) collective-permute-start(bf16[4,4096]{1,0:T(4,128)(2,1)S(1)} %shard_map.146.refs_0_.p0), channel_id=1, source_target_pairs={{0,8},{8,0},{16,24},{24,16},{32,40},{40,32},{48,56},{56,48},{64,72... | collective-permute-start | bytes 98312 | tf_op jit(solution)/shard_map/ppermute | solution.py:449
  19.2 2.2 %shard_map.147 = bf16[2,4096,2,128]{3,2,1,0:T(2,128)(2,1)S(1)} custom-call(bf16[1,4096,2,768]{3,2,1,0:T(2,128)(2,1)} %source.5, bf16[4,4096]{1,0:T(4,128)(2,1)S(1)} %shard_map.146.refs_0_.p0), custom_call_target="tpu_custom_call" | custom-call | bytes 4194304 | tf_op jit(solution)/shard_map/pallas_call | solution.py:222
  21.4 0.0 collective-permute-done.2.p3
  21.4 0.0 collective-permute-done.1.p2
  21.4 0.3 collective-permute-done.p1
  21.8 0.0 copy-start
  21.8 0.0 copy-start.1
  21.8 0.0 copy-start.2
  21.8 1.0 %collective-permute-start.5 = (bf16[4,4096]{1,0:T(4,128)(2,1)S(1)}, bf16[4,4096]{1,0:T(4,128)(2,1)S(1)}, u32[]{:S(2)}, u32[]{:S(2)}) collective-permute-start(bf16[4,4096]{1,0:T(4,128)(2,1)S(1)} %shard_map.148.refs_0_.p0), channel_id=1, source_target_pairs={{0,96},{8,104},{16,112},{24,120},{32,64},{40,72},{48,80},{56,88},{... | collective-permute-start | bytes 98312 | tf_op jit(solution)/shard_map/ppermute | solution.py:449
  22.8 1.2 %collective-permute-start.4 = (bf16[4,4096]{1,0:T(4,128)(2,1)S(1)}, bf16[4,4096]{1,0:T(4,128)(2,1)S(1)}, u32[]{:S(2)}, u32[]{:S(2)}) collective-permute-start(bf16[4,4096]{1,0:T(4,128)(2,1)S(1)} %shard_map.148.refs_0_.p0), channel_id=1, source_target_pairs={{0,64},{8,72},{16,80},{24,88},{32,96},{40,104},{48,112},{56,120},{... | collective-permute-start | bytes 98312 | tf_op jit(solution)/shard_map/ppermute | solution.py:449
  23.9 1.2 %collective-permute-start.3 = (bf16[4,4096]{1,0:T(4,128)(2,1)S(1)}, bf16[4,4096]{1,0:T(4,128)(2,1)S(1)}, u32[]{:S(2)}, u32[]{:S(2)}) collective-permute-start(bf16[4,4096]{1,0:T(4,128)(2,1)S(1)} %shard_map.148.refs_0_.p0), channel_id=1, source_target_pairs={{0,32},{8,40},{16,48},{24,56},{32,0},{40,8},{48,16},{56,24},{64,96... | collective-permute-start | bytes 98312 | tf_op jit(solution)/shard_map/ppermute | solution.py:449
  25.1 2.2 %shard_map.149 = bf16[2,4096,2,128]{3,2,1,0:T(2,128)(2,1)S(1)} custom-call(bf16[1,4096,2,768]{3,2,1,0:T(2,128)(2,1)} %source.5, bf16[4,4096]{1,0:T(4,128)(2,1)S(1)} %shard_map.148.refs_0_.p0), custom_call_target="tpu_custom_call" | custom-call | bytes 4194304 | tf_op jit(solution)/shard_map/pallas_call | solution.py:222
  27.3 0.0 collective-permute-done.5.p3
  27.4 0.0 collective-permute-done.4.p2
  27.4 0.0 collective-permute-done.3.p1
  27.4 0.0 copy-done
  27.4 0.0 copy-done.1
  27.4 0.0 copy-done.2
  27.4 0.2 shard_map.150
  27.6 0.0 slice-start
  27.6 0.0 slice-start.1
  27.7 2.8 %collective-permute-start.8 = (bf16[4,4224]{1,0:T(4,128)(2,1)S(1)}, bf16[4,4224]{1,0:T(4,128)(2,1)S(1)}, u32[]{:S(2)}, u32[]{:S(2)}) collective-permute-start(bf16[4,4224]{1,0:T(4,128)(2,1)S(1)} %get-tuple-element.11.refs_0_.p0), channel_id=1, source_target_pairs={{0,6},{1,7},{2,4},{3,5},{4,2},{5,3},{6,0},{7,1},{8,14},{9,15},{10,... | collective-permute-start | bytes 101384 | tf_op jit(solution)/shard_map/ppermute | solution.py:449
  30.5 0.3 collective-permute-start.7
  30.8 0.3 collective-permute-start.6
  31.1 2.2 %shard_map.151 = bf16[2,4096,2,128]{3,2,1,0:T(2,128)(2,1)S(1)} custom-call(bf16[1,4096,2,768]{3,2,1,0:T(2,128)(2,1)} %source.5, bf16[4,4224]{1,0:T(4,128)(2,1)S(1)} %get-tuple-element.11.refs_0_.p0), custom_call_target="tpu_custom_call" | custom-call | bytes 4194304 | tf_op jit(solution)/shard_map/pallas_call | solution.py:222
  33.4 0.0 collective-permute-done.8.p3
  33.4 1.4 %collective-permute-done.7.p2 = bf16[4,4224]{1,0:T(4,128)(2,1)S(1)} collective-permute-done((bf16[4,4224]{1,0:T(4,128)(2,1)S(1)}, bf16[4,4224]{1,0:T(4,128)(2,1)S(1)}, u32[]{:S(2)}, u32[]{:S(2)}) %collective-permute-start.7) | collective-permute-done | bytes 33824 | tf_op jit(solution)/shard_map/ppermute | solution.py:449
  34.7 0.0 collective-permute-done.6.p1
  34.8 0.0 copy-start.3
  34.8 6.4 %collective-permute-start.9 = (bf16[16,4224]{1,0:T(8,128)(2,1)S(1)}, bf16[16,4224]{1,0:T(8,128)(2,1)S(1)}, u32[]{:S(2)}, u32[]{:S(2)}) collective-permute-start(bf16[16,4224]{1,0:T(8,128)(2,1)S(1)} %shard_map.152.x0), channel_id=1, source_target_pairs={{0,1},{1,0},{2,3},{3,2},{4,5},{5,4},{6,7},{7,6},{8,9},{9,8},{10,11... | collective-permute-start | bytes 405512 | tf_op jit(solution)/shard_map/ppermute | solution.py:449
  41.2 1.0 %collective-permute-done.9.x1 = bf16[16,4224]{1,0:T(8,128)(2,1)S(1)} collective-permute-done((bf16[16,4224]{1,0:T(8,128)(2,1)S(1)}, bf16[16,4224]{1,0:T(8,128)(2,1)S(1)}, u32[]{:S(2)}, u32[]{:S(2)}) %collective-permute-start.9) | collective-permute-done | bytes 135200 | tf_op jit(solution)/shard_map/ppermute | solution.py:449
  42.2 0.0 slice-done
  42.2 0.0 slice-done.1
  42.2 4.8 %shard_map.153.after = bf16[128,4,128]{2,1,0:T(4,128)(2,1)} custom-call(bf16[16,4224]{1,0:T(8,128)(2,1)S(1)} %shard_map.152.x0, bf16[16,4224]{1,0:T(8,128)(2,1)S(1)} %collective-permute-done.9.x1, bf16[2,8192,128]{2,1,0:T(8,128)(2,1)S(1)} %bitcast.11, bf16[2,8192,128]{2,1,0:T(8,128)(2,1)S(1)} %bitcast.13, bf16[2,8192,128]{2,1,0:T(8,128)(2,1)S(1)} %bitcast.15, ...), custom_call_target="tpu_custom_call" | custom-call | tf_op jit(solution)/shard_map/pallas_call | solution.py:315
  46.9 6.2 %all-to-all-start.1 = ((bf16[128,4,128]{2,1,0:T(4,128)(2,1)}), bf16[128,4,128]{2,1,0:T(4,128)(2,1)S(1)}, u32[]{:S(2)}, u32[]{:S(2)}) async-start(bf16[128,4,128]{2,1,0:T(4,128)(2,1)} %shard_map.153.after), calls=%async_computation.1 | async-start | bytes 262144 | tf_op jit(solution)/shard_map/all_to_all | solution.py:504
  53.2 0.0 copy-done.3
  53.2 0.1 shard_map.154.mix
  53.3 10.0 %all-to-all-done.1 = bf16[128,4,128]{2,1,0:T(4,128)(2,1)S(1)} async-done(((bf16[128,4,128]{2,1,0:T(4,128)(2,1)}), bf16[128,4,128]{2,1,0:T(4,128)(2,1)S(1)}, u32[]{:S(2)}, u32[]{:S(2)}) %all-to-all-start.1) | async-done | bytes 131104 | tf_op jit(solution)/shard_map/all_to_all | solution.py:504
  63.3 0.7 %shard_map.155 = bf16[4,256]{1,0:T(4,128)(2,1)} custom-call(bf16[512,128]{1,0:T(8,128)(2,1)S(1)} %bitcast.18, bf16[16,512]{1,0:T(8,128)(2,1)S(1)} %shard_map.154.mix, f32[4,256]{1,0:T(4,128)S(1)} %get-tuple-element.12.own), custom_call_target="tpu_custom_call" | custom-call | tf_op jit(solution)/shard_map/pallas_call | solution.py:439
  (3 shorter events, 0.1 us)
Async XLA Ops:
  15.2 6.2 %collective-permute-start.2 = (bf16[4,4096]{1,0:T(4,128)(2,1)S(1)}, bf16[4,4096]{1,0:T(4,128)(2,1)S(1)}, u32[]{:S(2)}, u32[]{:S(2)}) collective-permute-start(bf16[4,4096]{1,0:T(4,128)(2,1)S(1)} %shard_map.146.refs_0_.p0), channel_id=1, source_target_pairs={{0,24},{8,16},{16,8},{24,0},{32,56},{40,48},{48,40},{56,32},{64,88... | collective-permute-start | bytes 98312 | tf_op jit(solution)/shard_map/ppermute | solution.py:449
  17.0 4.4 %collective-permute-start.1 = (bf16[4,4096]{1,0:T(4,128)(2,1)S(1)}, bf16[4,4096]{1,0:T(4,128)(2,1)S(1)}, u32[]{:S(2)}, u32[]{:S(2)}) collective-permute-start(bf16[4,4096]{1,0:T(4,128)(2,1)S(1)} %shard_map.146.refs_0_.p0), channel_id=1, source_target_pairs={{0,16},{8,24},{16,0},{24,8},{32,48},{40,56},{48,32},{56,40},{64,80... | collective-permute-start | bytes 98312 | tf_op jit(solution)/shard_map/ppermute | solution.py:449
  17.4 4.3 %collective-permute-start = (bf16[4,4096]{1,0:T(4,128)(2,1)S(1)}, bf16[4,4096]{1,0:T(4,128)(2,1)S(1)}, u32[]{:S(2)}, u32[]{:S(2)}) collective-permute-start(bf16[4,4096]{1,0:T(4,128)(2,1)S(1)} %shard_map.146.refs_0_.p0), channel_id=1, source_target_pairs={{0,8},{8,0},{16,24},{24,16},{32,40},{40,32},{48,56},{56,48},{64,72... | collective-permute-start | bytes 98312 | tf_op jit(solution)/shard_map/ppermute | solution.py:449
  21.8 5.6 %copy-start = (bf16[4,4096]{1,0:T(4,128)(2,1)S(1)}, bf16[4,4096]{1,0:T(4,128)(2,1)}, u32[]{:S(2)}) copy-start(bf16[4,4096]{1,0:T(4,128)(2,1)} %residual.1) | copy-start | bytes 98308
  21.8 5.6 %copy-start.1 = (f32[4096]{0:T(1024)S(1)}, f32[4096]{0:T(1024)}, u32[]{:S(2)}) copy-start(f32[4096]{0:T(1024)} %param.25) | copy-start | bytes 49156
  21.8 5.6 %copy-start.2 = (s32[4,8]{1,0:T(4,128)S(1)}, s32[4,8]{1,0:T(4,128)}, u32[]{:S(2)}) copy-start(s32[4,8]{1,0:T(4,128)} %ids.3) | copy-start | bytes 388
  21.8 5.6 %collective-permute-start.5 = (bf16[4,4096]{1,0:T(4,128)(2,1)S(1)}, bf16[4,4096]{1,0:T(4,128)(2,1)S(1)}, u32[]{:S(2)}, u32[]{:S(2)}) collective-permute-start(bf16[4,4096]{1,0:T(4,128)(2,1)S(1)} %shard_map.148.refs_0_.p0), channel_id=1, source_target_pairs={{0,96},{8,104},{16,112},{24,120},{32,64},{40,72},{48,80},{56,88},{... | collective-permute-start | bytes 98312 | tf_op jit(solution)/shard_map/ppermute | solution.py:449
  22.8 4.6 %collective-permute-start.4 = (bf16[4,4096]{1,0:T(4,128)(2,1)S(1)}, bf16[4,4096]{1,0:T(4,128)(2,1)S(1)}, u32[]{:S(2)}, u32[]{:S(2)}) collective-permute-start(bf16[4,4096]{1,0:T(4,128)(2,1)S(1)} %shard_map.148.refs_0_.p0), channel_id=1, source_target_pairs={{0,64},{8,72},{16,80},{24,88},{32,96},{40,104},{48,112},{56,120},{... | collective-permute-start | bytes 98312 | tf_op jit(solution)/shard_map/ppermute | solution.py:449
  23.9 3.4 %collective-permute-start.3 = (bf16[4,4096]{1,0:T(4,128)(2,1)S(1)}, bf16[4,4096]{1,0:T(4,128)(2,1)S(1)}, u32[]{:S(2)}, u32[]{:S(2)}) collective-permute-start(bf16[4,4096]{1,0:T(4,128)(2,1)S(1)} %shard_map.148.refs_0_.p0), channel_id=1, source_target_pairs={{0,32},{8,40},{16,48},{24,56},{32,0},{40,8},{48,16},{56,24},{64,96... | collective-permute-start | bytes 98312 | tf_op jit(solution)/shard_map/ppermute | solution.py:449
  27.6 14.5 %slice-start = ((s8[6291456]{0:T(1024)(128)(4,1)}), s8[4194304]{0:T(1024)(128)(4,1)S(1)}, s32[]{:S(2)}) async-start(s8[6291456]{0:T(1024)(128)(4,1)} %bitcast.16), calls=%async_computation.2 | async-start | bytes 8388608
  27.6 14.5 %slice-start.1 = ((s8[6291456]{0:T(1024)(128)(4,1)}), s8[2097152]{0:T(1024)(128)(4,1)S(1)}, s32[]{:S(2)}) async-start(s8[6291456]{0:T(1024)(128)(4,1)} %bitcast.16), calls=%async_computation.3 | async-start | bytes 4194304
  27.7 5.7 %collective-permute-start.8 = (bf16[4,4224]{1,0:T(4,128)(2,1)S(1)}, bf16[4,4224]{1,0:T(4,128)(2,1)S(1)}, u32[]{:S(2)}, u32[]{:S(2)}) collective-permute-start(bf16[4,4224]{1,0:T(4,128)(2,1)S(1)} %get-tuple-element.11.refs_0_.p0), channel_id=1, source_target_pairs={{0,6},{1,7},{2,4},{3,5},{4,2},{5,3},{6,0},{7,1},{8,14},{9,15},{10,... | collective-permute-start | bytes 101384 | tf_op jit(solution)/shard_map/ppermute | solution.py:449
  30.5 4.3 %collective-permute-start.7 = (bf16[4,4224]{1,0:T(4,128)(2,1)S(1)}, bf16[4,4224]{1,0:T(4,128)(2,1)S(1)}, u32[]{:S(2)}, u32[]{:S(2)}) collective-permute-start(bf16[4,4224]{1,0:T(4,128)(2,1)S(1)} %get-tuple-element.11.refs_0_.p0), channel_id=1, source_target_pairs={{0,4},{1,5},{2,6},{3,7},{4,0},{5,1},{6,2},{7,3},{8,12},{9,13},{10,... | collective-permute-start | bytes 101384 | tf_op jit(solution)/shard_map/ppermute | solution.py:449
  30.8 3.9 %collective-permute-start.6 = (bf16[4,4224]{1,0:T(4,128)(2,1)S(1)}, bf16[4,4224]{1,0:T(4,128)(2,1)S(1)}, u32[]{:S(2)}, u32[]{:S(2)}) collective-permute-start(bf16[4,4224]{1,0:T(4,128)(2,1)S(1)} %get-tuple-element.11.refs_0_.p0), channel_id=1, source_target_pairs={{0,2},{1,3},{2,0},{3,1},{4,6},{5,7},{6,4},{7,5},{8,10},{9,11},{10,... | collective-permute-start | bytes 101384 | tf_op jit(solution)/shard_map/ppermute | solution.py:449
  34.8 18.4 %copy-start.3 = (f32[4,8]{1,0:T(4,128)S(1)}, f32[4,8]{1,0:T(4,128)}, u32[]{:S(2)}) copy-start(f32[4,8]{1,0:T(4,128)} %gates.1) | copy-start | bytes 388
  34.8 7.4 %collective-permute-start.9 = (bf16[16,4224]{1,0:T(8,128)(2,1)S(1)}, bf16[16,4224]{1,0:T(8,128)(2,1)S(1)}, u32[]{:S(2)}, u32[]{:S(2)}) collective-permute-start(bf16[16,4224]{1,0:T(8,128)(2,1)S(1)} %shard_map.152.x0), channel_id=1, source_target_pairs={{0,1},{1,0},{2,3},{3,2},{4,5},{5,4},{6,7},{7,6},{8,9},{9,8},{10,11... | collective-permute-start | bytes 405512 | tf_op jit(solution)/shard_map/ppermute | solution.py:449
  46.9 16.4 %all-to-all-start.1 = ((bf16[128,4,128]{2,1,0:T(4,128)(2,1)}), bf16[128,4,128]{2,1,0:T(4,128)(2,1)S(1)}, u32[]{:S(2)}, u32[]{:S(2)}) async-start(bf16[128,4,128]{2,1,0:T(4,128)(2,1)} %shard_map.153.after), calls=%async_computation.1 | async-start | bytes 262144 | tf_op jit(solution)/shard_map/all_to_all | solution.py:504

commit v5 on v4

--- a/solution.py
+++ b/solution.py
@@ -17,6 +17,20 @@
 
 def in_hbm(value):
     return pltpu.with_memory_space_constraint(value, pltpu.HBM)
+
+
+def tile_copies(source, first, out, sem):
+    chunks = sem.shape[1]
+    part = source.shape[1] // chunks
+    return [
+        pltpu.make_async_copy(
+            source.at[0, pl.ds(c * part, part), :, pl.ds((first + t) * 128, 128)],
+            out.at[t, pl.ds(c * part, part)],
+            sem.at[t, c],
+        )
+        for c in range(chunks)
+        for t in range(out.shape[0])
+    ]
 
 
 def attention_kernel(
@@ -58,7 +72,7 @@
     small = [
         pltpu.make_async_copy(source, held, small_sem.at[i]) for i, (source, held) in enumerate(pairs)
     ]
-    for copy in small[:6]:
+    for copy in small:
         copy.start()
     small[0].wait()
     picked = ([], [])
@@ -76,7 +90,6 @@
                     )
                     copy.start()
                     picked[which].append(copy)
-    small[6].start()
     for copy in small[1:4] + picked[0]:
         copy.wait()
     rows = keys.shape[1]
@@ -199,18 +212,7 @@
 
 def fetch_kernel(first, source, *refs):
     out, sem = refs[-2:]
-    count = out.shape[0]
-    chunks = 4
-    part = source.shape[1] // chunks
-    copies = [
-        pltpu.make_async_copy(
-            source.at[0, pl.ds(c * part, part), :, pl.ds((first + t) * 128, 128)],
-            out.at[t, pl.ds(c * part, part)],
-            sem.at[t, c],
-        )
-        for c in range(chunks)
-        for t in range(count)
-    ]
+    copies = tile_copies(source, first, out, sem)
     for copy in copies:
         copy.start()
     for copy in copies:
@@ -233,10 +235,41 @@
     return tiles.reshape(count, 2 * depth, 128)
 
 
-def experts_kernel(order, x0, x1, *refs):
-    *tiles, down, out, spread = refs
+def spread_rows(x, model_dim, spread):
+    rows = x.shape[0]
+    source = lax.broadcasted_iota(jnp.int32, (128, 512), 0)
+    target = lax.broadcasted_iota(jnp.int32, (128, 512), 1)
+    ends = (target == 2 * source) | (target == 2 * source + 257)
+    to_both = jnp.where(ends, 1.0, 0.0).astype(jnp.bfloat16)
+    pieces = [x[:, j * 128 : (j + 1) * 128] for j in range(model_dim // 128)]
+    result = jnp.dot(
+        jnp.concatenate(pieces, axis=0), to_both, preferred_element_type=jnp.float32
+    ).astype(jnp.bfloat16)
+    for j in range(model_dim // 128):
+        columns = slice(j * 256, (j + 1) * 256)
+        spread[0:rows, columns] = result[j * rows : (j + 1) * rows, 0:256]
+        spread[rows : 2 * rows, columns] = result[j * rows : (j + 1) * rows, 256:512]
+
+
+def spread_kernel(x, spread):
+    spread_rows(x, spread.shape[1] // 2, spread)
+
+
+def spread_alone(x, model_dim):
+    return pl.pallas_call(
+        spread_kernel,
+        out_shape=pltpu.VMEM((2 * x.shape[0], 2 * model_dim), x.dtype),
+        in_specs=[VMEM_SPEC],
+        out_specs=VMEM_SPEC,
+        compiler_params=pltpu.CompilerParams(vmem_limit_bytes=4 << 20),
+        cost_estimate=pl.CostEstimate(flops=0, bytes_accessed=1 << 20, transcendentals=0),
+    )(x)
+
+
+def experts_kernel(order, x0, x1, first, *refs):
+    *tiles, down, out, second = refs
     half = x0.shape[0]
-    model_dim = spread.shape[1] // 2
+    model_dim = second.shape[1] // 2
     rows = 2 * half
     blocks = len(order)
     seq_count = rows // blocks
@@ -245,36 +278,12 @@
     names = jnp.concatenate([x0[:, model_dim:], x1[:, model_dim:]], axis=0).astype(jnp.float32)
     lane = lax.broadcasted_iota(jnp.int32, names.shape, 1)
     here = lax.axis_index("ctx") * blocks + exp_pos
-    named = jnp.sum(jnp.where(lane == here, names, 0.0), axis=-1, keepdims=True)
-    row = lax.broadcasted_iota(jnp.int32, (rows, rows), 0)
-    col = lax.broadcasted_iota(jnp.int32, (rows, rows), 1)
-    earlier = (row // seq_count == col // seq_count) & (row < col)
-    ones = jnp.ones((blocks * slots, rows), jnp.bfloat16)
-    by_column = jnp.dot(
-        ones, jnp.where(row == col, named, 0.0).astype(jnp.bfloat16), preferred_element_type=jnp.float32
-    )
-    rank = jnp.dot(
-        ones, jnp.where(earlier, named, 0.0).astype(jnp.bfloat16), preferred_element_type=jnp.float32
-    )
-    slot = lax.broadcasted_iota(jnp.int32, by_column.shape, 0)
-    member = lax.broadcasted_iota(jnp.int32, by_column.shape, 1)
-    chosen = (by_column > 0.5) & (slot // slots == member // seq_count)
-    chosen = chosen & (jnp.abs(rank - (slot % slots).astype(jnp.float32)) < 0.5)
-    chosen = jnp.where(chosen, 1.0, 0.0).astype(jnp.bfloat16)
-    source = lax.broadcasted_iota(jnp.int32, (128, 512), 0)
-    target = lax.broadcasted_iota(jnp.int32, (128, 512), 1)
-    ends = (target == 2 * source) | (target == 2 * source + 257)
-    to_both = jnp.where(ends, 1.0, 0.0).astype(jnp.bfloat16)
-    pieces = []
-    for j in range(model_dim // 128):
-        pieces += [x[:, j * 128 : (j + 1) * 128] for x in (x0, x1)]
-    result = jnp.dot(
-        jnp.concatenate(pieces, axis=0), to_both, preferred_element_type=jnp.float32
-    ).astype(jnp.bfloat16)
-    for j in range(model_dim // 128):
-        columns = slice(j * 256, (j + 1) * 256)
-        spread[0:rows, columns] = result[j * rows : (j + 1) * rows, 0:256]
-        spread[rows : 2 * rows, columns] = result[j * rows : (j + 1) * rows, 256:512]
+    code = jnp.sum(jnp.where(lane == here, names, 0.0), axis=-1, keepdims=True)
+    row = lax.broadcasted_iota(jnp.int32, names.shape, 0)
+    place = row // seq_count * slots + code.astype(jnp.int32) - 1
+    chosen = jnp.where((code > 0.5) & (place == lane), 1.0, 0.0)
+    chosen = chosen.T[: blocks * slots].astype(jnp.bfloat16)
+    spread_rows(x1, model_dim, second)
     lanes = [tile.at[t] for tile in tiles for t in range(tile.shape[0])]
     depth = 1024
     both = []
@@ -283,13 +292,15 @@
         for c in range(2 * model_dim // depth):
             here = slice(c * depth, (c + 1) * depth)
             right = jnp.concatenate([lanes[2 * u][here, :], lanes[2 * u + 1][here, :]], axis=1)
-            total = total + jnp.dot(spread[:, here], right, preferred_element_type=jnp.float32)
+            left = jnp.concatenate([first[:, here], second[:, here]], axis=0)
+            total = total + jnp.dot(left, right, preferred_element_type=jnp.float32)
         both.append(total)
     both = jnp.concatenate(both, axis=1)
-    gate, up = both[:rows], both[rows:]
+    gate = jnp.concatenate([both[0:half], both[rows : rows + half]], axis=0)
+    up = jnp.concatenate([both[half:rows], both[rows + half :]], axis=0)
     activated = (jax.nn.silu(gate) * up).astype(jnp.bfloat16)
     activated = jnp.dot(chosen, activated, preferred_element_type=jnp.float32).astype(jnp.bfloat16)
-    width = 1024
+    width = 2048
 
     def down_part(b, carry):
         columns = pl.ds(pl.multiple_of(b * width, width), width)
@@ -315,11 +326,11 @@
     return pl.pallas_call(
         functools.partial(experts_kernel, order),
         out_shape=pltpu.VMEM((model_dim // 256 * blocks, 2 * slots, 128), jnp.bfloat16),
-        in_specs=[VMEM_SPEC] * (3 + len(tiles)),
-        out_specs=VMEM_SPEC,
-        scratch_shapes=[pltpu.VMEM((2 * rows, 2 * model_dim), jnp.bfloat16)],
+        in_specs=[VMEM_SPEC] * (4 + len(tiles)),
+        out_specs=VMEM_SPEC,
+        scratch_shapes=[pltpu.VMEM((rows, 2 * model_dim), jnp.bfloat16)],
         compiler_params=pltpu.CompilerParams(vmem_limit_bytes=16 << 20),
-    )(*pieces, *tiles, down)
+    )(*pieces, spread_alone(pieces[0], model_dim), *tiles, down)
 
 
 def sum_kernel(p0, p1, p2, p3, before, out):
@@ -351,7 +362,10 @@
     names = jnp.zeros(lane.shape, jnp.float32)
     for k in range(ids.shape[1]):
         names = jnp.where(ids[:, k : k + 1] == lane, 1.0, names)
-    normed[:, model_dim:] = names.astype(normed.dtype)
+    slot = [names[0:1]]
+    for r in range(1, seq_count):
+        slot.append(slot[-1] + names[r : r + 1])
+    normed[:, model_dim:] = (names * jnp.concatenate(slot, axis=0)).astype(normed.dtype)
     place = lax.axis_index("ctx") * kvh_devices + lax.axis_index("kvh")
     width = own.shape[1]
     for p in range(model_dim // width):
@@ -487,19 +501,19 @@
     projected = project(parts, out_weight)
 
     axes = ("ctx", "kvh")
-    along_x = [projected] + [swapped(projected, axes, plane, m) for m in (1, 2, 3)]
+    along_x = [projected] + [swapped(projected, axes, plane, m) for m in (2, 3, 1)]
     tiles = [fetch(w_gate_up, 0, 2, projected)]
-    sums = sum_pieces(along_x, tiles[0])
-    along_z = [sums] + [swapped(sums, axes, plane, m) for m in range(4, plane, 4)]
+    sums = sum_pieces(along_x, tiles[-1])
+    along_z = [sums] + [swapped(sums, axes, plane, m) for m in (4, 12, 8)]
     tiles.append(fetch(w_gate_up, 2, 2, sums))
-    own, normed = norm(along_z, residual, norm_gain, expert_ids, tiles[1], kvh_devices)
-
-    steps = range(0, exp_devices, 2)
+    own, normed = norm(along_z, residual, norm_gain, expert_ids, tiles[-1], kvh_devices)
+
+    steps = (0, 2, 6, 4)
     along_y = [normed] + [swapped(normed, "exp", exp_devices, m) for m in steps[1:]]
     tiles.append(fetch(w_gate_up, 4, 2, normed))
-    mine = stack(along_y, tiles[2])
+    mine = stack(along_y, tiles[-1])
     other = swapped(mine, "exp", exp_devices, 1)
-    order = tuple(steps) + tuple(m + 1 for m in steps)
+    order = steps + tuple(m + 1 for m in steps)
     results = experts((mine, other), tiles, w_down, order, ROW_SLOTS)
     returned = lax.all_to_all(
         results, ("ctx", "kvh", "exp"), split_axis=0, concat_axis=0, tiled=True

time: 64.3 us -> 63.3 us (0.984)
  starting transfers between devices: 23.3 us -> 21.3 us
  waiting for transfers between devices: 12.7 us -> 13.8 us
    ppermute x10, starting transfers between devices: 17.1 us -> 15.9 us  [swapped(): return lax.ppermute(value, axes, [(i, i ^ mask) for i in range(count)])]
    ppermute x10, waiting for transfers between devices: 2.7 us -> 3.8 us  [swapped(): return lax.ppermute(value, axes, [(i, i ^ mask) for i in range(count)])]
    all_to_all x1, starting transfers between devices: 6.2 us -> 5.4 us  [body(): lax.all_to_all(results, ('ctx', 'kvh', 'exp'), split_axis=0, concat_axis=...]
  transfers between devices with their start and end apart: 11 -> 11, of which waited for: 4 -> 5; matrix products, arithmetic and copies ran while one was open for 0% -> 0% of each run, Pallas kernels for 11% -> 11%
where the time goes in v5:
time: 63.3 us; the launch traced here: 63.1 us
  starting transfers between devices  21.3 us (34%)
  Pallas kernels  15.9 us (25%)
  waiting for transfers between devices  13.8 us (22%)
  blocking collectives  11.8 us (19%)
    ppermute x10, starting transfers between devices, swapped(): return lax.ppermute(value, axes, [(i, i ^ mask) for i in range(count)])  15.9 us
    all_to_all x1, blocking collectives, body(): lax.all_to_all(parts, 'ctx', split_axis=0, concat_axis=0, tiled=True)  11.8 us
    all_to_all x1, waiting for transfers between devices, body(): lax.all_to_all(results, ('ctx', 'kvh', 'exp'), split_axis=0, concat_axis=...  10 us
    pallas_call x3, Pallas kernels, fetch(): pl.pallas_call(functools.partial(fetch_kernel, first), out_shape=pltpu.VM...  6.64 us
    all_to_all x1, starting transfers between devices, body(): lax.all_to_all(results, ('ctx', 'kvh', 'exp'), split_axis=0, concat_axis=...  5.4 us
    pallas_call x1, Pallas kernels, experts(): pl.pallas_call(functools.partial(experts_kernel, order), out_shape=pltpu....  4.51 us
    ppermute x10, waiting for transfers between devices, swapped(): return lax.ppermute(value, axes, [(i, i ^ mask) for i in range(count)])  3.8 us
    pallas_call x1, Pallas kernels, attention(): pl.pallas_call(attention_kernel, out_shape=(pltpu.VMEM((query_count, 2 *...  2.82 us
  transfers between devices with their start and end apart: 11, of which 5 were waited for; matrix products, arithmetic and copies ran while one was open for 0% of the time, Pallas kernels for 11%

profile of v5, /device:TPU:1, one launch (start us, length us, event | category | flops | bytes accessed | tf_op | source)
XLA Modules:
  0.0 63.1 jit_solution(16665518453039585651)
XLA Ops:
  0.0 2.8 %shard_map.145 = (f32[8,16,128]{2,1,0:T(8,128)S(1)}, bf16[2,1,128,4096]{3,2,1,0:T(8,128)(2,1)S(1)}) custom-call(s32[2,2,4]{2,1,0:T(2,128)} %bitcast.24, bf16[4,2,8,128]{3,2,1,0:T(8,128)(2,1)} %queries_in.1, bf16[4,2,128]{2,1,0:T(2,128)(2,1)} %new_key_in.1, bf16[4,2,128]{2,1,0:T(2,128)(2,1)} %new_value_in.1, bf16[4,128,128]{2,1,0:T(8,128)(2,1)} %bitcast.22, ...), custom_call_target="tpu_custom_call" | custom-call | tf_op jit(solution)/shard_map/pallas_call | solution.py:159
  2.8 11.8 %all_to_all.10.parts = f32[8,16,128]{2,1,0:T(8,128)S(1)} all-to-all(f32[8,16,128]{2,1,0:T(8,128)S(1)} %get-tuple-element.9), channel_id=1, replica_groups=mesh['ctx'=8,'kvh'=2,'exp'=8] {'ctx'}, dimensions={0} | all-to-all | bytes 131072 | tf_op jit(solution)/shard_map/all_to_all | solution.py:499
  14.6 0.5 shard_map.146.refs_0_.p0
  15.1 2.5 %collective-permute-start.2 = (bf16[4,4096]{1,0:T(4,128)(2,1)S(1)}, bf16[4,4096]{1,0:T(4,128)(2,1)S(1)}, u32[]{:S(2)}, u32[]{:S(2)}) collective-permute-start(bf16[4,4096]{1,0:T(4,128)(2,1)S(1)} %shard_map.146.refs_0_.p0), channel_id=1, source_target_pairs={{0,8},{8,0},{16,24},{24,16},{32,40},{40,32},{48,56},{56,48},{64,72... | collective-permute-start | bytes 98312 | tf_op jit(solution)/shard_map/ppermute | solution.py:463
  17.7 0.4 collective-permute-start.1
  18.1 0.0 collective-permute-start
  18.1 2.2 %shard_map.147 = bf16[2,4096,2,128]{3,2,1,0:T(2,128)(2,1)S(1)} custom-call(bf16[1,4096,2,768]{3,2,1,0:T(2,128)(2,1)} %source.5, bf16[4,4096]{1,0:T(4,128)(2,1)S(1)} %shard_map.146.refs_0_.p0), custom_call_target="tpu_custom_call" | custom-call | bytes 4194304 | tf_op jit(solution)/shard_map/pallas_call | solution.py:224
  20.3 0.0 collective-permute-done.2.p3
  20.3 1.6 %collective-permute-done.1.p2 = bf16[4,4096]{1,0:T(4,128)(2,1)S(1)} collective-permute-done((bf16[4,4096]{1,0:T(4,128)(2,1)S(1)}, bf16[4,4096]{1,0:T(4,128)(2,1)S(1)}, u32[]{:S(2)}, u32[]{:S(2)}) %collective-permute-start.1) | collective-permute-done | bytes 32800 | tf_op jit(solution)/shard_map/ppermute | solution.py:463
  21.9 0.0 collective-permute-done.p1
  22.0 0.0 copy-start
  22.0 0.0 copy-start.1
  22.0 0.0 copy-start.2
  22.0 1.1 %collective-permute-start.5 = (bf16[4,4096]{1,0:T(4,128)(2,1)S(1)}, bf16[4,4096]{1,0:T(4,128)(2,1)S(1)}, u32[]{:S(2)}, u32[]{:S(2)}) collective-permute-start(bf16[4,4096]{1,0:T(4,128)(2,1)S(1)} %shard_map.148.refs_0_.p0), channel_id=1, source_target_pairs={{0,64},{8,72},{16,80},{24,88},{32,96},{40,104},{48,112},{56,120},{... | collective-permute-start | bytes 98312 | tf_op jit(solution)/shard_map/ppermute | solution.py:463
  23.1 1.7 %collective-permute-start.4 = (bf16[4,4096]{1,0:T(4,128)(2,1)S(1)}, bf16[4,4096]{1,0:T(4,128)(2,1)S(1)}, u32[]{:S(2)}, u32[]{:S(2)}) collective-permute-start(bf16[4,4096]{1,0:T(4,128)(2,1)S(1)} %shard_map.148.refs_0_.p0), channel_id=1, source_target_pairs={{0,96},{8,104},{16,112},{24,120},{32,64},{40,72},{48,80},{56,88},{... | collective-permute-start | bytes 98312 | tf_op jit(solution)/shard_map/ppermute | solution.py:463
  24.8 0.0 collective-permute-start.3
  24.8 2.2 %shard_map.149 = bf16[2,4096,2,128]{3,2,1,0:T(2,128)(2,1)S(1)} custom-call(bf16[1,4096,2,768]{3,2,1,0:T(2,128)(2,1)} %source.5, bf16[4,4096]{1,0:T(4,128)(2,1)S(1)} %shard_map.148.refs_0_.p0), custom_call_target="tpu_custom_call" | custom-call | bytes 4194304 | tf_op jit(solution)/shard_map/pallas_call | solution.py:224
  27.0 0.0 collective-permute-done.5.p3
  27.0 0.0 collective-permute-done.4.p2
  27.0 0.5 collective-permute-done.3.p1
  27.5 0.0 copy-done
  27.5 0.0 copy-done.1
  27.5 0.0 copy-done.2
  27.5 0.2 shard_map.150
  27.8 0.0 slice-start
  27.8 0.0 slice-start.1
  27.8 3.0 %collective-permute-start.8 = (bf16[4,4224]{1,0:T(4,128)(2,1)S(1)}, bf16[4,4224]{1,0:T(4,128)(2,1)S(1)}, u32[]{:S(2)}, u32[]{:S(2)}) collective-permute-start(bf16[4,4224]{1,0:T(4,128)(2,1)S(1)} %get-tuple-element.11.refs_0_.p0), channel_id=1, source_target_pairs={{0,4},{1,5},{2,6},{3,7},{4,0},{5,1},{6,2},{7,3},{8,12},{9,13},{10,... | collective-permute-start | bytes 101384 | tf_op jit(solution)/shard_map/ppermute | solution.py:463
  30.8 0.8 %collective-permute-start.7 = (bf16[4,4224]{1,0:T(4,128)(2,1)S(1)}, bf16[4,4224]{1,0:T(4,128)(2,1)S(1)}, u32[]{:S(2)}, u32[]{:S(2)}) collective-permute-start(bf16[4,4224]{1,0:T(4,128)(2,1)S(1)} %get-tuple-element.11.refs_0_.p0), channel_id=1, source_target_pairs={{0,6},{1,7},{2,4},{3,5},{4,2},{5,3},{6,0},{7,1},{8,14},{9,15},{10,... | collective-permute-start | bytes 101384 | tf_op jit(solution)/shard_map/ppermute | solution.py:463
  31.6 0.0 collective-permute-start.6
  31.6 2.2 %shard_map.151 = bf16[2,4096,2,128]{3,2,1,0:T(2,128)(2,1)S(1)} custom-call(bf16[1,4096,2,768]{3,2,1,0:T(2,128)(2,1)} %source.5, bf16[4,4224]{1,0:T(4,128)(2,1)S(1)} %get-tuple-element.11.refs_0_.p0), custom_call_target="tpu_custom_call" | custom-call | bytes 4194304 | tf_op jit(solution)/shard_map/pallas_call | solution.py:224
  33.8 0.0 collective-permute-done.8.p3
  33.8 1.0 %collective-permute-done.7.p2 = bf16[4,4224]{1,0:T(4,128)(2,1)S(1)} collective-permute-done((bf16[4,4224]{1,0:T(4,128)(2,1)S(1)}, bf16[4,4224]{1,0:T(4,128)(2,1)S(1)}, u32[]{:S(2)}, u32[]{:S(2)}) %collective-permute-start.7) | collective-permute-done | bytes 33824 | tf_op jit(solution)/shard_map/ppermute | solution.py:463
  34.8 0.0 collective-permute-done.6.p1
  34.8 6.5 %collective-permute-start.9 = (bf16[16,4224]{1,0:T(8,128)(2,1)S(1)}, bf16[16,4224]{1,0:T(8,128)(2,1)S(1)}, u32[]{:S(2)}, u32[]{:S(2)}) collective-permute-start(bf16[16,4224]{1,0:T(8,128)(2,1)S(1)} %shard_map.152.x.x0), channel_id=1, source_target_pairs={{0,1},{1,0},{2,3},{3,2},{4,5},{5,4},{6,7},{7,6},{8,9},{9,8},{10,11... | collective-permute-start | bytes 405512 | tf_op jit(solution)/shard_map/ppermute | solution.py:463
  41.3 0.3 shard_map.153.first
  41.6 0.0 copy-start.3
  41.6 0.7 %collective-permute-done.9.x1 = bf16[16,4224]{1,0:T(8,128)(2,1)S(1)} collective-permute-done((bf16[16,4224]{1,0:T(8,128)(2,1)S(1)}, bf16[16,4224]{1,0:T(8,128)(2,1)S(1)}, u32[]{:S(2)}, u32[]{:S(2)}) %collective-permute-start.9) | collective-permute-done | bytes 135200 | tf_op jit(solution)/shard_map/ppermute | solution.py:463
  42.3 0.0 slice-done
  42.3 0.0 slice-done.1
  42.3 4.5 %shard_map.154.after = bf16[128,4,128]{2,1,0:T(4,128)(2,1)} custom-call(bf16[16,4224]{1,0:T(8,128)(2,1)S(1)} %shard_map.152.x.x0, bf16[16,4224]{1,0:T(8,128)(2,1)S(1)} %collective-permute-done.9.x1, bf16[32,8192]{1,0:T(8,128)(2,1)S(1)} %shard_map.153.first, bf16[2,8192,128]{2,1,0:T(8,128)(2,1)S(1)} %bitcast.11, bf16[2,8192,128]{2,1,0:T(8,128)(2,1)S(1)} %bitcast.13, ...), custom_call_target="tpu_custom_call" | custom-call | tf_op jit(solution)/shard_map/pallas_call | solution.py:326
  46.8 5.4 %all-to-all-start.1 = ((bf16[128,4,128]{2,1,0:T(4,128)(2,1)}), bf16[128,4,128]{2,1,0:T(4,128)(2,1)S(1)}, u32[]{:S(2)}, u32[]{:S(2)}) async-start(bf16[128,4,128]{2,1,0:T(4,128)(2,1)} %shard_map.154.after), calls=%async_computation.1 | async-start | bytes 262144 | tf_op jit(solution)/shard_map/all_to_all | solution.py:518
  52.2 0.0 copy-done.3
  52.2 0.1 shard_map.155.mix
  52.3 10.0 %all-to-all-done.1 = bf16[128,4,128]{2,1,0:T(4,128)(2,1)S(1)} async-done(((bf16[128,4,128]{2,1,0:T(4,128)(2,1)}), bf16[128,4,128]{2,1,0:T(4,128)(2,1)S(1)}, u32[]{:S(2)}, u32[]{:S(2)}) %all-to-all-start.1) | async-done | bytes 131104 | tf_op jit(solution)/shard_map/all_to_all | solution.py:518
  62.3 0.7 %shard_map.156 = bf16[4,256]{1,0:T(4,128)(2,1)} custom-call(bf16[512,128]{1,0:T(8,128)(2,1)S(1)} %bitcast.18, bf16[16,512]{1,0:T(8,128)(2,1)S(1)} %shard_map.155.mix, f32[4,256]{1,0:T(4,128)S(1)} %get-tuple-element.12.own), custom_call_target="tpu_custom_call" | custom-call | tf_op jit(solution)/shard_map/pallas_call | solution.py:453
  (3 shorter events, 0.1 us)
Async XLA Ops:
  15.1 5.2 %collective-permute-start.2 = (bf16[4,4096]{1,0:T(4,128)(2,1)S(1)}, bf16[4,4096]{1,0:T(4,128)(2,1)S(1)}, u32[]{:S(2)}, u32[]{:S(2)}) collective-permute-start(bf16[4,4096]{1,0:T(4,128)(2,1)S(1)} %shard_map.146.refs_0_.p0), channel_id=1, source_target_pairs={{0,8},{8,0},{16,24},{24,16},{32,40},{40,32},{48,56},{56,48},{64,72... | collective-permute-start | bytes 98312 | tf_op jit(solution)/shard_map/ppermute | solution.py:463
  17.7 4.3 %collective-permute-start.1 = (bf16[4,4096]{1,0:T(4,128)(2,1)S(1)}, bf16[4,4096]{1,0:T(4,128)(2,1)S(1)}, u32[]{:S(2)}, u32[]{:S(2)}) collective-permute-start(bf16[4,4096]{1,0:T(4,128)(2,1)S(1)} %shard_map.146.refs_0_.p0), channel_id=1, source_target_pairs={{0,24},{8,16},{16,8},{24,0},{32,56},{40,48},{48,40},{56,32},{64,88... | collective-permute-start | bytes 98312 | tf_op jit(solution)/shard_map/ppermute | solution.py:463
  18.1 3.9 %collective-permute-start = (bf16[4,4096]{1,0:T(4,128)(2,1)S(1)}, bf16[4,4096]{1,0:T(4,128)(2,1)S(1)}, u32[]{:S(2)}, u32[]{:S(2)}) collective-permute-start(bf16[4,4096]{1,0:T(4,128)(2,1)S(1)} %shard_map.146.refs_0_.p0), channel_id=1, source_target_pairs={{0,16},{8,24},{16,0},{24,8},{32,48},{40,56},{48,32},{56,40},{64,80... | collective-permute-start | bytes 98312 | tf_op jit(solution)/shard_map/ppermute | solution.py:463
  22.0 5.6 %copy-start = (bf16[4,4096]{1,0:T(4,128)(2,1)S(1)}, bf16[4,4096]{1,0:T(4,128)(2,1)}, u32[]{:S(2)}) copy-start(bf16[4,4096]{1,0:T(4,128)(2,1)} %residual.1) | copy-start | bytes 98308
  22.0 5.6 %copy-start.1 = (f32[4096]{0:T(1024)S(1)}, f32[4096]{0:T(1024)}, u32[]{:S(2)}) copy-start(f32[4096]{0:T(1024)} %param.25) | copy-start | bytes 49156
  22.0 5.5 %copy-start.2 = (s32[4,8]{1,0:T(4,128)S(1)}, s32[4,8]{1,0:T(4,128)}, u32[]{:S(2)}) copy-start(s32[4,8]{1,0:T(4,128)} %ids.3) | copy-start | bytes 388
  22.0 5.0 %collective-permute-start.5 = (bf16[4,4096]{1,0:T(4,128)(2,1)S(1)}, bf16[4,4096]{1,0:T(4,128)(2,1)S(1)}, u32[]{:S(2)}, u32[]{:S(2)}) collective-permute-start(bf16[4,4096]{1,0:T(4,128)(2,1)S(1)} %shard_map.148.refs_0_.p0), channel_id=1, source_target_pairs={{0,64},{8,72},{16,80},{24,88},{32,96},{40,104},{48,112},{56,120},{... | collective-permute-start | bytes 98312 | tf_op jit(solution)/shard_map/ppermute | solution.py:463
  23.1 4.0 %collective-permute-start.4 = (bf16[4,4096]{1,0:T(4,128)(2,1)S(1)}, bf16[4,4096]{1,0:T(4,128)(2,1)S(1)}, u32[]{:S(2)}, u32[]{:S(2)}) collective-permute-start(bf16[4,4096]{1,0:T(4,128)(2,1)S(1)} %shard_map.148.refs_0_.p0), channel_id=1, source_target_pairs={{0,96},{8,104},{16,112},{24,120},{32,64},{40,72},{48,80},{56,88},{... | collective-permute-start | bytes 98312 | tf_op jit(solution)/shard_map/ppermute | solution.py:463
  24.8 2.8 %collective-permute-start.3 = (bf16[4,4096]{1,0:T(4,128)(2,1)S(1)}, bf16[4,4096]{1,0:T(4,128)(2,1)S(1)}, u32[]{:S(2)}, u32[]{:S(2)}) collective-permute-start(bf16[4,4096]{1,0:T(4,128)(2,1)S(1)} %shard_map.148.refs_0_.p0), channel_id=1, source_target_pairs={{0,32},{8,40},{16,48},{24,56},{32,0},{40,8},{48,16},{56,24},{64,96... | collective-permute-start | bytes 98312 | tf_op jit(solution)/shard_map/ppermute | solution.py:463
  27.8 14.5 %slice-start = ((s8[6291456]{0:T(1024)(128)(4,1)}), s8[4194304]{0:T(1024)(128)(4,1)S(1)}, s32[]{:S(2)}) async-start(s8[6291456]{0:T(1024)(128)(4,1)} %bitcast.16), calls=%async_computation.2 | async-start | bytes 8388608
  27.8 14.5 %slice-start.1 = ((s8[6291456]{0:T(1024)(128)(4,1)}), s8[2097152]{0:T(1024)(128)(4,1)S(1)}, s32[]{:S(2)}) async-start(s8[6291456]{0:T(1024)(128)(4,1)} %bitcast.16), calls=%async_computation.3 | async-start | bytes 4194304
  27.8 6.0 %collective-permute-start.8 = (bf16[4,4224]{1,0:T(4,128)(2,1)S(1)}, bf16[4,4224]{1,0:T(4,128)(2,1)S(1)}, u32[]{:S(2)}, u32[]{:S(2)}) collective-permute-start(bf16[4,4224]{1,0:T(4,128)(2,1)S(1)} %get-tuple-element.11.refs_0_.p0), channel_id=1, source_target_pairs={{0,4},{1,5},{2,6},{3,7},{4,0},{5,1},{6,2},{7,3},{8,12},{9,13},{10,... | collective-permute-start | bytes 101384 | tf_op jit(solution)/shard_map/ppermute | solution.py:463
  30.8 4.0 %collective-permute-start.7 = (bf16[4,4224]{1,0:T(4,128)(2,1)S(1)}, bf16[4,4224]{1,0:T(4,128)(2,1)S(1)}, u32[]{:S(2)}, u32[]{:S(2)}) collective-permute-start(bf16[4,4224]{1,0:T(4,128)(2,1)S(1)} %get-tuple-element.11.refs_0_.p0), channel_id=1, source_target_pairs={{0,6},{1,7},{2,4},{3,5},{4,2},{5,3},{6,0},{7,1},{8,14},{9,15},{10,... | collective-permute-start | bytes 101384 | tf_op jit(solution)/shard_map/ppermute | solution.py:463
  31.6 3.2 %collective-permute-start.6 = (bf16[4,4224]{1,0:T(4,128)(2,1)S(1)}, bf16[4,4224]{1,0:T(4,128)(2,1)S(1)}, u32[]{:S(2)}, u32[]{:S(2)}) collective-permute-start(bf16[4,4224]{1,0:T(4,128)(2,1)S(1)} %get-tuple-element.11.refs_0_.p0), channel_id=1, source_target_pairs={{0,2},{1,3},{2,0},{3,1},{4,6},{5,7},{6,4},{7,5},{8,10},{9,11},{10,... | collective-permute-start | bytes 101384 | tf_op jit(solution)/shard_map/ppermute | solution.py:463
  34.8 7.5 %collective-permute-start.9 = (bf16[16,4224]{1,0:T(8,128)(2,1)S(1)}, bf16[16,4224]{1,0:T(8,128)(2,1)S(1)}, u32[]{:S(2)}, u32[]{:S(2)}) collective-permute-start(bf16[16,4224]{1,0:T(8,128)(2,1)S(1)} %shard_map.152.x.x0), channel_id=1, source_target_pairs={{0,1},{1,0},{2,3},{3,2},{4,5},{5,4},{6,7},{7,6},{8,9},{9,8},{10,11... | collective-permute-start | bytes 405512 | tf_op jit(solution)/shard_map/ppermute | solution.py:463
  41.6 10.6 %copy-start.3 = (f32[4,8]{1,0:T(4,128)S(1)}, f32[4,8]{1,0:T(4,128)}, u32[]{:S(2)}) copy-start(f32[4,8]{1,0:T(4,128)} %gates.1) | copy-start | bytes 388
  46.8 15.6 %all-to-all-start.1 = ((bf16[128,4,128]{2,1,0:T(4,128)(2,1)}), bf16[128,4,128]{2,1,0:T(4,128)(2,1)S(1)}, u32[]{:S(2)}, u32[]{:S(2)}) async-start(bf16[128,4,128]{2,1,0:T(4,128)(2,1)} %shard_map.154.after), calls=%async_computation.1 | async-start | bytes 262144 | tf_op jit(solution)/shard_map/all_to_all | solution.py:518

commit v6 on v5

--- a/solution.py
+++ b/solution.py
@@ -90,34 +90,45 @@
                     )
                     copy.start()
                     picked[which].append(copy)
-    for copy in small[1:4] + picked[0]:
-        copy.wait()
-    rows = keys.shape[1]
     heads = heads_kv * query_count
-    shape = (seq_count * heads, rows)
-    head_of_query = lax.broadcasted_iota(jnp.int32, shape, 0) // query_count % heads_kv
-    column = lax.broadcasted_iota(jnp.int32, shape, 1)
-    head_of_block = (column - centroid_rows) // (sel_count * block_rows)
-    valid = (column % heads_kv == head_of_query) & (
-        (column < centroid_rows) | (head_of_block == head_of_query)
-    )
     score_scale = 1.0 / math.sqrt(head_dim)
-    scores, own = [], []
-    for s in range(seq_count):
-        scores.append(
+
+    def scored(first, count, valid):
+        part = [
             lax.dot_general(
                 queries[s].reshape(heads, head_dim),
-                keys[s],
+                keys[s, first : first + count],
                 (((1,), (1,)), ((), ())),
                 preferred_element_type=jnp.float32,
             )
-        )
+            for s in range(seq_count)
+        ]
+        return jnp.where(valid, jnp.concatenate(part, axis=0) * score_scale, MASKED)
+
+    picked_rows = keys.shape[1] - centroid_rows
+    shape = (seq_count * heads, centroid_rows)
+    head_of_query = lax.broadcasted_iota(jnp.int32, shape, 0) // query_count % heads_kv
+    same_head = lax.broadcasted_iota(jnp.int32, shape, 1) % heads_kv == head_of_query
+    shape = (seq_count * heads, picked_rows)
+    head_of_query = lax.broadcasted_iota(jnp.int32, shape, 0) // query_count % heads_kv
+    column = lax.broadcasted_iota(jnp.int32, shape, 1)
+    same_block = (column % heads_kv == head_of_query) & (
+        column // (sel_count * block_rows) == head_of_query
+    )
+    for copy in small[1:4]:
+        copy.wait()
+    own = []
+    for s in range(seq_count):
         products = queries[s].astype(jnp.float32) * new_key[s].astype(jnp.float32)[:, None, :]
         own.append(jnp.sum(products, axis=-1, keepdims=True).reshape(heads, 1))
-    scores = jnp.where(valid, jnp.concatenate(scores, axis=0) * score_scale, MASKED)
     own = jnp.where(ctx_pos == 0, jnp.concatenate(own, axis=0) * score_scale, MASKED)
-    peak = jnp.maximum(jnp.max(scores, axis=-1, keepdims=True), own)
-    probs = jnp.exp(scores - peak)
+    to_centroids = scored(0, centroid_rows, same_head)
+    peak = jnp.maximum(jnp.max(to_centroids, axis=-1, keepdims=True), own)
+    for copy in picked[0]:
+        copy.wait()
+    to_picked = scored(centroid_rows, picked_rows, same_block)
+    peak = jnp.maximum(jnp.max(to_picked, axis=-1, keepdims=True), peak)
+    probs = jnp.exp(jnp.concatenate([to_centroids, to_picked], axis=1) - peak)
     own_prob = jnp.exp(own - peak)
     total = jnp.sum(probs, axis=-1, keepdims=True) + own_prob
     probs = probs.astype(jnp.bfloat16)
@@ -188,22 +199,18 @@
     total = jnp.sum(total * scale, axis=0)
     attended = (jnp.sum(weighted * scale, axis=0) / total).astype(jnp.bfloat16)
     seq_count = out.shape[0]
-    sums = None
-    for g in range(weight.shape[0]):
-        term = jnp.dot(
-            attended[g * seq_count : (g + 1) * seq_count],
-            weight[g, 0],
-            preferred_element_type=jnp.float32,
-        )
-        sums = term if sums is None else sums + term
+    attended = jnp.concatenate(
+        [attended[first : first + seq_count] for first in range(0, rows, seq_count)], axis=1
+    )
+    sums = jnp.dot(attended, weight[...], preferred_element_type=jnp.float32)
     out[...] = sums.astype(jnp.bfloat16)
 
 
 def project(parts, weight):
-    seq_count = parts.shape[1] // (2 * weight.shape[0])
+    seq_count = parts.shape[1] * parts.shape[2] // (2 * weight.shape[0])
     return pl.pallas_call(
         project_kernel,
-        out_shape=jax.ShapeDtypeStruct((seq_count, weight.shape[3]), jnp.bfloat16),
+        out_shape=jax.ShapeDtypeStruct((seq_count, weight.shape[1]), jnp.bfloat16),
         in_specs=[VMEM_SPEC, VMEM_SPEC],
         out_specs=VMEM_SPEC,
         compiler_params=pltpu.CompilerParams(vmem_limit_bytes=8 << 20),
@@ -494,7 +501,7 @@
         selected,
         new_key,
         new_value,
-        out_weight,
+        out_weight.reshape(-1, out_weight.shape[3]),
     )
     parts = lax.all_to_all(parts, "ctx", split_axis=0, concat_axis=0, tiled=True)
 

time: 63.3 us -> 63.2 us (level)
  no operation moved by 1% of the time
where the time goes in v6:
time: 63.2 us; the launch traced here: 63 us
  starting transfers between devices  21.3 us (34%)
  Pallas kernels  15.9 us (25%)
  waiting for transfers between devices  13.8 us (22%)
  blocking collectives  11.8 us (19%)
    ppermute x10, starting transfers between devices, swapped(): return lax.ppermute(value, axes, [(i, i ^ mask) for i in range(count)])  15.9 us
    all_to_all x1, blocking collectives, body(): lax.all_to_all(parts, 'ctx', split_axis=0, concat_axis=0, tiled=True)  11.8 us
    all_to_all x1, waiting for transfers between devices, body(): lax.all_to_all(results, ('ctx', 'kvh', 'exp'), split_axis=0, concat_axis=...  10 us
    pallas_call x3, Pallas kernels, fetch(): pl.pallas_call(functools.partial(fetch_kernel, first), out_shape=pltpu.VM...  6.64 us
    all_to_all x1, starting transfers between devices, body(): lax.all_to_all(results, ('ctx', 'kvh', 'exp'), split_axis=0, concat_axis=...  5.4 us
    pallas_call x1, Pallas kernels, experts(): pl.pallas_call(functools.partial(experts_kernel, order), out_shape=pltpu....  4.51 us
    ppermute x10, waiting for transfers between devices, swapped(): return lax.ppermute(value, axes, [(i, i ^ mask) for i in range(count)])  3.8 us
    pallas_call x1, Pallas kernels, attention(): pl.pallas_call(attention_kernel, out_shape=(pltpu.VMEM((query_count, 2 *...  2.78 us
  transfers between devices with their start and end apart: 11, of which 5 were waited for; matrix products, arithmetic and copies ran while one was open for 0% of the time, Pallas kernels for 11%

profile of v6, /device:TPU:1, one launch (start us, length us, event | category | flops | bytes accessed | tf_op | source)
XLA Modules:
  0.0 63.0 jit_solution(8782807110575828802)
XLA Ops:
  0.0 2.8 %shard_map.145 = (f32[8,16,128]{2,1,0:T(8,128)S(1)}, bf16[256,4096]{1,0:T(8,128)(2,1)S(1)}) custom-call(s32[2,2,4]{2,1,0:T(2,128)} %bitcast.26, bf16[4,2,8,128]{3,2,1,0:T(8,128)(2,1)} %queries_in.1, bf16[4,2,128]{2,1,0:T(2,128)(2,1)} %new_key_in.1, bf16[4,2,128]{2,1,0:T(2,128)(2,1)} %new_value_in.1, bf16[4,128,128]{2,1,0:T(8,128)(2,1)} %bitcast.24, ...), custom_call_target="tpu_custom_call" | custom-call | tf_op jit(solution)/shard_map/pallas_call | solution.py:170
  2.8 11.8 %all_to_all.10.parts = f32[8,16,128]{2,1,0:T(8,128)S(1)} all-to-all(f32[8,16,128]{2,1,0:T(8,128)S(1)} %get-tuple-element.9), channel_id=1, replica_groups=mesh['ctx'=8,'kvh'=2,'exp'=8] {'ctx'}, dimensions={0} | all-to-all | bytes 131072 | tf_op jit(solution)/shard_map/all_to_all | solution.py:506
  14.6 0.5 shard_map.146.refs_0_.p0
  15.1 2.5 %collective-permute-start.2 = (bf16[4,4096]{1,0:T(4,128)(2,1)S(1)}, bf16[4,4096]{1,0:T(4,128)(2,1)S(1)}, u32[]{:S(2)}, u32[]{:S(2)}) collective-permute-start(bf16[4,4096]{1,0:T(4,128)(2,1)S(1)} %shard_map.146.refs_0_.p0), channel_id=1, source_target_pairs={{0,8},{8,0},{16,24},{24,16},{32,40},{40,32},{48,56},{56,48},{64,72... | collective-permute-start | bytes 98312 | tf_op jit(solution)/shard_map/ppermute | solution.py:470
  17.6 0.4 collective-permute-start.1
  18.0 0.0 collective-permute-start
  18.0 2.2 %shard_map.147 = bf16[2,4096,2,128]{3,2,1,0:T(2,128)(2,1)S(1)} custom-call(bf16[1,4096,2,768]{3,2,1,0:T(2,128)(2,1)} %source.5, bf16[4,4096]{1,0:T(4,128)(2,1)S(1)} %shard_map.146.refs_0_.p0), custom_call_target="tpu_custom_call" | custom-call | bytes 4194304 | tf_op jit(solution)/shard_map/pallas_call | solution.py:231
  20.2 0.0 collective-permute-done.2.p3
  20.2 1.6 %collective-permute-done.1.p2 = bf16[4,4096]{1,0:T(4,128)(2,1)S(1)} collective-permute-done((bf16[4,4096]{1,0:T(4,128)(2,1)S(1)}, bf16[4,4096]{1,0:T(4,128)(2,1)S(1)}, u32[]{:S(2)}, u32[]{:S(2)}) %collective-permute-start.1) | collective-permute-done | bytes 32800 | tf_op jit(solution)/shard_map/ppermute | solution.py:470
  21.9 0.0 collective-permute-done.p1
  21.9 0.0 copy-start
  21.9 0.0 copy-start.1
  21.9 0.0 copy-start.2
  21.9 1.1 %collective-permute-start.5 = (bf16[4,4096]{1,0:T(4,128)(2,1)S(1)}, bf16[4,4096]{1,0:T(4,128)(2,1)S(1)}, u32[]{:S(2)}, u32[]{:S(2)}) collective-permute-start(bf16[4,4096]{1,0:T(4,128)(2,1)S(1)} %shard_map.148.refs_0_.p0), channel_id=1, source_target_pairs={{0,64},{8,72},{16,80},{24,88},{32,96},{40,104},{48,112},{56,120},{... | collective-permute-start | bytes 98312 | tf_op jit(solution)/shard_map/ppermute | solution.py:470
  23.0 1.7 %collective-permute-start.4 = (bf16[4,4096]{1,0:T(4,128)(2,1)S(1)}, bf16[4,4096]{1,0:T(4,128)(2,1)S(1)}, u32[]{:S(2)}, u32[]{:S(2)}) collective-permute-start(bf16[4,4096]{1,0:T(4,128)(2,1)S(1)} %shard_map.148.refs_0_.p0), channel_id=1, source_target_pairs={{0,96},{8,104},{16,112},{24,120},{32,64},{40,72},{48,80},{56,88},{... | collective-permute-start | bytes 98312 | tf_op jit(solution)/shard_map/ppermute | solution.py:470
  24.7 0.0 collective-permute-start.3
  24.7 2.2 %shard_map.149 = bf16[2,4096,2,128]{3,2,1,0:T(2,128)(2,1)S(1)} custom-call(bf16[1,4096,2,768]{3,2,1,0:T(2,128)(2,1)} %source.5, bf16[4,4096]{1,0:T(4,128)(2,1)S(1)} %shard_map.148.refs_0_.p0), custom_call_target="tpu_custom_call" | custom-call | bytes 4194304 | tf_op jit(solution)/shard_map/pallas_call | solution.py:231
  26.9 0.0 collective-permute-done.5.p3
  26.9 0.0 collective-permute-done.4.p2
  27.0 0.5 collective-permute-done.3.p1
  27.4 0.0 copy-done
  27.4 0.0 copy-done.1
  27.5 0.0 copy-done.2
  27.5 0.2 shard_map.150
  27.7 0.0 slice-start
  27.7 0.0 slice-start.1
  27.7 3.0 %collective-permute-start.8 = (bf16[4,4224]{1,0:T(4,128)(2,1)S(1)}, bf16[4,4224]{1,0:T(4,128)(2,1)S(1)}, u32[]{:S(2)}, u32[]{:S(2)}) collective-permute-start(bf16[4,4224]{1,0:T(4,128)(2,1)S(1)} %get-tuple-element.11.refs_0_.p0), channel_id=1, source_target_pairs={{0,4},{1,5},{2,6},{3,7},{4,0},{5,1},{6,2},{7,3},{8,12},{9,13},{10,... | collective-permute-start | bytes 101384 | tf_op jit(solution)/shard_map/ppermute | solution.py:470
  30.7 0.8 %collective-permute-start.7 = (bf16[4,4224]{1,0:T(4,128)(2,1)S(1)}, bf16[4,4224]{1,0:T(4,128)(2,1)S(1)}, u32[]{:S(2)}, u32[]{:S(2)}) collective-permute-start(bf16[4,4224]{1,0:T(4,128)(2,1)S(1)} %get-tuple-element.11.refs_0_.p0), channel_id=1, source_target_pairs={{0,6},{1,7},{2,4},{3,5},{4,2},{5,3},{6,0},{7,1},{8,14},{9,15},{10,... | collective-permute-start | bytes 101384 | tf_op jit(solution)/shard_map/ppermute | solution.py:470
  31.5 0.0 collective-permute-start.6
  31.5 2.2 %shard_map.151 = bf16[2,4096,2,128]{3,2,1,0:T(2,128)(2,1)S(1)} custom-call(bf16[1,4096,2,768]{3,2,1,0:T(2,128)(2,1)} %source.5, bf16[4,4224]{1,0:T(4,128)(2,1)S(1)} %get-tuple-element.11.refs_0_.p0), custom_call_target="tpu_custom_call" | custom-call | bytes 4194304 | tf_op jit(solution)/shard_map/pallas_call | solution.py:231
  33.7 0.0 collective-permute-done.8.p3
  33.7 1.0 %collective-permute-done.7.p2 = bf16[4,4224]{1,0:T(4,128)(2,1)S(1)} collective-permute-done((bf16[4,4224]{1,0:T(4,128)(2,1)S(1)}, bf16[4,4224]{1,0:T(4,128)(2,1)S(1)}, u32[]{:S(2)}, u32[]{:S(2)}) %collective-permute-start.7) | collective-permute-done | bytes 33824 | tf_op jit(solution)/shard_map/ppermute | solution.py:470
  34.7 0.0 collective-permute-done.6.p1
  34.7 6.5 %collective-permute-start.9 = (bf16[16,4224]{1,0:T(8,128)(2,1)S(1)}, bf16[16,4224]{1,0:T(8,128)(2,1)S(1)}, u32[]{:S(2)}, u32[]{:S(2)}) collective-permute-start(bf16[16,4224]{1,0:T(8,128)(2,1)S(1)} %shard_map.152.x.x0), channel_id=1, source_target_pairs={{0,1},{1,0},{2,3},{3,2},{4,5},{5,4},{6,7},{7,6},{8,9},{9,8},{10,11... | collective-permute-start | bytes 405512 | tf_op jit(solution)/shard_map/ppermute | solution.py:470
  41.2 0.3 shard_map.153.first
  41.5 0.0 copy-start.3
  41.5 0.7 %collective-permute-done.9.x1 = bf16[16,4224]{1,0:T(8,128)(2,1)S(1)} collective-permute-done((bf16[16,4224]{1,0:T(8,128)(2,1)S(1)}, bf16[16,4224]{1,0:T(8,128)(2,1)S(1)}, u32[]{:S(2)}, u32[]{:S(2)}) %collective-permute-start.9) | collective-permute-done | bytes 135200 | tf_op jit(solution)/shard_map/ppermute | solution.py:470
  42.2 0.0 slice-done
  42.2 0.0 slice-done.1
  42.2 4.5 %shard_map.154.after = bf16[128,4,128]{2,1,0:T(4,128)(2,1)} custom-call(bf16[16,4224]{1,0:T(8,128)(2,1)S(1)} %shard_map.152.x.x0, bf16[16,4224]{1,0:T(8,128)(2,1)S(1)} %collective-permute-done.9.x1, bf16[32,8192]{1,0:T(8,128)(2,1)S(1)} %shard_map.153.first, bf16[2,8192,128]{2,1,0:T(8,128)(2,1)S(1)} %bitcast.12, bf16[2,8192,128]{2,1,0:T(8,128)(2,1)S(1)} %bitcast.14, ...), custom_call_target="tpu_custom_call" | custom-call | tf_op jit(solution)/shard_map/pallas_call | solution.py:333
  46.7 5.4 %all-to-all-start.1 = ((bf16[128,4,128]{2,1,0:T(4,128)(2,1)}), bf16[128,4,128]{2,1,0:T(4,128)(2,1)S(1)}, u32[]{:S(2)}, u32[]{:S(2)}) async-start(bf16[128,4,128]{2,1,0:T(4,128)(2,1)} %shard_map.154.after), calls=%async_computation.1 | async-start | bytes 262144 | tf_op jit(solution)/shard_map/all_to_all | solution.py:525
  52.1 0.0 copy-done.3
  52.1 0.1 shard_map.155.mix
  52.2 10.0 %all-to-all-done.1 = bf16[128,4,128]{2,1,0:T(4,128)(2,1)S(1)} async-done(((bf16[128,4,128]{2,1,0:T(4,128)(2,1)}), bf16[128,4,128]{2,1,0:T(4,128)(2,1)S(1)}, u32[]{:S(2)}, u32[]{:S(2)}) %all-to-all-start.1) | async-done | bytes 131104 | tf_op jit(solution)/shard_map/all_to_all | solution.py:525
  62.3 0.7 %shard_map.156 = bf16[4,256]{1,0:T(4,128)(2,1)} custom-call(bf16[512,128]{1,0:T(8,128)(2,1)S(1)} %bitcast.19, bf16[16,512]{1,0:T(8,128)(2,1)S(1)} %shard_map.155.mix, f32[4,256]{1,0:T(4,128)S(1)} %get-tuple-element.12.own), custom_call_target="tpu_custom_call" | custom-call | tf_op jit(solution)/shard_map/pallas_call | solution.py:460
  (3 shorter events, 0.1 us)
Async XLA Ops:
  15.1 5.1 %collective-permute-start.2 = (bf16[4,4096]{1,0:T(4,128)(2,1)S(1)}, bf16[4,4096]{1,0:T(4,128)(2,1)S(1)}, u32[]{:S(2)}, u32[]{:S(2)}) collective-permute-start(bf16[4,4096]{1,0:T(4,128)(2,1)S(1)} %shard_map.146.refs_0_.p0), channel_id=1, source_target_pairs={{0,8},{8,0},{16,24},{24,16},{32,40},{40,32},{48,56},{56,48},{64,72... | collective-permute-start | bytes 98312 | tf_op jit(solution)/shard_map/ppermute | solution.py:470
  17.6 4.3 %collective-permute-start.1 = (bf16[4,4096]{1,0:T(4,128)(2,1)S(1)}, bf16[4,4096]{1,0:T(4,128)(2,1)S(1)}, u32[]{:S(2)}, u32[]{:S(2)}) collective-permute-start(bf16[4,4096]{1,0:T(4,128)(2,1)S(1)} %shard_map.146.refs_0_.p0), channel_id=1, source_target_pairs={{0,24},{8,16},{16,8},{24,0},{32,56},{40,48},{48,40},{56,32},{64,88... | collective-permute-start | bytes 98312 | tf_op jit(solution)/shard_map/ppermute | solution.py:470
  18.0 3.9 %collective-permute-start = (bf16[4,4096]{1,0:T(4,128)(2,1)S(1)}, bf16[4,4096]{1,0:T(4,128)(2,1)S(1)}, u32[]{:S(2)}, u32[]{:S(2)}) collective-permute-start(bf16[4,4096]{1,0:T(4,128)(2,1)S(1)} %shard_map.146.refs_0_.p0), channel_id=1, source_target_pairs={{0,16},{8,24},{16,0},{24,8},{32,48},{40,56},{48,32},{56,40},{64,80... | collective-permute-start | bytes 98312 | tf_op jit(solution)/shard_map/ppermute | solution.py:470
  21.9 5.6 %copy-start = (bf16[4,4096]{1,0:T(4,128)(2,1)S(1)}, bf16[4,4096]{1,0:T(4,128)(2,1)}, u32[]{:S(2)}) copy-start(bf16[4,4096]{1,0:T(4,128)(2,1)} %residual.1) | copy-start | bytes 98308
  21.9 5.6 %copy-start.1 = (f32[4096]{0:T(1024)S(1)}, f32[4096]{0:T(1024)}, u32[]{:S(2)}) copy-start(f32[4096]{0:T(1024)} %param.25) | copy-start | bytes 49156
  21.9 5.5 %copy-start.2 = (s32[4,8]{1,0:T(4,128)S(1)}, s32[4,8]{1,0:T(4,128)}, u32[]{:S(2)}) copy-start(s32[4,8]{1,0:T(4,128)} %ids.3) | copy-start | bytes 388
  21.9 5.0 %collective-permute-start.5 = (bf16[4,4096]{1,0:T(4,128)(2,1)S(1)}, bf16[4,4096]{1,0:T(4,128)(2,1)S(1)}, u32[]{:S(2)}, u32[]{:S(2)}) collective-permute-start(bf16[4,4096]{1,0:T(4,128)(2,1)S(1)} %shard_map.148.refs_0_.p0), channel_id=1, source_target_pairs={{0,64},{8,72},{16,80},{24,88},{32,96},{40,104},{48,112},{56,120},{... | collective-permute-start | bytes 98312 | tf_op jit(solution)/shard_map/ppermute | solution.py:470
  23.0 4.0 %collective-permute-start.4 = (bf16[4,4096]{1,0:T(4,128)(2,1)S(1)}, bf16[4,4096]{1,0:T(4,128)(2,1)S(1)}, u32[]{:S(2)}, u32[]{:S(2)}) collective-permute-start(bf16[4,4096]{1,0:T(4,128)(2,1)S(1)} %shard_map.148.refs_0_.p0), channel_id=1, source_target_pairs={{0,96},{8,104},{16,112},{24,120},{32,64},{40,72},{48,80},{56,88},{... | collective-permute-start | bytes 98312 | tf_op jit(solution)/shard_map/ppermute | solution.py:470
  24.7 2.8 %collective-permute-start.3 = (bf16[4,4096]{1,0:T(4,128)(2,1)S(1)}, bf16[4,4096]{1,0:T(4,128)(2,1)S(1)}, u32[]{:S(2)}, u32[]{:S(2)}) collective-permute-start(bf16[4,4096]{1,0:T(4,128)(2,1)S(1)} %shard_map.148.refs_0_.p0), channel_id=1, source_target_pairs={{0,32},{8,40},{16,48},{24,56},{32,0},{40,8},{48,16},{56,24},{64,96... | collective-permute-start | bytes 98312 | tf_op jit(solution)/shard_map/ppermute | solution.py:470
  27.7 14.5 %slice-start = ((s8[6291456]{0:T(1024)(128)(4,1)}), s8[4194304]{0:T(1024)(128)(4,1)S(1)}, s32[]{:S(2)}) async-start(s8[6291456]{0:T(1024)(128)(4,1)} %bitcast.17), calls=%async_computation.2 | async-start | bytes 8388608
  27.7 14.5 %slice-start.1 = ((s8[6291456]{0:T(1024)(128)(4,1)}), s8[2097152]{0:T(1024)(128)(4,1)S(1)}, s32[]{:S(2)}) async-start(s8[6291456]{0:T(1024)(128)(4,1)} %bitcast.17), calls=%async_computation.3 | async-start | bytes 4194304
  27.7 6.0 %collective-permute-start.8 = (bf16[4,4224]{1,0:T(4,128)(2,1)S(1)}, bf16[4,4224]{1,0:T(4,128)(2,1)S(1)}, u32[]{:S(2)}, u32[]{:S(2)}) collective-permute-start(bf16[4,4224]{1,0:T(4,128)(2,1)S(1)} %get-tuple-element.11.refs_0_.p0), channel_id=1, source_target_pairs={{0,4},{1,5},{2,6},{3,7},{4,0},{5,1},{6,2},{7,3},{8,12},{9,13},{10,... | collective-permute-start | bytes 101384 | tf_op jit(solution)/shard_map/ppermute | solution.py:470
  30.7 4.0 %collective-permute-start.7 = (bf16[4,4224]{1,0:T(4,128)(2,1)S(1)}, bf16[4,4224]{1,0:T(4,128)(2,1)S(1)}, u32[]{:S(2)}, u32[]{:S(2)}) collective-permute-start(bf16[4,4224]{1,0:T(4,128)(2,1)S(1)} %get-tuple-element.11.refs_0_.p0), channel_id=1, source_target_pairs={{0,6},{1,7},{2,4},{3,5},{4,2},{5,3},{6,0},{7,1},{8,14},{9,15},{10,... | collective-permute-start | bytes 101384 | tf_op jit(solution)/shard_map/ppermute | solution.py:470
  31.5 3.2 %collective-permute-start.6 = (bf16[4,4224]{1,0:T(4,128)(2,1)S(1)}, bf16[4,4224]{1,0:T(4,128)(2,1)S(1)}, u32[]{:S(2)}, u32[]{:S(2)}) collective-permute-start(bf16[4,4224]{1,0:T(4,128)(2,1)S(1)} %get-tuple-element.11.refs_0_.p0), channel_id=1, source_target_pairs={{0,2},{1,3},{2,0},{3,1},{4,6},{5,7},{6,4},{7,5},{8,10},{9,11},{10,... | collective-permute-start | bytes 101384 | tf_op jit(solution)/shard_map/ppermute | solution.py:470
  34.7 7.5 %collective-permute-start.9 = (bf16[16,4224]{1,0:T(8,128)(2,1)S(1)}, bf16[16,4224]{1,0:T(8,128)(2,1)S(1)}, u32[]{:S(2)}, u32[]{:S(2)}) collective-permute-start(bf16[16,4224]{1,0:T(8,128)(2,1)S(1)} %shard_map.152.x.x0), channel_id=1, source_target_pairs={{0,1},{1,0},{2,3},{3,2},{4,5},{5,4},{6,7},{7,6},{8,9},{9,8},{10,11... | collective-permute-start | bytes 405512 | tf_op jit(solution)/shard_map/ppermute | solution.py:470
  41.5 10.6 %copy-start.3 = (f32[4,8]{1,0:T(4,128)S(1)}, f32[4,8]{1,0:T(4,128)}, u32[]{:S(2)}) copy-start(f32[4,8]{1,0:T(4,128)} %gates.1) | copy-start | bytes 388
  46.7 15.6 %all-to-all-start.1 = ((bf16[128,4,128]{2,1,0:T(4,128)(2,1)}), bf16[128,4,128]{2,1,0:T(4,128)(2,1)S(1)}, u32[]{:S(2)}, u32[]{:S(2)}) async-start(bf16[128,4,128]{2,1,0:T(4,128)(2,1)} %shard_map.154.after), calls=%async_computation.1 | async-start | bytes 262144 | tf_op jit(solution)/shard_map/all_to_all | solution.py:525

commit v7 on v6

--- a/solution.py
+++ b/solution.py
@@ -508,14 +508,14 @@
     projected = project(parts, out_weight)
 
     axes = ("ctx", "kvh")
-    along_x = [projected] + [swapped(projected, axes, plane, m) for m in (2, 3, 1)]
+    along_x = [projected] + [swapped(projected, axes, plane, m) for m in (3, 2, 1)]
     tiles = [fetch(w_gate_up, 0, 2, projected)]
     sums = sum_pieces(along_x, tiles[-1])
-    along_z = [sums] + [swapped(sums, axes, plane, m) for m in (4, 12, 8)]
+    along_z = [sums] + [swapped(sums, axes, plane, m) for m in (12, 4, 8)]
     tiles.append(fetch(w_gate_up, 2, 2, sums))
     own, normed = norm(along_z, residual, norm_gain, expert_ids, tiles[-1], kvh_devices)
 
-    steps = (0, 2, 6, 4)
+    steps = (0, 6, 2, 4)
     along_y = [normed] + [swapped(normed, "exp", exp_devices, m) for m in steps[1:]]
     tiles.append(fetch(w_gate_up, 4, 2, normed))
     mine = stack(along_y, tiles[-1])

time: 63.2 us -> 62.6 us (level)
    all_to_all x1, starting transfers between devices: 5.4 us -> 4.03 us  [body(): lax.all_to_all(results, ('ctx', 'kvh', 'exp'), split_axis=0, concat_axis=...]
    ppermute x10, starting transfers between devices: 15.9 us -> 17.2 us  [swapped(): return lax.ppermute(value, axes, [(i, i ^ mask) for i in range(count)])]
  transfers between devices with their start and end apart: 11 -> 11, of which waited for: 5 -> 4; matrix products, arithmetic and copies ran while one was open for 0% -> 0% of each run, Pallas kernels for 11% -> 11%
where the time goes in v7:
time: 62.6 us; the launch traced here: 62.4 us
  starting transfers between devices  21.2 us (34%)
  Pallas kernels  15.9 us (25%)
  waiting for transfers between devices  13.3 us (21%)
  blocking collectives  11.8 us (19%)
    ppermute x10, starting transfers between devices, swapped(): return lax.ppermute(value, axes, [(i, i ^ mask) for i in range(count)])  17.2 us
    all_to_all x1, blocking collectives, body(): lax.all_to_all(parts, 'ctx', split_axis=0, concat_axis=0, tiled=True)  11.8 us
    all_to_all x1, waiting for transfers between devices, body(): lax.all_to_all(results, ('ctx', 'kvh', 'exp'), split_axis=0, concat_axis=...  10 us
    pallas_call x3, Pallas kernels, fetch(): pl.pallas_call(functools.partial(fetch_kernel, first), out_shape=pltpu.VM...  6.64 us
    pallas_call x1, Pallas kernels, experts(): pl.pallas_call(functools.partial(experts_kernel, order), out_shape=pltpu....  4.51 us
    all_to_all x1, starting transfers between devices, body(): lax.all_to_all(results, ('ctx', 'kvh', 'exp'), split_axis=0, concat_axis=...  4.03 us
    ppermute x10, waiting for transfers between devices, swapped(): return lax.ppermute(value, axes, [(i, i ^ mask) for i in range(count)])  3.26 us
    pallas_call x1, Pallas kernels, attention(): pl.pallas_call(attention_kernel, out_shape=(pltpu.VMEM((query_count, 2 *...  2.78 us
  transfers between devices with their start and end apart: 11, of which 4 were waited for; matrix products, arithmetic and copies ran while one was open for 0% of the time, Pallas kernels for 11%

profile of v7, /device:TPU:1, one launch (start us, length us, event | category | flops | bytes accessed | tf_op | source)
XLA Modules:
  0.0 62.4 jit_solution(1882648216477057795)
XLA Ops:
  0.0 2.8 %shard_map.145 = (f32[8,16,128]{2,1,0:T(8,128)S(1)}, bf16[256,4096]{1,0:T(8,128)(2,1)S(1)}) custom-call(s32[2,2,4]{2,1,0:T(2,128)} %bitcast.26, bf16[4,2,8,128]{3,2,1,0:T(8,128)(2,1)} %queries_in.1, bf16[4,2,128]{2,1,0:T(2,128)(2,1)} %new_key_in.1, bf16[4,2,128]{2,1,0:T(2,128)(2,1)} %new_value_in.1, bf16[4,128,128]{2,1,0:T(8,128)(2,1)} %bitcast.24, ...), custom_call_target="tpu_custom_call" | custom-call | tf_op jit(solution)/shard_map/pallas_call | solution.py:170
  2.8 11.8 %all_to_all.10.parts = f32[8,16,128]{2,1,0:T(8,128)S(1)} all-to-all(f32[8,16,128]{2,1,0:T(8,128)S(1)} %get-tuple-element.9), channel_id=1, replica_groups=mesh['ctx'=8,'kvh'=2,'exp'=8] {'ctx'}, dimensions={0} | all-to-all | bytes 131072 | tf_op jit(solution)/shard_map/all_to_all | solution.py:506
  14.6 0.5 shard_map.146.refs_0_.p0
  15.1 2.5 %collective-permute-start.2 = (bf16[4,4096]{1,0:T(4,128)(2,1)S(1)}, bf16[4,4096]{1,0:T(4,128)(2,1)S(1)}, u32[]{:S(2)}, u32[]{:S(2)}) collective-permute-start(bf16[4,4096]{1,0:T(4,128)(2,1)S(1)} %shard_map.146.refs_0_.p0), channel_id=1, source_target_pairs={{0,8},{8,0},{16,24},{24,16},{32,40},{40,32},{48,56},{56,48},{64,72... | collective-permute-start | bytes 98312 | tf_op jit(solution)/shard_map/ppermute | solution.py:470
  17.6 0.0 collective-permute-start.1
  17.6 0.8 %collective-permute-start = (bf16[4,4096]{1,0:T(4,128)(2,1)S(1)}, bf16[4,4096]{1,0:T(4,128)(2,1)S(1)}, u32[]{:S(2)}, u32[]{:S(2)}) collective-permute-start(bf16[4,4096]{1,0:T(4,128)(2,1)S(1)} %shard_map.146.refs_0_.p0), channel_id=1, source_target_pairs={{0,24},{8,16},{16,8},{24,0},{32,56},{40,48},{48,40},{56,32},{64,88... | collective-permute-start | bytes 98312 | tf_op jit(solution)/shard_map/ppermute | solution.py:470
  18.4 2.2 %shard_map.147 = bf16[2,4096,2,128]{3,2,1,0:T(2,128)(2,1)S(1)} custom-call(bf16[1,4096,2,768]{3,2,1,0:T(2,128)(2,1)} %source.5, bf16[4,4096]{1,0:T(4,128)(2,1)S(1)} %shard_map.146.refs_0_.p0), custom_call_target="tpu_custom_call" | custom-call | bytes 4194304 | tf_op jit(solution)/shard_map/pallas_call | solution.py:231
  20.6 0.0 collective-permute-done.2.p3
  20.6 0.0 collective-permute-done.1.p2
  20.6 1.2 %collective-permute-done.p1 = bf16[4,4096]{1,0:T(4,128)(2,1)S(1)} collective-permute-done((bf16[4,4096]{1,0:T(4,128)(2,1)S(1)}, bf16[4,4096]{1,0:T(4,128)(2,1)S(1)}, u32[]{:S(2)}, u32[]{:S(2)}) %collective-permute-start) | collective-permute-done | bytes 32800 | tf_op jit(solution)/shard_map/ppermute | solution.py:470
  21.9 0.0 copy-start
  21.9 0.0 copy-start.1
  21.9 0.0 copy-start.2
  21.9 1.1 %collective-permute-start.5 = (bf16[4,4096]{1,0:T(4,128)(2,1)S(1)}, bf16[4,4096]{1,0:T(4,128)(2,1)S(1)}, u32[]{:S(2)}, u32[]{:S(2)}) collective-permute-start(bf16[4,4096]{1,0:T(4,128)(2,1)S(1)} %shard_map.148.refs_0_.p0), channel_id=1, source_target_pairs={{0,64},{8,72},{16,80},{24,88},{32,96},{40,104},{48,112},{56,120},{... | collective-permute-start | bytes 98312 | tf_op jit(solution)/shard_map/ppermute | solution.py:470
  23.0 0.5 collective-permute-start.4
  23.5 1.8 %collective-permute-start.3 = (bf16[4,4096]{1,0:T(4,128)(2,1)S(1)}, bf16[4,4096]{1,0:T(4,128)(2,1)S(1)}, u32[]{:S(2)}, u32[]{:S(2)}) collective-permute-start(bf16[4,4096]{1,0:T(4,128)(2,1)S(1)} %shard_map.148.refs_0_.p0), channel_id=1, source_target_pairs={{0,96},{8,104},{16,112},{24,120},{32,64},{40,72},{48,80},{56,88},{... | collective-permute-start | bytes 98312 | tf_op jit(solution)/shard_map/ppermute | solution.py:470
  25.3 2.2 %shard_map.149 = bf16[2,4096,2,128]{3,2,1,0:T(2,128)(2,1)S(1)} custom-call(bf16[1,4096,2,768]{3,2,1,0:T(2,128)(2,1)} %source.5, bf16[4,4096]{1,0:T(4,128)(2,1)S(1)} %shard_map.148.refs_0_.p0), custom_call_target="tpu_custom_call" | custom-call | bytes 4194304 | tf_op jit(solution)/shard_map/pallas_call | solution.py:231
  27.5 0.0 collective-permute-done.5.p3
  27.5 0.0 collective-permute-done.4.p2
  27.5 0.0 collective-permute-done.3.p1
  27.5 0.0 copy-done
  27.5 0.0 copy-done.1
  27.5 0.0 copy-done.2
  27.5 0.2 shard_map.150
  27.8 0.0 slice-start
  27.8 0.0 slice-start.1
  27.8 3.0 %collective-permute-start.8 = (bf16[4,4224]{1,0:T(4,128)(2,1)S(1)}, bf16[4,4224]{1,0:T(4,128)(2,1)S(1)}, u32[]{:S(2)}, u32[]{:S(2)}) collective-permute-start(bf16[4,4224]{1,0:T(4,128)(2,1)S(1)} %get-tuple-element.11.refs_0_.p0), channel_id=1, source_target_pairs={{0,4},{1,5},{2,6},{3,7},{4,0},{5,1},{6,2},{7,3},{8,12},{9,13},{10,... | collective-permute-start | bytes 101384 | tf_op jit(solution)/shard_map/ppermute | solution.py:470
  30.8 0.4 collective-permute-start.7
  31.2 0.4 collective-permute-start.6
  31.6 2.2 %shard_map.151 = bf16[2,4096,2,128]{3,2,1,0:T(2,128)(2,1)S(1)} custom-call(bf16[1,4096,2,768]{3,2,1,0:T(2,128)(2,1)} %source.5, bf16[4,4224]{1,0:T(4,128)(2,1)S(1)} %get-tuple-element.11.refs_0_.p0), custom_call_target="tpu_custom_call" | custom-call | bytes 4194304 | tf_op jit(solution)/shard_map/pallas_call | solution.py:231
  33.8 0.0 collective-permute-done.8.p3
  33.8 0.0 collective-permute-done.7.p2
  33.8 1.4 %collective-permute-done.6.p1 = bf16[4,4224]{1,0:T(4,128)(2,1)S(1)} collective-permute-done((bf16[4,4224]{1,0:T(4,128)(2,1)S(1)}, bf16[4,4224]{1,0:T(4,128)(2,1)S(1)}, u32[]{:S(2)}, u32[]{:S(2)}) %collective-permute-start.6) | collective-permute-done | bytes 33824 | tf_op jit(solution)/shard_map/ppermute | solution.py:470
  35.2 6.8 %collective-permute-start.9 = (bf16[16,4224]{1,0:T(8,128)(2,1)S(1)}, bf16[16,4224]{1,0:T(8,128)(2,1)S(1)}, u32[]{:S(2)}, u32[]{:S(2)}) collective-permute-start(bf16[16,4224]{1,0:T(8,128)(2,1)S(1)} %shard_map.152.x.x0), channel_id=1, source_target_pairs={{0,1},{1,0},{2,3},{3,2},{4,5},{5,4},{6,7},{7,6},{8,9},{9,8},{10,11... | collective-permute-start | bytes 405512 | tf_op jit(solution)/shard_map/ppermute | solution.py:470
  42.0 0.3 shard_map.153.first
  42.3 0.0 copy-start.3
  42.3 0.7 %collective-permute-done.9.x1 = bf16[16,4224]{1,0:T(8,128)(2,1)S(1)} collective-permute-done((bf16[16,4224]{1,0:T(8,128)(2,1)S(1)}, bf16[16,4224]{1,0:T(8,128)(2,1)S(1)}, u32[]{:S(2)}, u32[]{:S(2)}) %collective-permute-start.9) | collective-permute-done | bytes 135200 | tf_op jit(solution)/shard_map/ppermute | solution.py:470
  43.0 0.0 slice-done
  43.0 0.0 slice-done.1
  43.0 4.5 %shard_map.154.after = bf16[128,4,128]{2,1,0:T(4,128)(2,1)} custom-call(bf16[16,4224]{1,0:T(8,128)(2,1)S(1)} %shard_map.152.x.x0, bf16[16,4224]{1,0:T(8,128)(2,1)S(1)} %collective-permute-done.9.x1, bf16[32,8192]{1,0:T(8,128)(2,1)S(1)} %shard_map.153.first, bf16[2,8192,128]{2,1,0:T(8,128)(2,1)S(1)} %bitcast.12, bf16[2,8192,128]{2,1,0:T(8,128)(2,1)S(1)} %bitcast.14, ...), custom_call_target="tpu_custom_call" | custom-call | tf_op jit(solution)/shard_map/pallas_call | solution.py:333
  47.5 4.0 %all-to-all-start.1 = ((bf16[128,4,128]{2,1,0:T(4,128)(2,1)}), bf16[128,4,128]{2,1,0:T(4,128)(2,1)S(1)}, u32[]{:S(2)}, u32[]{:S(2)}) async-start(bf16[128,4,128]{2,1,0:T(4,128)(2,1)} %shard_map.154.after), calls=%async_computation.1 | async-start | bytes 262144 | tf_op jit(solution)/shard_map/all_to_all | solution.py:525
  51.5 0.0 copy-done.3
  51.6 0.1 shard_map.155.mix
  51.7 10.0 %all-to-all-done.1 = bf16[128,4,128]{2,1,0:T(4,128)(2,1)S(1)} async-done(((bf16[128,4,128]{2,1,0:T(4,128)(2,1)}), bf16[128,4,128]{2,1,0:T(4,128)(2,1)S(1)}, u32[]{:S(2)}, u32[]{:S(2)}) %all-to-all-start.1) | async-done | bytes 131104 | tf_op jit(solution)/shard_map/all_to_all | solution.py:525
  61.7 0.7 %shard_map.156 = bf16[4,256]{1,0:T(4,128)(2,1)} custom-call(bf16[512,128]{1,0:T(8,128)(2,1)S(1)} %bitcast.19, bf16[16,512]{1,0:T(8,128)(2,1)S(1)} %shard_map.155.mix, f32[4,256]{1,0:T(4,128)S(1)} %get-tuple-element.12.own), custom_call_target="tpu_custom_call" | custom-call | tf_op jit(solution)/shard_map/pallas_call | solution.py:460
  (3 shorter events, 0.1 us)
Async XLA Ops:
  15.1 5.5 %collective-permute-start.2 = (bf16[4,4096]{1,0:T(4,128)(2,1)S(1)}, bf16[4,4096]{1,0:T(4,128)(2,1)S(1)}, u32[]{:S(2)}, u32[]{:S(2)}) collective-permute-start(bf16[4,4096]{1,0:T(4,128)(2,1)S(1)} %shard_map.146.refs_0_.p0), channel_id=1, source_target_pairs={{0,8},{8,0},{16,24},{24,16},{32,40},{40,32},{48,56},{56,48},{64,72... | collective-permute-start | bytes 98312 | tf_op jit(solution)/shard_map/ppermute | solution.py:470
  17.6 3.0 %collective-permute-start.1 = (bf16[4,4096]{1,0:T(4,128)(2,1)S(1)}, bf16[4,4096]{1,0:T(4,128)(2,1)S(1)}, u32[]{:S(2)}, u32[]{:S(2)}) collective-permute-start(bf16[4,4096]{1,0:T(4,128)(2,1)S(1)} %shard_map.146.refs_0_.p0), channel_id=1, source_target_pairs={{0,16},{8,24},{16,0},{24,8},{32,48},{40,56},{48,32},{56,40},{64,80... | collective-permute-start | bytes 98312 | tf_op jit(solution)/shard_map/ppermute | solution.py:470
  17.6 4.3 %collective-permute-start = (bf16[4,4096]{1,0:T(4,128)(2,1)S(1)}, bf16[4,4096]{1,0:T(4,128)(2,1)S(1)}, u32[]{:S(2)}, u32[]{:S(2)}) collective-permute-start(bf16[4,4096]{1,0:T(4,128)(2,1)S(1)} %shard_map.146.refs_0_.p0), channel_id=1, source_target_pairs={{0,24},{8,16},{16,8},{24,0},{32,56},{40,48},{48,40},{56,32},{64,88... | collective-permute-start | bytes 98312 | tf_op jit(solution)/shard_map/ppermute | solution.py:470
  21.9 5.6 %copy-start = (bf16[4,4096]{1,0:T(4,128)(2,1)S(1)}, bf16[4,4096]{1,0:T(4,128)(2,1)}, u32[]{:S(2)}) copy-start(bf16[4,4096]{1,0:T(4,128)(2,1)} %residual.1) | copy-start | bytes 98308
  21.9 5.6 %copy-start.1 = (f32[4096]{0:T(1024)S(1)}, f32[4096]{0:T(1024)}, u32[]{:S(2)}) copy-start(f32[4096]{0:T(1024)} %param.25) | copy-start | bytes 49156
  21.9 5.6 %copy-start.2 = (s32[4,8]{1,0:T(4,128)S(1)}, s32[4,8]{1,0:T(4,128)}, u32[]{:S(2)}) copy-start(s32[4,8]{1,0:T(4,128)} %ids.3) | copy-start | bytes 388
  21.9 5.6 %collective-permute-start.5 = (bf16[4,4096]{1,0:T(4,128)(2,1)S(1)}, bf16[4,4096]{1,0:T(4,128)(2,1)S(1)}, u32[]{:S(2)}, u32[]{:S(2)}) collective-permute-start(bf16[4,4096]{1,0:T(4,128)(2,1)S(1)} %shard_map.148.refs_0_.p0), channel_id=1, source_target_pairs={{0,64},{8,72},{16,80},{24,88},{32,96},{40,104},{48,112},{56,120},{... | collective-permute-start | bytes 98312 | tf_op jit(solution)/shard_map/ppermute | solution.py:470
  23.0 4.5 %collective-permute-start.4 = (bf16[4,4096]{1,0:T(4,128)(2,1)S(1)}, bf16[4,4096]{1,0:T(4,128)(2,1)S(1)}, u32[]{:S(2)}, u32[]{:S(2)}) collective-permute-start(bf16[4,4096]{1,0:T(4,128)(2,1)S(1)} %shard_map.148.refs_0_.p0), channel_id=1, source_target_pairs={{0,32},{8,40},{16,48},{24,56},{32,0},{40,8},{48,16},{56,24},{64,96... | collective-permute-start | bytes 98312 | tf_op jit(solution)/shard_map/ppermute | solution.py:470
  23.5 4.0 %collective-permute-start.3 = (bf16[4,4096]{1,0:T(4,128)(2,1)S(1)}, bf16[4,4096]{1,0:T(4,128)(2,1)S(1)}, u32[]{:S(2)}, u32[]{:S(2)}) collective-permute-start(bf16[4,4096]{1,0:T(4,128)(2,1)S(1)} %shard_map.148.refs_0_.p0), channel_id=1, source_target_pairs={{0,96},{8,104},{16,112},{24,120},{32,64},{40,72},{48,80},{56,88},{... | collective-permute-start | bytes 98312 | tf_op jit(solution)/shard_map/ppermute | solution.py:470
  27.8 15.2 %slice-start = ((s8[6291456]{0:T(1024)(128)(4,1)}), s8[4194304]{0:T(1024)(128)(4,1)S(1)}, s32[]{:S(2)}) async-start(s8[6291456]{0:T(1024)(128)(4,1)} %bitcast.17), calls=%async_computation.2 | async-start | bytes 8388608
  27.8 15.2 %slice-start.1 = ((s8[6291456]{0:T(1024)(128)(4,1)}), s8[2097152]{0:T(1024)(128)(4,1)S(1)}, s32[]{:S(2)}) async-start(s8[6291456]{0:T(1024)(128)(4,1)} %bitcast.17), calls=%async_computation.3 | async-start | bytes 4194304
  27.8 6.0 %collective-permute-start.8 = (bf16[4,4224]{1,0:T(4,128)(2,1)S(1)}, bf16[4,4224]{1,0:T(4,128)(2,1)S(1)}, u32[]{:S(2)}, u32[]{:S(2)}) collective-permute-start(bf16[4,4224]{1,0:T(4,128)(2,1)S(1)} %get-tuple-element.11.refs_0_.p0), channel_id=1, source_target_pairs={{0,4},{1,5},{2,6},{3,7},{4,0},{5,1},{6,2},{7,3},{8,12},{9,13},{10,... | collective-permute-start | bytes 101384 | tf_op jit(solution)/shard_map/ppermute | solution.py:470
  30.8 3.0 %collective-permute-start.7 = (bf16[4,4224]{1,0:T(4,128)(2,1)S(1)}, bf16[4,4224]{1,0:T(4,128)(2,1)S(1)}, u32[]{:S(2)}, u32[]{:S(2)}) collective-permute-start(bf16[4,4224]{1,0:T(4,128)(2,1)S(1)} %get-tuple-element.11.refs_0_.p0), channel_id=1, source_target_pairs={{0,2},{1,3},{2,0},{3,1},{4,6},{5,7},{6,4},{7,5},{8,10},{9,11},{10,... | collective-permute-start | bytes 101384 | tf_op jit(solution)/shard_map/ppermute | solution.py:470
  31.2 4.0 %collective-permute-start.6 = (bf16[4,4224]{1,0:T(4,128)(2,1)S(1)}, bf16[4,4224]{1,0:T(4,128)(2,1)S(1)}, u32[]{:S(2)}, u32[]{:S(2)}) collective-permute-start(bf16[4,4224]{1,0:T(4,128)(2,1)S(1)} %get-tuple-element.11.refs_0_.p0), channel_id=1, source_target_pairs={{0,6},{1,7},{2,4},{3,5},{4,2},{5,3},{6,0},{7,1},{8,14},{9,15},{10,... | collective-permute-start | bytes 101384 | tf_op jit(solution)/shard_map/ppermute | solution.py:470
  35.2 7.8 %collective-permute-start.9 = (bf16[16,4224]{1,0:T(8,128)(2,1)S(1)}, bf16[16,4224]{1,0:T(8,128)(2,1)S(1)}, u32[]{:S(2)}, u32[]{:S(2)}) collective-permute-start(bf16[16,4224]{1,0:T(8,128)(2,1)S(1)} %shard_map.152.x.x0), channel_id=1, source_target_pairs={{0,1},{1,0},{2,3},{3,2},{4,5},{5,4},{6,7},{7,6},{8,9},{9,8},{10,11... | collective-permute-start | bytes 405512 | tf_op jit(solution)/shard_map/ppermute | solution.py:470
  42.3 9.2 %copy-start.3 = (f32[4,8]{1,0:T(4,128)S(1)}, f32[4,8]{1,0:T(4,128)}, u32[]{:S(2)}) copy-start(f32[4,8]{1,0:T(4,128)} %gates.1) | copy-start | bytes 388
  47.5 14.2 %all-to-all-start.1 = ((bf16[128,4,128]{2,1,0:T(4,128)(2,1)}), bf16[128,4,128]{2,1,0:T(4,128)(2,1)S(1)}, u32[]{:S(2)}, u32[]{:S(2)}) async-start(bf16[128,4,128]{2,1,0:T(4,128)(2,1)} %shard_map.154.after), calls=%async_computation.1 | async-start | bytes 262144 | tf_op jit(solution)/shard_map/all_to_all | solution.py:525
